TPU v7x, 32 devices: a whole 2x2x4 slice. The times are simulated.
32 devices in a mesh: seq: 8 (over z, x), ctx: 4 (over y, core).
Axes of the slice: x: 2, y: 2, z: 4, core: 2. Of those that a mesh axis runs over, the one named last changes fastest.
Arguments:
- hidden_in: bfloat16 [8, 1024, 1024], P('seq', 'ctx'), may hold values from -6 to 6
- segments: int32 [8, 1024], P('seq', 'ctx'), may hold values from 0 to 32, as said below
- positions: int32 [8, 1024], P('seq', 'ctx'), may hold values from 0 to 3070, as said below
- ln1_gain: bfloat16 [1024], P(('seq', 'ctx')), may hold values from 0.5 to 1.5
- ln1_bias: bfloat16 [1024], P(('seq', 'ctx')), may hold values from -1.1953125 to 1.1953125
- ln2_gain: bfloat16 [1024], P(('seq', 'ctx')), may hold values from 0.5 to 1.5
- ln2_bias: bfloat16 [1024], P(('seq', 'ctx')), may hold values from -1.1953125 to 1.1953125
- qkv_weight: bfloat16 [1024, 3072], P(('seq', 'ctx')), may hold values from -0.25 to 0.25
- qkv_bias: bfloat16 [3072], P(('seq', 'ctx')), may hold values from -1.796875 to 1.796875
- out_weight: bfloat16 [1024, 1024], P(('seq', 'ctx')), may hold values from -0.5 to 0.5
- out_bias: bfloat16 [1024], P(('seq', 'ctx')), may hold values from -1.796875 to 1.796875
- up_weight: bfloat16 [1024, 4096], P(('seq', 'ctx')), may hold values from -0.1875 to 0.1875
- up_bias: bfloat16 [4096], P(('seq', 'ctx')), may hold values from -1.796875 to 1.796875
- down_weight: bfloat16 [4096, 1024], P(('seq', 'ctx')), may hold values from -0.09375 to 0.09375
- down_bias: bfloat16 [1024], P(('seq', 'ctx')), may hold values from -1.796875 to 1.796875
- out_grad: bfloat16 [8, 1024, 1024], P('seq', 'ctx'), may hold values from -6 to 6
Outputs:
- hidden_out: bfloat16 [8, 1024, 1024], P('seq', 'ctx')
- input_grad: float32 [8, 1024, 1024], P('seq', 'ctx')
- ln1_gain_grad: float32 [1024], P(('seq', 'ctx'))
- ln1_bias_grad: float32 [1024], P(('seq', 'ctx'))
- ln2_gain_grad: float32 [1024], P(('seq', 'ctx'))
- ln2_bias_grad: float32 [1024], P(('seq', 'ctx'))
- qkv_weight_grad: float32 [1024, 3072], P(('seq', 'ctx'))
- qkv_bias_grad: float32 [3072], P(('seq', 'ctx'))
- out_weight_grad: float32 [1024, 1024], P(('seq', 'ctx'))
- out_bias_grad: float32 [1024], P(('seq', 'ctx'))
- up_weight_grad: float32 [1024, 4096], P(('seq', 'ctx'))
- up_bias_grad: float32 [4096], P(('seq', 'ctx'))
- down_weight_grad: float32 [4096, 1024], P(('seq', 'ctx'))
- down_bias_grad: float32 [1024], P(('seq', 'ctx'))
Inputs may be any that keep to these rules, and one draw needn't show every extreme that they name: `segments`: in each row, segment numbers start at 0, never fall, and rise by one at the first token of each document. Within a document, positions rise by one from token to token.
All inputs are finite; a program needn't handle non-finite values.
Results may differ from a plain program's by a relative error of at most 0.012.
The roundings to bfloat16 on the way count: a program that leaves them out, or rounds other values in their place, can miss the bound.
Values may be sent and summed in bfloat16 or wider, within the bound.
No kernel may reach another device: no remote copies, remote signals or barrier semaphores. Data moves between devices by JAX's collectives and lax.ppermute only.
A program may use at most 192 MiB of HBM per device.

v0:
```python
from functools import partial
import math

import jax
import jax.numpy as jnp
from jax import lax
from jax.sharding import PartitionSpec as P

H = 16
HD = 64
ROT = 16


EPS = 1e-05
NEG = -1000000000.0


def norm_layer(value, gain, shift):
    average = jnp.mean(value, -1, keepdims=True)
    centred = value - average
    variance = jnp.mean(centred * centred, -1, keepdims=True)
    return centred * lax.rsqrt(variance + EPS) * gain + shift


def rotate(tensor, cosine, sine):
    half = ROT // 2
    first = tensor[..., :half]
    second = tensor[..., half:ROT]
    cosine = cosine[:, None, :]
    sine = sine[:, None, :]
    return jnp.concatenate(
        [first * cosine - second * sine, second * cosine + first * sine, tensor[..., ROT:]], -1
    )


def angles(places):
    index = jnp.arange(ROT // 2).astype(jnp.float32)
    frequency = 10000.0 ** (-2.0 * index / ROT)
    turned = places.astype(jnp.float32)[:, None] * frequency[None, :]
    return (jnp.cos(turned), jnp.sin(turned))


def contract_rows(left, right):
    return lax.dot_general(
        left, right, (((0,), (0,)), ((), ())), preferred_element_type=jnp.float32
    )


def contract_cols(left, right):
    return lax.dot_general(
        left, right, (((1,), (1,)), ((), ())), preferred_element_type=jnp.float32
    )


def local(
    hidden_in,
    segments,
    positions,
    ln1_gain,
    ln1_bias,
    ln2_gain,
    ln2_bias,
    qkv_weight,
    qkv_bias,
    out_weight,
    out_bias,
    up_weight,
    up_bias,
    down_weight,
    down_bias,
    out_grad,
):
    params = (
        ln1_gain,
        ln1_bias,
        ln2_gain,
        ln2_bias,
        qkv_weight,
        qkv_bias,
        out_weight,
        out_bias,
        up_weight,
        up_bias,
        down_weight,
        down_bias,
    )
    gathered = (
        lax.all_gather(params[0], ("seq", "ctx"), axis=0, tiled=True),
        lax.all_gather(params[1], ("seq", "ctx"), axis=0, tiled=True),
        lax.all_gather(params[2], ("seq", "ctx"), axis=0, tiled=True),
        lax.all_gather(params[3], ("seq", "ctx"), axis=0, tiled=True),
        lax.all_gather(params[4], ("seq", "ctx"), axis=0, tiled=True),
        lax.all_gather(params[5], ("seq", "ctx"), axis=0, tiled=True),
        lax.all_gather(params[6], ("seq", "ctx"), axis=0, tiled=True),
        lax.all_gather(params[7], ("seq", "ctx"), axis=0, tiled=True),
        lax.all_gather(params[8], ("seq", "ctx"), axis=0, tiled=True),
        lax.all_gather(params[9], ("seq", "ctx"), axis=0, tiled=True),
        lax.all_gather(params[10], ("seq", "ctx"), axis=0, tiled=True),
        lax.all_gather(params[11], ("seq", "ctx"), axis=0, tiled=True),
    )
    (
        gain_one,
        bias_one,
        gain_two,
        bias_two,
        w_qkv,
        b_qkv,
        w_out,
        b_out,
        w_up,
        b_up,
        w_down,
        b_down,
    ) = gathered
    rows = hidden_in.shape[1]
    width = hidden_in.shape[2]
    scale = 1.0 / math.sqrt(HD)
    source = hidden_in[0].astype(jnp.float32)
    normed_one, pull_one = jax.vjp(
        norm_layer, source, gain_one.astype(jnp.float32), bias_one.astype(jnp.float32)
    )
    normed_two, pull_two = jax.vjp(
        norm_layer, source, gain_two.astype(jnp.float32), bias_two.astype(jnp.float32)
    )
    input_one = normed_one.astype(jnp.bfloat16)
    input_two = normed_two.astype(jnp.bfloat16)
    linear = jnp.dot(input_one, w_qkv, preferred_element_type=jnp.float32) + b_qkv.astype(
        jnp.float32
    )
    shaped = linear.reshape(rows, 3, H, HD)
    cosine, sine = angles(positions[0])
    query = (rotate(shaped[:, 0], cosine, sine) * scale).astype(jnp.bfloat16)
    keys = rotate(shaped[:, 1], cosine, sine).astype(jnp.bfloat16)
    values = shaped[:, 2].astype(jnp.bfloat16)
    key_flat = keys.reshape(rows, width)
    value_flat = values.reshape(rows, width)
    segment_own = segments[0]
    segment_low = segment_own.astype(jnp.bfloat16)
    query_doc = segment_own.astype(jnp.float32)
    query_place = lax.axis_index("ctx") * rows + jnp.arange(rows)

    def masked_scores(key_block, doc_block, place_block):
        scores = jnp.einsum("qhd,khd->qhk", query, key_block, preferred_element_type=jnp.float32)
        allowed = (query_doc[:, None] == doc_block[None, :].astype(jnp.float32)) & (
            query_place[:, None] >= place_block[None, :]
        )
        return (scores, allowed[:, None, :])

    initial = (
        jnp.zeros((rows, H, HD), jnp.float32),
        jnp.full((rows, H), NEG, jnp.float32),
        jnp.zeros((rows, H), jnp.float32),
    )
    key_piece = lax.all_gather(key_flat, "ctx", axis=0, tiled=True)
    value_piece = lax.all_gather(value_flat, "ctx", axis=0, tiled=True)
    doc_piece = lax.all_gather(segment_low, "ctx", axis=0, tiled=True)
    count = key_piece.shape[0]
    attend_block = math.gcd(count, 512)
    number = count // attend_block
    key_blocks = key_piece.reshape(number, attend_block, H, HD)
    value_blocks = value_piece.reshape(number, attend_block, H, HD)
    doc_blocks = doc_piece.reshape(number, attend_block)
    offsets = jnp.arange(number) * attend_block

    def one_block(state, items):
        total, top, weight_sum = state
        key_block, value_block, doc_block, offset = items
        scores, allowed = masked_scores(key_block, doc_block, offset + jnp.arange(attend_block))
        scores = jnp.where(allowed, scores, NEG)
        new_top = jnp.maximum(top, jnp.max(scores, -1))
        raw_weight = jnp.where(allowed, jnp.exp(scores - new_top[..., None]), 0.0)
        factor = jnp.exp(top - new_top)
        weight_sum = weight_sum * factor + jnp.sum(raw_weight, -1)
        total = total * factor[..., None] + jnp.einsum(
            "qhk,khd->qhd",
            raw_weight.astype(jnp.bfloat16),
            value_block,
            preferred_element_type=jnp.float32,
        )
        return ((total, new_top, weight_sum), None)

    state, unused = lax.scan(one_block, initial, (key_blocks, value_blocks, doc_blocks, offsets))
    total, top, weight_sum = state
    output_full = total / weight_sum[..., None]
    attn_low = output_full.reshape(rows, width).astype(jnp.bfloat16)
    branch_attn = jnp.dot(attn_low, w_out, preferred_element_type=jnp.float32) + b_out.astype(
        jnp.float32
    )
    upper = jnp.dot(input_two, w_up, preferred_element_type=jnp.float32) + b_up.astype(jnp.float32)
    active, pull_active = jax.vjp(partial(jax.nn.gelu, approximate=False), upper)
    active_low = active.astype(jnp.bfloat16)
    branch_mlp = jnp.dot(active_low, w_down, preferred_element_type=jnp.float32) + b_down.astype(
        jnp.float32
    )
    result = (source + branch_attn + branch_mlp).astype(jnp.bfloat16)[None]
    reused = (
        lax.all_gather(params[0], ("seq", "ctx"), axis=0, tiled=True),
        lax.all_gather(params[1], ("seq", "ctx"), axis=0, tiled=True),
        lax.all_gather(params[2], ("seq", "ctx"), axis=0, tiled=True),
        lax.all_gather(params[3], ("seq", "ctx"), axis=0, tiled=True),
        lax.all_gather(params[4], ("seq", "ctx"), axis=0, tiled=True),
        lax.all_gather(params[5], ("seq", "ctx"), axis=0, tiled=True),
        lax.all_gather(params[6], ("seq", "ctx"), axis=0, tiled=True),
        lax.all_gather(params[7], ("seq", "ctx"), axis=0, tiled=True),
        lax.all_gather(params[8], ("seq", "ctx"), axis=0, tiled=True),
        lax.all_gather(params[9], ("seq", "ctx"), axis=0, tiled=True),
        lax.all_gather(params[10], ("seq", "ctx"), axis=0, tiled=True),
        lax.all_gather(params[11], ("seq", "ctx"), axis=0, tiled=True),
    )
    back_qkv = reused[4]
    back_out = reused[6]
    back_up = reused[8]
    back_down = reused[10]
    cotangent = out_grad[0]
    cotangent_full = cotangent.astype(jnp.float32)
    grad_down_w = contract_rows(active_low, cotangent)
    grad_down_b = jnp.sum(cotangent_full, 0)
    grad_active = contract_cols(cotangent, back_down)
    (grad_upper,) = pull_active(grad_active)
    upper_low = grad_upper.astype(jnp.bfloat16)
    grad_up_w = contract_rows(input_two, upper_low)
    grad_up_b = jnp.sum(upper_low.astype(jnp.float32), 0)
    grad_two = contract_cols(upper_low, back_up)
    grad_out_w = contract_rows(attn_low, cotangent)
    grad_out_b = jnp.sum(cotangent_full, 0)
    grad_attn = contract_cols(cotangent, back_out).astype(jnp.bfloat16).reshape(rows, H, HD)
    delta_term = jnp.sum(grad_attn.astype(jnp.float32) * output_full, -1)
    key_all, value_all, doc_all = (
        lax.all_gather(key_flat, "ctx", axis=0, tiled=True),
        lax.all_gather(value_flat, "ctx", axis=0, tiled=True),
        lax.all_gather(segment_low, "ctx", axis=0, tiled=True),
    )
    length = key_all.shape[0]
    block = math.gcd(length, 512)
    number = length // block

    def block_terms(key_block, value_block, doc_block, offset):
        scores, allowed = masked_scores(key_block, doc_block, offset + jnp.arange(block))
        prob = jnp.where(allowed, jnp.exp(scores - top[..., None]) / weight_sum[..., None], 0.0)
        grad_prob = jnp.einsum(
            "qhd,khd->qhk", grad_attn, value_block, preferred_element_type=jnp.float32
        )
        grad_score = (prob * (grad_prob - delta_term[..., None])).astype(jnp.bfloat16)
        return (prob.astype(jnp.bfloat16), grad_score)

    block_items = (
        key_all.reshape(number, block, H, HD),
        value_all.reshape(number, block, H, HD),
        doc_all.reshape(number, block),
        jnp.arange(number) * block,
    )
    empty_query = jnp.zeros((rows, H, HD), jnp.float32)

    def back_block(grad_query, items):
        key_block, value_block, doc_block, offset = items
        prob_low, grad_score = block_terms(key_block, value_block, doc_block, offset)
        grad_value = jnp.einsum(
            "qhk,qhd->khd", prob_low, grad_attn, preferred_element_type=jnp.float32
        )
        grad_query = grad_query + jnp.einsum(
            "qhk,khd->qhd", grad_score, key_block, preferred_element_type=jnp.float32
        )
        grad_key = jnp.einsum("qhk,qhd->khd", grad_score, query, preferred_element_type=jnp.float32)
        return (grad_query, (grad_key.reshape(block, width), grad_value.reshape(block, width)))

    grad_query, (key_terms, value_terms) = lax.scan(back_block, empty_query, block_items)
    key_sum, value_sum = (
        lax.psum_scatter(
            key_terms.reshape(length, width).astype(jnp.bfloat16),
            "ctx",
            scatter_dimension=0,
            tiled=True,
        ).astype(jnp.float32),
        lax.psum_scatter(
            value_terms.reshape(length, width).astype(jnp.bfloat16),
            "ctx",
            scatter_dimension=0,
            tiled=True,
        ).astype(jnp.float32),
    )
    grad_query_lin = rotate(grad_query * scale, cosine, -sine)
    grad_key_lin = rotate(key_sum.reshape(rows, H, HD), cosine, -sine)
    grad_linear = (
        jnp.stack([grad_query_lin, grad_key_lin, value_sum.reshape(rows, H, HD)], 1)
        .reshape(rows, 3 * width)
        .astype(jnp.bfloat16)
    )
    grad_qkv_w = contract_rows(input_one, grad_linear)
    grad_qkv_b = jnp.sum(grad_linear.astype(jnp.float32), 0)
    grad_one = contract_cols(grad_linear, back_qkv)
    grad_source_one, grad_gain_one, grad_bias_one = pull_one(grad_one)
    grad_source_two, grad_gain_two, grad_bias_two = pull_two(grad_two)
    input_grad = (cotangent_full + grad_source_one + grad_source_two)[None]
    summed = (
        lax.psum_scatter(grad_gain_one, ("seq", "ctx"), scatter_dimension=0, tiled=True),
        lax.psum_scatter(grad_bias_one, ("seq", "ctx"), scatter_dimension=0, tiled=True),
        lax.psum_scatter(grad_gain_two, ("seq", "ctx"), scatter_dimension=0, tiled=True),
        lax.psum_scatter(grad_bias_two, ("seq", "ctx"), scatter_dimension=0, tiled=True),
        lax.psum_scatter(grad_qkv_w, ("seq", "ctx"), scatter_dimension=0, tiled=True),
        lax.psum_scatter(grad_qkv_b, ("seq", "ctx"), scatter_dimension=0, tiled=True),
        lax.psum_scatter(grad_out_w, ("seq", "ctx"), scatter_dimension=0, tiled=True),
        lax.psum_scatter(grad_out_b, ("seq", "ctx"), scatter_dimension=0, tiled=True),
        lax.psum_scatter(grad_up_w, ("seq", "ctx"), scatter_dimension=0, tiled=True),
        lax.psum_scatter(grad_up_b, ("seq", "ctx"), scatter_dimension=0, tiled=True),
        lax.psum_scatter(grad_down_w, ("seq", "ctx"), scatter_dimension=0, tiled=True),
        lax.psum_scatter(grad_down_b, ("seq", "ctx"), scatter_dimension=0, tiled=True),
    )
    return (result, input_grad) + tuple(summed)


def solution(mesh):
    in_specs = (
        P("seq", "ctx", None),
        P("seq", "ctx"),
        P("seq", "ctx"),
        P(("seq", "ctx")),
        P(("seq", "ctx")),
        P(("seq", "ctx")),
        P(("seq", "ctx")),
        P(("seq", "ctx"), None),
        P(("seq", "ctx")),
        P(("seq", "ctx"), None),
        P(("seq", "ctx")),
        P(("seq", "ctx"), None),
        P(("seq", "ctx")),
        P(("seq", "ctx"), None),
        P(("seq", "ctx")),
        P("seq", "ctx", None),
    )
    out_specs = (
        P("seq", "ctx", None),
        P("seq", "ctx", None),
        P(("seq", "ctx")),
        P(("seq", "ctx")),
        P(("seq", "ctx")),
        P(("seq", "ctx")),
        P(("seq", "ctx"), None),
        P(("seq", "ctx")),
        P(("seq", "ctx"), None),
        P(("seq", "ctx")),
        P(("seq", "ctx"), None),
        P(("seq", "ctx")),
        P(("seq", "ctx"), None),
        P(("seq", "ctx")),
    )
    return jax.shard_map(local, mesh=mesh, in_specs=in_specs, out_specs=out_specs, check_vma=False)
```

profile of v0, /device:TPU:6, one launch (start us, length us, event | category | flops | bytes accessed | tf_op | source)
XLA Modules:
  0.0 1183.4 jit_solution(18417885947766031895)
XLA Ops:
  14.6 41.5 %all-reduce.15 = (bf16[1024]{0:T(1024)(128)(2,1)}, bf16[1024]{0:T(1024)(128)(2,1)}, bf16[1024]{0:T(1024)(128)(2,1)}, bf16[3072]{0:T(1024)(128)(2,1)S(1)}, bf16[1...) all-reduce(bf16[1024]{0:T(1024)(128)(2,1)S(1)} %dynamic-update-slic, ...), channel_id=1, replica_groups=mesh['seq'=8,'ctx'=4] {'seq','ctx'}, use_global_device_ids=true, to_apply=%add.5 | all-reduce | flops 9216 | bytes 36864
  60.7 20.2 %all-gather.9.cloned.1.call-done = bf16[1024,3072]{1,0:T(8,128)(2,1)} async-done(((bf16[32,3072]{1,0:T(8,128)(2,1)}), bf16[1024,3072]{1,0:T(8,128)(2,1)}) %all-gather.9.cloned.1.call-update) | async-done | bytes 6291472 | tf_op jit(solution)/shard_map/all_gather | solution.py:92
  81.0 6.5 convolution_add_fusion.1
  93.0 5.4 all-gather
  98.5 40.4 %all-gather.15.cloned.1.call-done = bf16[1024,1024]{1,0:T(8,128)(2,1)} async-done(((bf16[32,1024]{1,0:T(8,128)(2,1)}), bf16[1024,1024]{1,0:T(8,128)(2,1)}) %all-gather.15.cloned.1.call-update) | async-done | bytes 2097168 | tf_op jit(solution)/shard_map/all_gather | solution.py:94
  141.8 20.9 %all-gather.11.cloned.1.call-done = bf16[1024,1024]{0,1:T(8,128)(2,1)} async-done(((bf16[256,1024]{0,1:T(8,128)(2,1)}), bf16[1024,1024]{0,1:T(8,128)(2,1)}) %all-gather.11.cloned.1.call-update) | async-done | bytes 2097168 | tf_op jit(solution)/shard_map/all_gather | solution.py:154
  169.2 18.3 %all-gather.13.cloned.1.call-done = bf16[1024,1024]{0,1:T(8,128)(2,1)} async-done(((bf16[256,1024]{0,1:T(8,128)(2,1)}), bf16[1024,1024]{0,1:T(8,128)(2,1)}) %all-gather.13.cloned.1.call-update) | async-done | bytes 2097168 | tf_op jit(solution)/shard_map/all_gather | solution.py:155
  195.4 32.5 %while.30 = (s32[]{:T(128)}, f32[256,16,64]{0,2,1:T(8,128)}, f32[256,16]{0,1:T(8,128)S(1)}, f32[256,16]{0,1:T(8,128)S(1)}, f32[256]{0:T(256)S(1)}, /*index=5*/bf...) while((s32[]{:T(128)}, f32[256,16,64]{0,2,1:T(8,128)}, ...), condition=%wide.region_5.6_spmd.clone, body=%wide.region_2.5_spmd.clone.sunk | while | flops 559043840 | bytes 64238268 | solution.py:182
  201.5 5.2 fusion.164
  217.6 5.2 fusion.164
  230.1 44.8 %while.31 = (s32[]{:T(128)}, f32[256,16,64]{0,2,1:T(8,128)}, bf16[2,512,1024]{2,1,0:T(8,128)(2,1)}, bf16[2,512,1024]{2,1,0:T(8,128)(2,1)}, bf16[2,512,16,64]{1,3...) while((s32[]{:T(128)}, f32[256,16,64]{0,2,1:T(8,128)}, ...), condition=%wide.region_8.9_spmd.clone, body=%wide.region_7.8_spmd.clone.sunk | while | flops 1357776128 | bytes 139785680 | solution.py:266
  241.2 4.8 fusion.180
  263.4 4.8 fusion.180
  270.2 4.7 fusion.179
  281.3 25.3 %reduce-scatter.7.cloned.1.call-done = bf16[256,1024]{1,0:T(8,128)(2,1)} async-done(((bf16[1024,1024]{1,0:T(8,128)(2,1)}), bf16[256,1024]{1,0:T(8,128)(2,1)}) %reduce-scatter.7.cloned.1.call-update) | async-done | bytes 524304 | tf_op jit(solution)/shard_map/reduce_scatter | solution.py:268
  310.0 30.5 %reduce-scatter.9.cloned.1.call-done = bf16[256,1024]{1,0:T(8,128)(2,1)} async-done(((bf16[1024,1024]{1,0:T(8,128)(2,1)}), bf16[256,1024]{1,0:T(8,128)(2,1)}) %reduce-scatter.9.cloned.1.call-update) | async-done | bytes 524304 | tf_op jit(solution)/shard_map/reduce_scatter | solution.py:274
  343.5 6.5 fusion.81
  350.7 34.2 %all-gather.1 = bf16[32,1,128]{2,1,0:T(2,128)(2,1)S(1)} all-gather(bf16[1,1,128]{2,1,0:T(2,128)(2,1)S(1)} %bitcast.271), channel_id=1, replica_groups=mesh['seq'=8,'ctx'=4] {'seq','ctx'}, dimensions={0}, use_global_device_ids=true | all-gather | bytes 8448 | tf_op jit(solution)/shard_map/all_gather | solution.py:97
  385.0 36.1 %all-gather.17.cloned.1.call-done = bf16[1024,4096]{1,0:T(8,128)(2,1)} async-done(((bf16[32,4096]{1,0:T(8,128)(2,1)}), bf16[1024,4096]{1,0:T(8,128)(2,1)}) %all-gather.17.cloned.1.call-update) | async-done | bytes 8388624 | tf_op jit(solution)/shard_map/all_gather | solution.py:96
  421.1 16.5 %multiply_convert_fusion = (bf16[256,4096]{1,0:T(8,128)(2,1)}, f32[256,4096]{1,0:T(8,128)}, f32[256,4096]{1,0:T(8,128)}) fusion(f32[4096]{0:T(1024)S(1)} %bitcast.269, bf16[1024,4096]{1,0:T(8,128)(2,1)} %all-gather.17.cloned.1.call-done, bf16[1,256,1024]{2,1,0:T(8,128)(2,1)S(1)} %copy-done.10, f32[1024]{0:T(1024)S(1)} %convert_element_type.175, ...), kind=kOutput, calls=%fused_computation.60 | convolution fusion | flops 2218262528 | bytes 19425280 | tf_op jit(solution)/shard_map/dot_general | solution.py:189
  437.6 62.5 %all-gather.19.cloned.1.call-done = bf16[4096,1024]{1,0:T(8,128)(2,1)} async-done(((bf16[128,1024]{1,0:T(8,128)(2,1)}), bf16[4096,1024]{1,0:T(8,128)(2,1)}) %all-gather.19.cloned.1.call-update) | async-done | bytes 8388624 | tf_op jit(solution)/shard_map/all_gather | solution.py:98
  500.1 11.4 convert_reduce_fusion
  512.9 8.3 fusion.104
  521.4 9.7 fusion.84
  531.8 6.5 convolution_add_fusion.3
  540.0 6.7 fusion.114
  546.8 5.3 fusion.110
  554.8 42.2 %all-reduce.14 = (f32[1024]{0:T(1024)S(1)}, f32[1024]{0:T(1024)S(1)}, f32[1024]{0:T(1024)S(1)}, f32[1024]{0:T(1024)S(1)}, f32[3072]{0:T(1024)S(1)}, /*index=5*/f32[1024]{0:T(1024)S(1)}, f32[4096]{0:T(1024)S(1)}) all-reduce(f32[1024]{0:T(1024)S(1)} %get-tuple-element.324, ...), channel_id=5, replica_groups=mesh['seq'=8,'ctx'=4] {'seq','ctx'}, use_global_device_ids=true, to_apply=%region_16.17.clone | all-reduce | flops 12288 | bytes 98304
  600.5 27.7 %reduce-scatter.13.cloned.1.call-done = f32[32,1024]{1,0:T(8,128)} async-done(((f32[1024,1024]{1,0:T(8,128)}), f32[32,1024]{1,0:T(8,128)}) %reduce-scatter.13.cloned.1.call-update) | async-done | bytes 131088 | tf_op jit(solution)/shard_map/reduce_scatter | solution.py:301
  628.2 173.1 %reduce-scatter.11.cloned.1.call-done = f32[32,3072]{1,0:T(8,128)} async-done(((f32[1024,3072]{1,0:T(8,128)}), f32[32,3072]{1,0:T(8,128)}) %reduce-scatter.11.cloned.1.call-update) | async-done | bytes 393232 | tf_op jit(solution)/shard_map/reduce_scatter | solution.py:299
  801.3 187.3 %reduce-scatter.15.cloned.1.call-done = f32[32,4096]{1,0:T(8,128)} async-done(((f32[1024,4096]{1,0:T(8,128)}), f32[32,4096]{1,0:T(8,128)}) %reduce-scatter.15.cloned.1.call-update) | async-done | bytes 524304 | tf_op jit(solution)/shard_map/reduce_scatter | solution.py:303
  988.6 187.3 %reduce-scatter.17.cloned.1.call-done = f32[128,1024]{1,0:T(8,128)} async-done(((f32[4096,1024]{1,0:T(8,128)}), f32[128,1024]{1,0:T(8,128)}) %reduce-scatter.17.cloned.1.call-update) | async-done | bytes 524304 | tf_op jit(solution)/shard_map/reduce_scatter | solution.py:305
  (248 shorter events, 112.7 us)
Async XLA Ops:
  7.2 73.8 %all-gather.9.cloned.1.call-start = ((), (), s32[]{:S(2)}) async-start(), calls=%async_computation.6 | async-start | bytes 6488064 | tf_op jit(solution)/shard_map/all_gather | solution.py:92
  7.9 130.9 %all-gather.15.cloned.1.call-start = ((), (), s32[]{:S(2)}) async-start(), calls=%async_computation.9 | async-start | bytes 2162688 | tf_op jit(solution)/shard_map/all_gather | solution.py:94
  8.7 154.0 %all-gather.11.cloned.1.call-start = ((), (), s32[]{:S(2)}) async-start(), calls=%async_computation.7 | async-start | bytes 2621440 | tf_op jit(solution)/shard_map/all_gather | solution.py:154
  56.1 24.9 %copy-start.21 = (f32[1024]{0:T(1024)}, f32[1024]{0:T(1024)S(1)}, u32[]{:S(2)}) copy-start(f32[1024]{0:T(1024)S(1)} %convert_element_type.161) | copy-start | bytes 12292
  56.1 24.9 %copy-start.23 = (f32[1024]{0:T(1024)}, f32[1024]{0:T(1024)S(1)}, u32[]{:S(2)}) copy-start(f32[1024]{0:T(1024)S(1)} %convert_element_type.162) | copy-start | bytes 12292
  58.0 23.0 %copy-start.25 = (f32[256]{0:T(256)}, f32[256]{0:T(256)S(1)}, u32[]{:S(2)}) copy-start(f32[256]{0:T(256)S(1)} %broadcast_multiply_fusion.1) | copy-start | bytes 3076
  60.0 21.0 %copy-start.29 = (f32[256]{0:T(256)}, f32[256]{0:T(256)S(1)}, u32[]{:S(2)}) copy-start(f32[256]{0:T(256)S(1)} %fusion.103) | copy-start | bytes 3076
  60.7 29.4 %copy-start.27 = (f32[256,8]{0,1:T(8,128)}, f32[256,8]{0,1:T(8,128)S(1)}, u32[]{:S(2)}) copy-start(f32[256,8]{0,1:T(8,128)S(1)} %get-tuple-element.425) | copy-start | bytes 24580
  92.0 95.6 %all-gather.13.cloned.1.call-start = ((), (), s32[]{:S(2)}) async-start(), calls=%async_computation.8 | async-start | bytes 2621440 | tf_op jit(solution)/shard_map/all_gather | solution.py:155
  92.9 48.7 %copy-start.16 = (f32[256,16,64]{0,2,1:T(8,128)S(1)}, f32[256,16,64]{0,2,1:T(8,128)}, u32[]{:S(2)}) copy-start(f32[256,16,64]{0,2,1:T(8,128)} %copy-done.15) | copy-start | bytes 3145732
  92.9 213.7 %reduce-scatter.7.cloned.1.call-start = ((), (), s32[]{:S(2)}) async-start(), calls=%async_computation.12 | async-start | bytes 2621440 | tf_op jit(solution)/shard_map/reduce_scatter | solution.py:268
  201.5 5.8 copy-start.1
  217.6 5.8 copy-start.1
  275.0 65.6 %reduce-scatter.9.cloned.1.call-start = ((), (), s32[]{:S(2)}) async-start(), calls=%async_computation.13 | async-start | bytes 2621440 | tf_op jit(solution)/shard_map/reduce_scatter | solution.py:274
  275.6 145.5 %all-gather.17.cloned.1.call-start = ((), (), s32[]{:S(2)}) async-start(), calls=%async_computation.10 | async-start | bytes 8650752 | tf_op jit(solution)/shard_map/all_gather | solution.py:96
  276.3 223.8 %all-gather.19.cloned.1.call-start = ((), (), s32[]{:S(2)}) async-start(), calls=%async_computation.11 | async-start | bytes 8650752 | tf_op jit(solution)/shard_map/all_gather | solution.py:98
  277.1 351.1 %reduce-scatter.13.cloned.1.call-start = ((), (), s32[]{:S(2)}) async-start(), calls=%async_computation.15 | async-start | bytes 4325376 | tf_op jit(solution)/shard_map/reduce_scatter | solution.py:301
  279.9 61.9 %copy-start.28 = (f32[256,8]{0,1:T(8,128)S(1)}, f32[256,8]{0,1:T(8,128)}, u32[]{:S(2)}) copy-start(f32[256,8]{0,1:T(8,128)} %copy-done.27) | copy-start | bytes 24580
  279.9 61.9 %copy-start.31 = (f32[256,8]{0,1:T(8,128)S(1)}, f32[256,8]{0,1:T(8,128)}, u32[]{:S(2)}) copy-start(f32[256,8]{0,1:T(8,128)} %get-tuple-element.423) | copy-start | bytes 24580
  280.0 521.3 %reduce-scatter.11.cloned.1.call-start = ((), (), s32[]{:S(2)}) async-start(), calls=%async_computation.14 | async-start | bytes 12976128 | tf_op jit(solution)/shard_map/reduce_scatter | solution.py:299
  308.8 34.7 %copy-start.10 = (bf16[1,256,1024]{2,1,0:T(8,128)(2,1)S(1)}, bf16[1,256,1024]{2,1,0:T(8,128)(2,1)}, u32[]{:S(2)}) copy-start(bf16[1,256,1024]{2,1,0:T(8,128)(2,1)} %param.20) | copy-start | bytes 1572868
  308.8 34.7 %copy-start.22 = (f32[1024]{0:T(1024)S(1)}, f32[1024]{0:T(1024)}, u32[]{:S(2)}) copy-start(f32[1024]{0:T(1024)} %copy-done.21) | copy-start | bytes 12292
  308.8 34.7 %copy-start.24 = (f32[1024]{0:T(1024)S(1)}, f32[1024]{0:T(1024)}, u32[]{:S(2)}) copy-start(f32[1024]{0:T(1024)} %copy-done.23) | copy-start | bytes 12292
  308.8 34.7 %copy-start.26 = (f32[256]{0:T(256)S(1)}, f32[256]{0:T(256)}, u32[]{:S(2)}) copy-start(f32[256]{0:T(256)} %copy-done.25) | copy-start | bytes 3076
  308.8 34.7 %copy-start.30 = (f32[256]{0:T(256)S(1)}, f32[256]{0:T(256)}, u32[]{:S(2)}) copy-start(f32[256]{0:T(256)} %copy-done.29) | copy-start | bytes 3076
  350.1 638.5 %reduce-scatter.15.cloned.1.call-start = ((), (), s32[]{:S(2)}) async-start(), calls=%async_computation.16 | async-start | bytes 17301504 | tf_op jit(solution)/shard_map/reduce_scatter | solution.py:303
  421.1 79.0 %copy-start.14 = (bf16[1,256,1024]{2,1,0:T(8,128)(2,1)S(1)}, bf16[1,256,1024]{2,1,0:T(8,128)(2,1)}, u32[]{:S(2)}) copy-start(bf16[1,256,1024]{2,1,0:T(8,128)(2,1)} %param.35) | copy-start | bytes 1572868
  521.2 654.7 %reduce-scatter.17.cloned.1.call-start = ((), (), s32[]{:S(2)}) async-start(), calls=%async_computation.17 | async-start | bytes 17301504 | tf_op jit(solution)/shard_map/reduce_scatter | solution.py:305
  531.8 6.5 copy-start.18
  546.8 5.3 copy-start.33
  546.8 5.3 copy-start.17
  597.0 579.4 %copy-start.40 = (f32[32]{0:T(128)}, f32[32]{0:T(128)S(1)}, u32[]{:S(2)}) copy-start(f32[32]{0:T(128)S(1)} %dynamic-slice.5) | copy-start | bytes 388
  (31 other events, 83.2 us)
Sparse Core Ops, SparseCore 0:
  10.9 70.0 all-gather.8
  83.8 54.9 all-gather.14
  141.0 21.6 all-gather.10
  164.7 22.8 all-gather.12
  275.1 31.4 reduce-scatter.6
  309.1 31.3 reduce-scatter.8
  343.4 77.6 all-gather.16
  423.9 76.1 all-gather.18
  503.0 125.1 reduce-scatter.12
  634.7 166.5 reduce-scatter.10
  804.3 184.2 reduce-scatter.14
  991.4 184.4 reduce-scatter.16
where the time goes:
time: 1190 us; the launch traced here: 1180 us
  waiting for transfers between devices  833 us (70%)
  matrix products  130 us (11%)
  blocking collectives  123 us (10%)
  local copies, waits for them, and re-layouts  54.8 us (5%)
  other arithmetic  25.7 us (2%)
  between operations  14.9 us (1%)
    reduce_scatter x1, waiting for transfers between devices, local(): lax.psum_scatter(grad_up_w, ('seq', 'ctx'), scatter_dimension=0, tiled=True)  187 us
    reduce_scatter x1, waiting for transfers between devices, local(): lax.psum_scatter(grad_down_w, ('seq', 'ctx'), scatter_dimension=0, tiled=...  187 us
    reduce_scatter x1, waiting for transfers between devices, local(): lax.psum_scatter(grad_qkv_w, ('seq', 'ctx'), scatter_dimension=0, tiled=T...  173 us
    unnamed x2, blocking collectives  83.6 us
    all_gather x1, waiting for transfers between devices, local(): lax.all_gather(params[10], ('seq', 'ctx'), axis=0, tiled=True)  62.5 us
    all_gather x1, waiting for transfers between devices, local(): lax.all_gather(params[6], ('seq', 'ctx'), axis=0, tiled=True)  40.4 us
    all_gather x1, waiting for transfers between devices, local(): lax.all_gather(params[8], ('seq', 'ctx'), axis=0, tiled=True)  36.1 us
    all_gather x1, blocking collectives, local(): lax.all_gather(params[9], ('seq', 'ctx'), axis=0, tiled=True)  34.2 us
  transfers between devices with their start and end apart: 12, of which 12 were waited for; matrix products, arithmetic and copies ran while one was open for 10% of the time, Pallas kernels for 0%

commit v1 on v0

v1 whole, which is shorter than its diff:
```python
from functools import partial
import math

import jax
import jax.numpy as jnp
from jax import lax
from jax.experimental import pallas as pl
from jax.experimental.pallas import tpu as pltpu
from jax.sharding import PartitionSpec as P

H = 16
HD = 64
ROT = 16

EPS = 1e-05
NEG = -1000000000.0
BF = jnp.bfloat16
F32 = jnp.float32


def contract_rows(left, right):
    return lax.dot_general(left, right, (((0,), (0,)), ((), ())), preferred_element_type=F32)


def contract_cols(left, right):
    return lax.dot_general(left, right, (((1,), (1,)), ((), ())), preferred_element_type=F32)


def dot(left, right):
    return jnp.dot(left, right, preferred_element_type=F32)


def swap(value, axis, size, bits):
    return lax.ppermute(value, axis, [(i, i ^ bits) for i in range(size)])


def transpose_owner(value, seq, ctx, back=False):
    pairs = [(c * seq + s, s * ctx + c) for s in range(seq) for c in range(ctx)]
    if back:
        pairs = [(b, a) for a, b in pairs]
    return lax.ppermute(value, ("seq", "ctx"), pairs)


def outer_groups(seq):
    return [[2 * z + x for z in range(seq // 2)] for x in range(2)]


def gather_seq(shard, seq, inner):
    own = lax.all_gather(shard, "seq", axis=0, axis_index_groups=outer_groups(seq))
    other = swap(own, "seq", seq, 1)
    first = jnp.where(inner == 0, own, other)
    second = jnp.where(inner == 0, other, own)
    return jnp.stack([first, second], 1).reshape((seq,) + shard.shape)


def scatter_seq(terms, seq, inner):
    split = terms.astype(BF).reshape((seq // 2, 2) + terms.shape[1:])
    sent = lax.dynamic_index_in_dim(split, 1 - inner, 1, keepdims=False)
    kept = lax.dynamic_index_in_dim(split, inner, 1, keepdims=False)
    got = swap(sent, "seq", seq, 1)
    half = (kept.astype(F32) + got.astype(F32)).astype(BF)
    out = lax.psum_scatter(
        half, "seq", scatter_dimension=0, tiled=True, axis_index_groups=outer_groups(seq)
    )
    return out[0]


def gather_ctx(own, ctx):
    even = [own] + [swap(own, "ctx", ctx, k) for k in range(2, ctx, 2)]
    odd = [swap(block, "ctx", ctx, 1) for block in even]
    return even + odd


def natural(blocks, index):
    count = len(blocks)
    half = count // 2
    values = [blocks[(k >> 1) + (k & 1) * half] for k in range(count)]
    bit = 1
    while bit < count:
        on = (index & bit) != 0
        values = [jnp.where(on, values[k ^ bit], values[k]) for k in range(count)]
        bit *= 2
    return values


def scatter_ctx(terms, ctx):
    low = terms.astype(BF)
    half = low.shape[0] // 2
    rows = low.shape[0] // ctx
    got = swap(low[half:], "ctx", ctx, 1)
    pair = low[:half].astype(F32) + got.astype(F32)
    total = pair[:rows]
    for k in range(2, ctx, 2):
        block = pair[(k // 2) * rows : (k // 2 + 1) * rows].astype(BF)
        total = total + swap(block, "ctx", ctx, k).astype(F32)
    return total


def attend_kernel(
    heads,
    ctx,
    spot_ref,
    linear_ref,
    cos_ref,
    sin_ref,
    seg_col_ref,
    seg_row_ref,
    grad_ref,
    out_ref,
    back_ref,
    q_s,
    k_s,
    v_s,
    g_s,
    dq_s,
    dk_s,
    dv_s,
):
    length = linear_ref.shape[0]
    width = grad_ref.shape[1]
    rows = length // ctx
    block = math.gcd(rows, 256)
    scale = 1.0 / math.sqrt(HD)
    lane = lax.broadcasted_iota(jnp.int32, (rows, width), 1) % HD
    low_lane = lane < ROT // 2
    spot = spot_ref[0]

    def place(i):
        other = spot ^ i
        return pl.multiple_of(((other >> 1) + (other & 1) * (ctx // 2)) * rows, rows)

    def turn(u, cosine, sine):
        moved = jnp.where(
            low_lane, pltpu.roll(u, width - ROT // 2, 1), pltpu.roll(u, ROT // 2, 1)
        )
        return u * cosine + moved * sine

    def split(target, value, i):
        low = value.astype(BF)
        for h in range(heads):
            target[h, pl.ds(i * rows, rows), :] = low[:, h * HD : (h + 1) * HD]

    def join(source, i):
        return jnp.concatenate([source[h, pl.ds(i * rows, rows), :] for h in range(heads)], -1)

    def prepare(i, carry):
        at = pl.ds(place(i), rows)
        cosine, sine = cos_ref[at, :], sin_ref[at, :]
        split(q_s, turn(linear_ref[at, 0:width], cosine, sine) * scale, i)
        split(k_s, turn(linear_ref[at, width : 2 * width], cosine, sine), i)
        split(v_s, linear_ref[at, 2 * width : 3 * width], i)
        split(g_s, grad_ref[at, :], i)
        return carry

    lax.fori_loop(0, ctx, prepare, 0)
    dk_s[...] = jnp.zeros_like(dk_s)
    dv_s[...] = jnp.zeros_like(dv_s)

    def one(h, start, size):
        at = pl.ds(start, block)
        query, grad = q_s[h, at, :], g_s[h, at, :]
        keys, values = k_s[h, 0:size, :], v_s[h, 0:size, :]
        scores = contract_cols(query, keys)
        row = start + lax.broadcasted_iota(jnp.int32, (block, size), 0)
        col = lax.broadcasted_iota(jnp.int32, (block, size), 1)
        allowed = (seg_col_ref[at, :] == seg_row_ref[:, 0:size]) & (row >= col)
        scores = jnp.where(allowed, scores, NEG)
        raw = jnp.exp(scores - jnp.max(scores, -1, keepdims=True))
        prob = raw * (1.0 / jnp.sum(raw, -1, keepdims=True))
        prob_low = prob.astype(BF)
        grad_prob = contract_cols(grad, values)
        delta = jnp.sum(prob * grad_prob, -1, keepdims=True)
        grad_score = (prob * (grad_prob - delta)).astype(BF)
        dv_s[h, 0:size, :] += contract_rows(prob_low, grad)
        dk_s[h, 0:size, :] += contract_rows(grad_score, query)
        dq_s[h, at, :] = dot(grad_score, keys)
        q_s[h, at, :] = dot(prob_low, values).astype(BF)

    count = length // block
    if count <= 4:

        def each(h, carry):
            for i in range(count):
                one(h, i * block, (i + 1) * block)
            return carry

        lax.fori_loop(0, heads, each, 0)
    else:

        def each(step, carry):
            one(step // count, pl.multiple_of(step % count * block, block), length)
            return carry

        lax.fori_loop(0, heads * count, each, 0)

    def finish(i, carry):
        at = pl.ds(place(i), rows)
        cosine, sine = cos_ref[at, :], -sin_ref[at, :]
        out_ref[at, :] = join(q_s, i)
        back_ref[at, 0:width] = (turn(join(dq_s, i) * scale, cosine, sine)).astype(BF)
        back_ref[at, width : 2 * width] = turn(join(dk_s, i), cosine, sine).astype(BF)
        back_ref[at, 2 * width : 3 * width] = join(dv_s, i).astype(BF)
        return carry

    lax.fori_loop(0, ctx, finish, 0)


def attend(spot, linear, cosine, sine, seg, grad, heads, ctx):
    length, width = grad.shape
    whole = lambda: pl.BlockSpec(memory_space=pltpu.VMEM)
    shape = (heads, length, HD)
    return pl.pallas_call(
        partial(attend_kernel, heads, ctx),
        out_shape=(
            jax.ShapeDtypeStruct((length, width), BF),
            jax.ShapeDtypeStruct((length, 3 * width), BF),
        ),
        in_specs=[pl.BlockSpec(memory_space=pltpu.SMEM)] + [whole() for _ in range(6)],
        out_specs=(whole(), whole()),
        scratch_shapes=[pltpu.VMEM(shape, BF)] * 4 + [pltpu.VMEM(shape, F32)] * 3,
        compiler_params=pltpu.CompilerParams(vmem_limit_bytes=60 * 1024 * 1024),
        cost_estimate=pl.CostEstimate(
            flops=12 * heads * length * length * HD,
            bytes_accessed=16 * length * width,
            transcendentals=heads * length * length,
        ),
        name="attend",
    )(spot[None], linear, cosine, sine, seg[:, None], seg[None, :], grad)


def local(
    seq,
    ctx,
    hidden_in,
    segments,
    positions,
    ln1_gain,
    ln1_bias,
    ln2_gain,
    ln2_bias,
    qkv_weight,
    qkv_bias,
    out_weight,
    out_bias,
    up_weight,
    up_bias,
    down_weight,
    down_bias,
    out_grad,
):
    spot = lax.axis_index("ctx")
    inner = lax.axis_index("seq") % 2
    tokens, width = hidden_in.shape[1:]
    rows = qkv_weight.shape[0]
    depth = rows * ctx
    hidden = up_weight.shape[1]
    piece = hidden // (seq * ctx)
    share = hidden // ctx
    heads = H // ctx
    part = heads * HD
    source_own = hidden_in[0]
    cotangent_own = out_grad[0]

    out_part = transpose_owner(out_weight, seq, ctx)
    first_shard = jnp.concatenate([down_weight, out_part], 0)
    first = gather_seq(first_shard, seq, inner)

    qkv_cut = qkv_weight.reshape(rows, 3, ctx, part).transpose(2, 0, 1, 3)
    up_cut = up_weight.reshape(rows, seq, ctx, piece).transpose(2, 0, 1, 3)
    ratio = hidden // width
    small = jnp.stack([ln1_gain, ln1_bias, ln2_gain, ln2_bias, out_bias, down_bias], 1)
    small = jnp.concatenate(
        [small, qkv_bias.reshape(rows, 3), up_bias.reshape(rows, ratio)], 1
    )
    count = small.shape[1]
    small = jnp.pad(small, ((0, 0), (0, 128 - count)))
    payload = jnp.concatenate(
        [
            qkv_cut.reshape(ctx, rows, 3 * part),
            up_cut.reshape(ctx, rows, share),
            jnp.broadcast_to(small[None], (ctx, rows, 128)),
        ],
        2,
    )
    payload = lax.all_to_all(payload, "ctx", 0, 0, tiled=True).reshape(depth, -1)
    second = gather_seq(payload[:, 3 * part :], seq, inner)
    third = gather_seq(payload[:, : 3 * part], seq, inner)

    w_down = first[:, : hidden // (seq * ctx)].reshape(share, width)
    w_out = first[:, hidden // (seq * ctx) :].reshape(part, width)
    second = second.reshape(width, share + 128)
    w_up = second[:, :share]
    vectors = second[:, share : share + count]
    gain_one, bias_one, gain_two, bias_two, b_out, b_down = vectors[:, :6].astype(F32).T
    b_qkv = vectors[:, 6:9].reshape(3, ctx, part)
    b_qkv = lax.dynamic_index_in_dim(b_qkv, spot, 1, keepdims=False).reshape(-1).astype(F32)
    b_up = vectors[:, 9:].reshape(seq, ctx, piece)
    b_up = lax.dynamic_index_in_dim(b_up, spot, 1, keepdims=False).reshape(-1).astype(F32)
    w_qkv = third.reshape(width, 3 * part)

    source = jnp.concatenate(gather_ctx(source_own, ctx), 0)
    cotangent = jnp.concatenate(gather_ctx(cotangent_own, ctx), 0)
    marks = gather_ctx(jnp.concatenate([segments, positions], 0), ctx)
    places = jnp.concatenate([mark[1] for mark in marks], 0)
    seg = jnp.concatenate([mark[0] for mark in natural(marks, spot)], 0)

    index = jnp.arange(ROT // 2).astype(F32)
    frequency = 10000.0 ** (-2.0 * index / ROT)
    theta = places.astype(F32)[None, :] * frequency[:, None]
    cosine, sine = jnp.cos(theta), jnp.sin(theta)
    length = places.shape[0]
    cos_wide = jnp.concatenate([cosine, cosine, jnp.ones((HD - ROT, length), F32)], 0)
    sin_wide = jnp.concatenate([-sine, sine, jnp.zeros((HD - ROT, length), F32)], 0)
    cos_wide = jnp.tile(cos_wide.T, (1, heads))
    sin_wide = jnp.tile(sin_wide.T, (1, heads))

    wide = source.astype(F32)
    average = jnp.mean(wide, -1, keepdims=True)
    centred = wide - average
    inverse = lax.rsqrt(jnp.mean(centred * centred, -1, keepdims=True) + EPS)
    unit = centred * inverse
    input_one = (unit * gain_one + bias_one).astype(BF)
    input_two = (unit * gain_two + bias_two).astype(BF)

    grad_active = contract_cols(cotangent, w_down)
    upper = dot(input_two, w_up) + b_up
    cdf = 0.5 * lax.erfc(-upper * math.sqrt(0.5))
    active = (upper * cdf).astype(BF)
    density = jnp.exp(-0.5 * upper * upper) * (1.0 / math.sqrt(2.0 * math.pi))
    upper_low = (grad_active * (cdf + upper * density)).astype(BF)
    down_terms = contract_rows(active, cotangent).reshape(seq, piece, width)
    up_terms = contract_rows(input_two, upper_low).reshape(seq, depth, share)
    grad_down_w = scatter_seq(down_terms, seq, inner).astype(F32)
    up_sum = scatter_seq(up_terms, seq, inner)
    up_back = lax.all_to_all(up_sum.reshape(ctx, rows, share), "ctx", 0, 0, tiled=True)
    grad_up_w = (
        up_back.reshape(ctx, rows, seq, piece).transpose(1, 2, 0, 3).reshape(rows, hidden)
    ).astype(F32)
    grad_up_b = jnp.sum(upper_low.astype(F32), 0)
    branch_mlp = dot(active, w_down)
    grad_two = contract_cols(upper_low, w_up)

    grad_attn = contract_cols(cotangent, w_out).astype(BF)
    linear = dot(input_one, w_qkv) + b_qkv
    attended, grad_linear = attend(
        spot, linear, cos_wide, sin_wide, seg, grad_attn, heads, ctx
    )
    hidden_part = branch_mlp + dot(attended, w_out)
    hidden_sum = scatter_ctx(hidden_part, ctx)
    result = (source_own.astype(F32) + hidden_sum + (b_out + b_down)).astype(BF)[None]

    grad_one = contract_cols(grad_linear, w_qkv)
    qkv_terms = contract_rows(input_one, grad_linear).astype(BF)
    out_terms = contract_rows(attended, cotangent).astype(BF)
    cotangent_full = cotangent_own.astype(F32)
    grad_bias = jnp.sum(cotangent_full, 0)
    grad_qkv_b = jnp.sum(grad_linear.astype(F32), 0).reshape(3, 1, part)
    mine = (jnp.arange(ctx) == spot)[None, :, None]
    grad_qkv_b = jnp.where(mine, grad_qkv_b, 0.0).reshape(width, 3)
    pad_up = (-piece) % depth
    grad_up_b = jnp.pad(grad_up_b.reshape(seq, piece), ((0, 0), (0, pad_up))).reshape(
        seq, -1, depth
    )
    table = jnp.stack(
        [
            jnp.sum(grad_one * unit, 0),
            jnp.sum(grad_one, 0),
            jnp.sum(grad_two * unit, 0),
            jnp.sum(grad_two, 0),
            grad_bias,
        ]
        + [grad_qkv_b[:, k] for k in range(3)]
        + [grad_up_b[:, k].reshape(-1) for k in range(grad_up_b.shape[1])],
        0,
    )
    table = jnp.pad(table, ((0, 128 - table.shape[0]), (0, 0))).T.astype(BF)
    out_rows = part // seq
    cuts = depth // out_rows
    out_terms = out_terms.reshape(seq, out_rows, cuts, width // cuts).transpose(0, 2, 1, 3)
    last = jnp.concatenate(
        [
            qkv_terms.reshape(seq, depth, 3 * part),
            out_terms.reshape(seq, depth, width // cuts),
            table.reshape(seq, depth, 128),
        ],
        2,
    )
    last = scatter_seq(last, seq, inner)
    qkv_sum, out_sum, table = (
        last[:, : 3 * part],
        last[:, 3 * part : 3 * part + width // cuts],
        last[:, 3 * part + width // cuts :],
    )
    out_sum = out_sum.reshape(cuts, out_rows, width // cuts).transpose(1, 0, 2)
    grad_out_w = transpose_owner(
        out_sum.reshape(out_rows, width), seq, ctx, back=True
    ).astype(F32)
    grad_up_b = table[:, 8 : 8 + grad_up_b.shape[1]].T.reshape(-1)[:piece].astype(F32)
    back = jnp.concatenate([qkv_sum, table], 1).reshape(ctx, rows, 3 * part + 128)
    back = lax.all_to_all(back, "ctx", 0, 0, tiled=True)
    grad_qkv_w = (
        back[:, :, : 3 * part]
        .reshape(ctx, rows, 3, part)
        .transpose(1, 2, 0, 3)
        .reshape(rows, 3 * width)
        .astype(F32)
    )
    vectors = jnp.sum(back[:, :, 3 * part :].astype(F32), 0)
    grad_qkv_b = vectors[:, 5:8].reshape(-1)

    flow = scatter_ctx(grad_one * gain_one + grad_two * gain_two, ctx)
    unit_own = unit[:tokens]
    passed = (
        flow
        - jnp.mean(flow, -1, keepdims=True)
        - unit_own * jnp.mean(flow * unit_own, -1, keepdims=True)
    ) * inverse[:tokens]
    input_grad = (cotangent_full + passed)[None]
    return (
        result,
        input_grad,
        vectors[:, 0],
        vectors[:, 1],
        vectors[:, 2],
        vectors[:, 3],
        grad_qkv_w,
        grad_qkv_b,
        grad_out_w,
        vectors[:, 4],
        grad_up_w,
        grad_up_b,
        grad_down_w,
        vectors[:, 4],
    )


def solution(mesh):
    both = P(("seq", "ctx"))
    matrix = P(("seq", "ctx"), None)
    row = P("seq", "ctx", None)
    params = (both, both, both, both, matrix, both, matrix, both, matrix, both, matrix, both)
    in_specs = (row, P("seq", "ctx"), P("seq", "ctx")) + params + (row,)
    out_specs = (row, row) + params
    body = partial(local, mesh.shape["seq"], mesh.shape["ctx"])
    return jax.shard_map(body, mesh=mesh, in_specs=in_specs, out_specs=out_specs, check_vma=False)
```

time: 1190 us -> 345 us (0.29)
  waiting for transfers between devices: 833 us -> 101 us
  blocking collectives: 123 us -> 32 us
  matrix products: 130 us -> 62.1 us
  starting transfers between devices: 0.65 us -> 34.4 us
  Pallas kernels: 0 us -> 25.7 us
  local copies, waits for them, and re-layouts: 54.8 us -> 36.1 us
    reduce_scatter x6 -> x3, waiting for transfers between devices: 631 us -> 11.2 us  [scatter_seq(): lax.psum_scatter(half, 'seq', scatter_dimension=0, tiled=True, axis_index...]
    all_gather x6 -> x2, waiting for transfers between devices: 198 us -> 0.02 us  [gather_seq(): lax.all_gather(shard, 'seq', axis=0, axis_index_groups=outer_groups(seq))]
    ppermute x0 -> x21, waiting for transfers between devices: none -> 87.6 us  [the longest x19 75.7 us: swap(): return lax.ppermute(value, axis, [(i, i ^ bits) for i in range(size)])]
    unnamed x2 -> x0, blocking collectives: 83.6 us -> none
    dot_general x18 -> x4, matrix products: 77.3 us -> 24.9 us  [dot(): return jnp.dot(left, right, preferred_element_type=F32)]
    pallas_call x0 -> x1, Pallas kernels: none -> 25.7 us  [attend(): pl.pallas_call(partial(attend_kernel, heads, ctx), out_shape=(jax.ShapeDt...]
    ppermute x0 -> x21, starting transfers between devices: none -> 25.4 us  [the longest x19 16.2 us: swap(): return lax.ppermute(value, axis, [(i, i ^ bits) for i in range(size)])]
    all_gather x2 -> x1, blocking collectives: 39.6 us -> 22.1 us  [gather_seq(): lax.all_gather(shard, 'seq', axis=0, axis_index_groups=outer_groups(seq))]
  transfers between devices with their start and end apart: 12 -> 28, of which waited for: 12 -> 11; matrix products, arithmetic and copies ran while one was open for 10% -> 33% of each run, Pallas kernels for 0% -> 8%
where the time goes in v1:
time: 345 us; the launch traced here: 340 us
  waiting for transfers between devices  101 us (29%)
  matrix products  62.1 us (18%)
  local copies, waits for them, and re-layouts  36.1 us (10%)
  starting transfers between devices  34.4 us (10%)
  other arithmetic  33.3 us (10%)
  blocking collectives  32 us (9%)
  Pallas kernels  25.7 us (7%)
  between operations  15 us (4%)
    ppermute x19, waiting for transfers between devices, swap(): return lax.ppermute(value, axis, [(i, i ^ bits) for i in range(size)])  75.7 us
    pallas_call x1, Pallas kernels, attend(): pl.pallas_call(partial(attend_kernel, heads, ctx), out_shape=(jax.ShapeDt...  25.7 us
    dot_general x4, matrix products, dot(): return jnp.dot(left, right, preferred_element_type=F32)  24.9 us
    dot_general x4, matrix products, contract_cols(): lax.dot_general(left, right, (((1,), (1,)), ((), ())), preferred_element_...  22.4 us
    all_gather x1, blocking collectives, gather_seq(): lax.all_gather(shard, 'seq', axis=0, axis_index_groups=outer_groups(seq))  22.1 us
    ppermute x19, starting transfers between devices, swap(): return lax.ppermute(value, axis, [(i, i ^ bits) for i in range(size)])  16.2 us
    dot_general x4, matrix products, contract_rows(): lax.dot_general(left, right, (((0,), (0,)), ((), ())), preferred_element_...  14.9 us
    ppermute x2, waiting for transfers between devices, transpose_owner(): return lax.ppermute(value, ('seq', 'ctx'), pairs)  11.8 us
  transfers between devices with their start and end apart: 28, of which 11 were waited for; matrix products, arithmetic and copies ran while one was open for 33% of the time, Pallas kernels for 8%

profile of v1, /device:TPU:6, one launch (start us, length us, event | category | flops | bytes accessed | tf_op | source)
XLA Modules:
  0.0 340.1 jit_solution(4746716803878460105)
XLA Ops:
  16.3 9.9 %all_to_all.15 = bf16[4,32,1920]{2,1,0:T(8,128)(2,1)S(1)} all-to-all(bf16[4,32,1920]{2,1,0:T(8,128)(2,1)S(1)} %pad_maximum_fusion.6), channel_id=1, replica_groups=mesh['seq'=8,'ctx'=4] {'ctx'}, dimensions={0} | all-to-all | bytes 983040 | tf_op jit(solution)/shard_map/all_to_all | solution.py:285
  33.2 9.5 %collective-permute-done.7 = s32[2,256]{1,0:T(2,128)S(1)} collective-permute-done((s32[2,256]{1,0:T(2,128)S(1)}, s32[2,256]{1,0:T(2,128)S(1)}, u32[]{:S(2)}, u32[]{:S(2)}) %collective-permute-start.7) | collective-permute-done | bytes 2080 | tf_op jit(solution)/shard_map/ppermute | solution.py:34
  44.2 6.6 %collective-permute-start.4 = (bf16[32,1024]{1,0:T(8,128)(2,1)S(1)}, bf16[32,1024]{1,0:T(8,128)(2,1)S(1)}, u32[]{:S(2)}, u32[]{:S(2)}) collective-permute-start(bf16[32,1024]{1,0:T(8,128)(2,1)S(1)} %copy-done.31), channel_id=1, source_target_pairs={{0,0},{8,1},{16,2},{24,3},{1,4},{9,5},{17,6},{25,7},{2,8},{10,9},{... | collective-permute-start | bytes 196616 | tf_op jit(solution)/shard_map/ppermute | solution.py:41
  52.2 6.1 %collective-permute-done.4 = bf16[32,1024]{1,0:T(8,128)(2,1)S(1)} collective-permute-done((bf16[32,1024]{1,0:T(8,128)(2,1)S(1)}, bf16[32,1024]{1,0:T(8,128)(2,1)S(1)}, u32[]{:S(2)}, u32[]{:S(2)}) %collective-permute-start.4) | collective-permute-done | bytes 65568 | tf_op jit(solution)/shard_map/ppermute | solution.py:41
  63.2 22.1 %all-gather.2 = bf16[512,768]{1,0:T(8,128)(2,1)S(1)} all-gather(bf16[128,768]{1,0:T(8,128)(2,1)S(1)} %slice.177), channel_id=4, replica_groups={{0,8,16,24},{4,12,20,28},{1,9,17,25},{5,13,21,29},{2,10,18,26},{6,14,22..., dimensions={0}, use_global_device_ids=true | all-gather | bytes 983040 | tf_op jit(solution)/shard_map/all_gather | solution.py:49
  90.0 15.9 %collective-permute-done.6 = bf16[4,128,768]{2,1,0:T(8,128)(2,1)} collective-permute-done((bf16[4,128,768]{2,1,0:T(8,128)(2,1)S(1)}, bf16[4,128,768]{2,1,0:T(8,128)(2,1)}, u32[]{:S(2)}, u32[]{:S(2)}) %collective-permute-start.6) | collective-permute-done | bytes 786464 | tf_op jit(solution)/shard_map/ppermute | solution.py:34
  109.9 21.2 %collective-permute-done.3 = bf16[4,128,1152]{2,1,0:T(8,128)(2,1)} collective-permute-done((bf16[4,128,1152]{2,1,0:T(8,128)(2,1)}, bf16[4,128,1152]{2,1,0:T(8,128)(2,1)}, u32[]{:S(2)}, u32[]{:S(2)}) %collective-permute-start.3) | collective-permute-done | bytes 1179680 | tf_op jit(solution)/shard_map/ppermute | solution.py:34
  136.9 16.1 %multiply_convert_fusion = (bf16[1024,1024]{1,0:T(8,128)(2,1)}, f32[1024,1024]{1,0:T(8,128)}, f32[1024,1024]{1,0:T(8,128)}) fusion(f32[1024]{0:T(1024)S(1)} %bitcast.188, bf16[1024,1152]{1,0:T(8,128)(2,1)S(1)} %bitcast.147, f32[1024]{0:T(1024)S(1)} %get-tuple-element.27, f32[1024]{0:T(1024)S(1)} %get-tuple-element.28, f32[1024]{0:T(1024)S(1)} %add_rsqrt_fusion, ...), kind=kOutput, calls=%fused_computation.20 | convolution fusion | flops 2230321152 | bytes 14700544 | tf_op jit(solution)/shard_map/dot_general | solution.py:30
  153.7 4.7 %convolution_convert_fusion = bf16[1024,1024]{1,0:T(8,128)(2,1)S(1)} fusion(bf16[1024,1024]{1,0:T(8,128)(2,1)} %get-tuple-element.37, bf16[256,1024]{1,0:T(8,128)(2,1)} %collective-permute-done.12, bf16[256,1024]{1,0:T(8,128)(2,1)} %collective-permute-done.11, bf16[256,1024]{1,0:T(8,128)(2,1)} %collective-permute-done.10, bf16[256,1024]{1,0:T(8,128)(2,1)} %bitcast.43), kind=kOutput, calls=%fused_computation.50 | convolution fusion | flops 2156920832 | bytes 6291456 | tf_op jit(solution)/shard_map/dot_general | solution.py:22
  161.0 5.6 %convolution_add_fusion.linear_ref = f32[1024,768]{1,0:T(8,128)} fusion(bf16[1024,768]{1,0:T(8,128)(2,1)S(1)} %bitcast.168, f32[768]{0:T(1024)S(1)} %reshape.247, f32[1024]{0:T(1024)S(1)} %get-tuple-element.25, f32[1024]{0:T(1024)S(1)} %get-tuple-element.26, f32[1024]{0:T(1024)S(1)} %add_rsqrt_fusion, f32[1024]{0:T(1024)S(1)} %broadcast_multiply_fusion, ...), kind=kOutput, calls=%fused_computation.56 | convolution fusion | flops 1625030656 | bytes 6835200 | tf_op jit(solution)/shard_map/dot_general | solution.py:30
  168.8 2.5 copy-done.33
  172.6 4.7 %fusion.34 = (bf16[1024]{0:T(1024)(128)(2,1)S(1)}, bf16[1024,1024]{1,0:T(8,128)(2,1)S(1)}) fusion(f32[1024,1024]{1,0:T(8,128)S(1)} %copy-done.33, f32[1024,1024]{1,0:T(8,128)S(1)} %copy-done.34, f32[1024]{0:T(1024)S(1)} %bitcast.189, bf16[1024,1024]{1,0:T(8,128)(2,1)S(1)} %bitcast.162, bf16[256,1024]{1,0:T(8,128)(2,1)} %collective-permute-done.12, ...), kind=kOutput, calls=%fused_computation.134 | convolution fusion | flops 2165308416 | bytes 14686208 | tf_op jit(solution)/shard_map/dot_general | solution.py:26
  177.2 2.8 convolution_convert_fusion.1
  181.8 3.1 convolution_convert_fusion.4.grad_ref
  184.9 25.7 %attend.1 = (bf16[1024,256]{1,0:T(8,128)(2,1)}, bf16[1024,768]{1,0:T(8,128)(2,1)}) custom-call(s32[1]{0:T(128)} %bitcast.23.spot_ref, f32[1024,768]{1,0:T(8,128)} %convolution_add_fusion.linear_ref, f32[1024,256]{1,0:T(8,128)} %copy.119.cos_ref, f32[1024,256]{1,0:T(8,128)} %copy.120.sin_ref, s32[1024,1]{1,0:T(8,128)} %copy.121.seg_col_ref, ...), custom_call_target="tpu_custom_call" | custom-call | flops 3221225472 | bytes 4194304 | tf_op jit(solution)/shard_map/attend/pallas_call | solution.py:212
  210.6 5.9 %fusion.36 = f32[1024,1024]{1,0:T(8,128)} fusion(bf16[1024,768]{1,0:T(8,128)(2,1)} %get-tuple-element.17, bf16[1024,768]{1,0:T(8,128)(2,1)} %bitcast.167), kind=kOutput, calls=%fused_computation.136 | convolution fusion | flops 1610612736 | bytes 7340032 | tf_op jit(solution)/shard_map/dot_general | solution.py:26
  216.5 2.6 fusion.19
  219.3 8.7 %fusion.31 = (bf16[1024]{0:T(1024)(128)(2,1)S(1)}, bf16[1024]{0:T(1024)(128)(2,1)S(1)}, bf16[1024,1024]{1,0:T(8,128)(2,1)}, bf16[1024]{0:T(1024)(128)(2,1)S(1)},...) fusion(f32[1024]{0:T(1024)S(1)} %add_rsqrt_fusion, f32[1024]{0:T(1024)S(1)} %broadcast_multiply_fusion, ...), kind=kOutput, calls=%fused_computation.132 | convolution fusion | flops 2168451072 | bytes 16801792 | tf_op jit(solution)/shard_map/dot_general | solution.py:26
  229.7 2.5 convolution_convert_fusion.3
  232.7 4.9 %convolution_convert_fusion.2 = bf16[1024,768]{1,0:T(8,128)(2,1)} fusion(bf16[1024,768]{1,0:T(8,128)(2,1)} %get-tuple-element.17, f32[1024]{0:T(1024)S(1)} %get-tuple-element.25, f32[1024]{0:T(1024)S(1)} %get-tuple-element.26, f32[1024]{0:T(1024)S(1)} %add_rsqrt_fusion, f32[1024]{0:T(1024)S(1)} %broadcast_multiply_fusion, ...), kind=kOutput, calls=%fused_computation.57 | convolution fusion | flops 1625030656 | bytes 5259264 | tf_op jit(solution)/shard_map/dot_general | solution.py:22
  237.6 2.6 fusion.18
  250.0 15.0 %collective-permute-done.17 = bf16[4,128,1152]{2,1,0:T(8,128)(2,1)S(1)} collective-permute-done((bf16[4,128,1152]{2,1,0:T(8,128)(2,1)S(1)}, bf16[4,128,1152]{2,1,0:T(8,128)(2,1)S(1)}, u32[]{:S(2)}, u32[]{:S(2)}) %collective-permute-start.17) | collective-permute-done | bytes 1179680 | tf_op jit(solution)/shard_map/ppermute | solution.py:34
  268.4 3.4 %collective-permute-start.16 = (bf16[256,1024]{1,0:T(8,128)(2,1)S(1)}, bf16[256,1024]{1,0:T(8,128)(2,1)S(1)}, u32[]{:S(2)}, u32[]{:S(2)}) collective-permute-start(bf16[256,1024]{1,0:T(8,128)(2,1)S(1)} %slice.261), channel_id=1, source_target_pairs={{0,2},{1,3},{2,0},{3,1},{4,6},{5,7},{6,4},{7,5},{8,10},{9,11},{10,... | collective-permute-start | bytes 1572872 | tf_op jit(solution)/shard_map/ppermute | solution.py:34
  273.8 7.8 %collective-permute-done.16 = bf16[256,1024]{1,0:T(8,128)(2,1)S(1)} collective-permute-done((bf16[256,1024]{1,0:T(8,128)(2,1)S(1)}, bf16[256,1024]{1,0:T(8,128)(2,1)S(1)}, u32[]{:S(2)}, u32[]{:S(2)}) %collective-permute-start.16) | collective-permute-done | bytes 524320 | tf_op jit(solution)/shard_map/ppermute | solution.py:34
  281.9 5.3 %collective-permute-done.14 = bf16[256,1024]{1,0:T(8,128)(2,1)S(1)} collective-permute-done((bf16[256,1024]{1,0:T(8,128)(2,1)S(1)}, bf16[256,1024]{1,0:T(8,128)(2,1)S(1)}, u32[]{:S(2)}, u32[]{:S(2)}) %collective-permute-start.14) | collective-permute-done | bytes 524320 | tf_op jit(solution)/shard_map/ppermute | solution.py:34
  288.3 2.4 add_bitcast_fusion
  290.6 4.7 %all-to-all-start.2 = ((bf16[4,32,1024]{2,1,0:T(8,128)(2,1)}), bf16[4,32,1024]{2,1,0:T(8,128)(2,1)S(1)}, u32[]{:S(2)}, u32[]{:S(2)}) async-start(bf16[4,32,1024]{2,1,0:T(8,128)(2,1)} %bitcast.182), calls=%async_computation.4 | async-start | bytes 524288 | tf_op jit(solution)/shard_map/all_to_all | solution.py:335
  297.1 2.6 all-to-all-done.2
  299.7 11.1 %reduce-scatter.4.cloned.1.call-done = bf16[1,128,1152]{2,1,0:T(8,128)(2,1)} async-done(((bf16[4,128,1152]{2,1,0:T(8,128)(2,1)}), bf16[1,128,1152]{2,1,0:T(8,128)(2,1)}) %reduce-scatter.4.cloned.1.call-update) | async-done | bytes 294928 | tf_op jit(solution)/shard_map/reduce_scatter | solution.py:62
  313.3 3.9 %all-to-all-start.1 = ((bf16[4,32,896]{2,1,0:T(8,128)(2,1)}), bf16[4,32,896]{2,1,0:T(8,128)(2,1)S(1)}, u32[]{:S(2)}, u32[]{:S(2)}) async-start(bf16[4,32,896]{2,1,0:T(8,128)(2,1)} %bitcast.56), calls=%async_computation.2 | async-start | bytes 458752 | tf_op jit(solution)/shard_map/all_to_all | solution.py:400
  319.5 2.6 collective-permute-start.18
  323.5 5.7 %collective-permute-done.18 = bf16[32,1024]{1,0:T(8,128)(2,1)S(1)} collective-permute-done((bf16[32,1024]{1,0:T(8,128)(2,1)S(1)}, bf16[32,1024]{1,0:T(8,128)(2,1)S(1)}, u32[]{:S(2)}, u32[]{:S(2)}) %collective-permute-start.18) | collective-permute-done | bytes 65568 | tf_op jit(solution)/shard_map/ppermute | solution.py:41
  (241 shorter events, 76.8 us)
Async XLA Ops:
  7.2 37.0 %copy-start.31 = (bf16[32,1024]{1,0:T(8,128)(2,1)S(1)}, bf16[32,1024]{1,0:T(8,128)(2,1)}, u32[]{:S(2)}) copy-start(bf16[32,1024]{1,0:T(8,128)(2,1)} %param.25) | copy-start | bytes 196612
  7.2 51.1 %copy-start.25 = (bf16[128,1024]{1,0:T(8,128)(2,1)S(1)}, bf16[128,1024]{1,0:T(8,128)(2,1)}, u32[]{:S(2)}) copy-start(bf16[128,1024]{1,0:T(8,128)(2,1)} %param.29) | copy-start | bytes 786436
  7.2 80.0 %all-gather.6.cloned.1.call-start = ((), (), s32[]{:S(2)}) async-start(), calls=%async_computation.9 | async-start | bytes 1474560 | tf_op jit(solution)/shard_map/all_gather | solution.py:49
  27.7 80.7 %all-gather.8.cloned.1.call-start = ((), (), s32[]{:S(2)}) async-start(), calls=%async_computation.10 | async-start | bytes 1638400 | tf_op jit(solution)/shard_map/all_gather | solution.py:49
  27.8 31.4 %collective-permute-start = (bf16[256,1024]{1,0:T(8,128)(2,1)S(1)}, bf16[256,1024]{1,0:T(8,128)(2,1)S(1)}, u32[]{:S(2)}, u32[]{:S(2)}) collective-permute-start(bf16[256,1024]{1,0:T(8,128)(2,1)S(1)} %bitcast.136), channel_id=1, source_target_pairs={{0,2},{1,3},{2,0},{3,1},{4,6},{5,7},{6,4},{7,5},{8,10},{9,11},{10,... | collective-permute-start | bytes 1572872 | tf_op jit(solution)/shard_map/ppermute | solution.py:34
  29.5 57.3 %collective-permute-start.1 = (bf16[256,1024]{1,0:T(8,128)(2,1)S(1)}, bf16[256,1024]{1,0:T(8,128)(2,1)S(1)}, u32[]{:S(2)}, u32[]{:S(2)}) collective-permute-start(bf16[256,1024]{1,0:T(8,128)(2,1)S(1)} %bitcast.137), channel_id=1, source_target_pairs={{0,1},{1,0},{2,3},{3,2},{4,5},{5,4},{6,7},{7,6},{8,9},{9,8},{10,11... | collective-permute-start | bytes 1572872 | tf_op jit(solution)/shard_map/ppermute | solution.py:34
  29.5 13.2 %collective-permute-start.7 = (s32[2,256]{1,0:T(2,128)S(1)}, s32[2,256]{1,0:T(2,128)S(1)}, u32[]{:S(2)}, u32[]{:S(2)}) collective-permute-start(s32[2,256]{1,0:T(2,128)S(1)} %pad_add_fusion.1), channel_id=1, source_target_pairs={{0,2},{1,3},{2,0},{3,1},{4,6},{5,7},{6,4},{7,5},{8,10},{9,11},{10,... | collective-permute-start | bytes 6152 | tf_op jit(solution)/shard_map/ppermute | solution.py:34
  30.0 12.7 %collective-permute-start.8 = (s32[2,256]{1,0:T(2,128)S(1)}, s32[2,256]{1,0:T(2,128)S(1)}, u32[]{:S(2)}, u32[]{:S(2)}) collective-permute-start(s32[2,256]{1,0:T(2,128)S(1)} %pad_add_fusion.1), channel_id=1, source_target_pairs={{0,1},{1,0},{2,3},{3,2},{4,5},{5,4},{6,7},{7,6},{8,9},{9,8},{10,11... | collective-permute-start | bytes 6152 | tf_op jit(solution)/shard_map/ppermute | solution.py:34
  30.2 56.6 %collective-permute-start.10 = (bf16[256,1024]{1,0:T(8,128)(2,1)}, bf16[256,1024]{1,0:T(8,128)(2,1)}, u32[]{:S(2)}, u32[]{:S(2)}) collective-permute-start(bf16[256,1024]{1,0:T(8,128)(2,1)} %bitcast.43), channel_id=1, source_target_pairs={{0,2},{1,3},{2,0},{3,1},{4,6},{5,7},{6,4},{7,5},{8,10},{9,11},{10,... | collective-permute-start | bytes 1572872 | tf_op jit(solution)/shard_map/ppermute | solution.py:34
  42.7 110.9 %collective-permute-start.11 = (bf16[256,1024]{1,0:T(8,128)(2,1)}, bf16[256,1024]{1,0:T(8,128)(2,1)}, u32[]{:S(2)}, u32[]{:S(2)}) collective-permute-start(bf16[256,1024]{1,0:T(8,128)(2,1)} %bitcast.43), channel_id=1, source_target_pairs={{0,1},{1,0},{2,3},{3,2},{4,5},{5,4},{6,7},{7,6},{8,9},{9,8},{10,11... | collective-permute-start | bytes 1572872 | tf_op jit(solution)/shard_map/ppermute | solution.py:34
  42.7 1.5 collective-permute-start.9
  44.2 14.1 %collective-permute-start.4 = (bf16[32,1024]{1,0:T(8,128)(2,1)S(1)}, bf16[32,1024]{1,0:T(8,128)(2,1)S(1)}, u32[]{:S(2)}, u32[]{:S(2)}) collective-permute-start(bf16[32,1024]{1,0:T(8,128)(2,1)S(1)} %copy-done.31), channel_id=1, source_target_pairs={{0,0},{8,1},{16,2},{24,3},{1,4},{9,5},{17,6},{25,7},{2,8},{10,9},{... | collective-permute-start | bytes 196616 | tf_op jit(solution)/shard_map/ppermute | solution.py:41
  59.1 231.5 %reduce-scatter.6.cloned.1.call-start = ((), (), s32[]{:S(2)}) async-start(), calls=%async_computation.7 | async-start | bytes 1310720 | tf_op jit(solution)/shard_map/reduce_scatter | solution.py:62
  59.2 28.6 %copy-start.10 = (bf16[256,1024]{1,0:T(8,128)(2,1)}, bf16[256,1024]{1,0:T(8,128)(2,1)S(1)}, u32[]{:S(2)}) copy-start(bf16[256,1024]{1,0:T(8,128)(2,1)S(1)} %collective-permute-done) | copy-start | bytes 1572868
  59.2 27.7 %collective-permute-start.2 = (bf16[256,1024]{1,0:T(8,128)(2,1)S(1)}, bf16[256,1024]{1,0:T(8,128)(2,1)S(1)}, u32[]{:S(2)}, u32[]{:S(2)}) collective-permute-start(bf16[256,1024]{1,0:T(8,128)(2,1)S(1)} %collective-permute-done), channel_id=1, source_target_pairs={{0,1},{1,0},{2,3},{3,2},{4,5},{5,4},{6,7},{7,6},{8,9},{9,8},{10,11... | collective-permute-start | bytes 1572872 | tf_op jit(solution)/shard_map/ppermute | solution.py:34
  85.3 20.6 %collective-permute-start.6 = (bf16[4,128,768]{2,1,0:T(8,128)(2,1)S(1)}, bf16[4,128,768]{2,1,0:T(8,128)(2,1)}, u32[]{:S(2)}, u32[]{:S(2)}) collective-permute-start(bf16[4,128,768]{2,1,0:T(8,128)(2,1)S(1)} %bitcast.152), channel_id=1, source_target_pairs={{0,4},{4,0},{8,12},{12,8},{16,20},{20,16},{24,28},{28,24},{1,5},{5... | collective-permute-start | bytes 2359304 | tf_op jit(solution)/shard_map/ppermute | solution.py:34
  86.8 66.8 %collective-permute-start.12 = (bf16[256,1024]{1,0:T(8,128)(2,1)}, bf16[256,1024]{1,0:T(8,128)(2,1)}, u32[]{:S(2)}, u32[]{:S(2)}) collective-permute-start(bf16[256,1024]{1,0:T(8,128)(2,1)} %collective-permute-done.10), channel_id=1, source_target_pairs={{0,1},{1,0},{2,3},{3,2},{4,5},{5,4},{6,7},{7,6},{8,9},{9,8},{10,11... | collective-permute-start | bytes 1572872 | tf_op jit(solution)/shard_map/ppermute | solution.py:34
  87.2 43.9 %collective-permute-start.3 = (bf16[4,128,1152]{2,1,0:T(8,128)(2,1)}, bf16[4,128,1152]{2,1,0:T(8,128)(2,1)}, u32[]{:S(2)}, u32[]{:S(2)}) collective-permute-start(bf16[4,128,1152]{2,1,0:T(8,128)(2,1)} %bitcast.172), channel_id=1, source_target_pairs={{0,4},{4,0},{8,12},{12,8},{16,20},{20,16},{24,28},{28,24},{1,5},{5... | collective-permute-start | bytes 3538952 | tf_op jit(solution)/shard_map/ppermute | solution.py:34
  90.0 181.8 %copy-start.28 = (f32[1024]{0:T(1024)}, f32[1024]{0:T(1024)S(1)}, u32[]{:S(2)}) copy-start(f32[1024]{0:T(1024)S(1)} %add_rsqrt_fusion) | copy-start | bytes 12292
  108.4 58.2 %collective-permute-start.5 = (bf16[4,160,1024]{2,1,0:T(8,128)(2,1)}, bf16[4,160,1024]{2,1,0:T(8,128)(2,1)}, u32[]{:S(2)}, u32[]{:S(2)}) collective-permute-start(bf16[4,160,1024]{2,1,0:T(8,128)(2,1)} %bitcast.170), channel_id=1, source_target_pairs={{0,4},{4,0},{8,12},{12,8},{16,20},{20,16},{24,28},{28,24},{1,5},{5... | collective-permute-start | bytes 3932168 | tf_op jit(solution)/shard_map/ppermute | solution.py:34
  159.5 78.1 %collective-permute-start.20 = (bf16[4,128,1024]{2,1,0:T(8,128)(2,1)}, bf16[4,128,1024]{2,1,0:T(8,128)(2,1)}, u32[]{:S(2)}, u32[]{:S(2)}) collective-permute-start(bf16[4,128,1024]{2,1,0:T(8,128)(2,1)} %dynamic-slice_bitcast_fusion.1), channel_id=1, source_target_pairs={{0,4},{4,0},{8,12},{12,8},{16,20},{20,16},{24,28},{28,24},{1,5},{5... | collective-permute-start | bytes 3145736 | tf_op jit(solution)/shard_map/ppermute | solution.py:34
  181.3 35.2 %collective-permute-start.19 = (bf16[4,128,1024]{2,1,0:T(8,128)(2,1)}, bf16[4,128,1024]{2,1,0:T(8,128)(2,1)}, u32[]{:S(2)}, u32[]{:S(2)}) collective-permute-start(bf16[4,128,1024]{2,1,0:T(8,128)(2,1)} %dynamic-slice_bitcast_fusion.2), channel_id=1, source_target_pairs={{0,4},{4,0},{8,12},{12,8},{16,20},{20,16},{24,28},{28,24},{1,5},{5... | collective-permute-start | bytes 3145736 | tf_op jit(solution)/shard_map/ppermute | solution.py:34
  219.2 76.1 %reduce-scatter.8.cloned.1.call-start = ((), (), s32[]{:S(2)}) async-start(), calls=%async_computation.8 | async-start | bytes 1310720 | tf_op jit(solution)/shard_map/reduce_scatter | solution.py:62
  240.2 70.6 %reduce-scatter.4.cloned.1.call-start = ((), (), s32[]{:S(2)}) async-start(), calls=%async_computation.6 | async-start | bytes 1474560 | tf_op jit(solution)/shard_map/reduce_scatter | solution.py:62
  242.5 22.5 %collective-permute-start.17 = (bf16[4,128,1152]{2,1,0:T(8,128)(2,1)S(1)}, bf16[4,128,1152]{2,1,0:T(8,128)(2,1)S(1)}, u32[]{:S(2)}, u32[]{:S(2)}) collective-permute-start(bf16[4,128,1152]{2,1,0:T(8,128)(2,1)S(1)} %dynamic-slice_bitcast_fusion), channel_id=1, source_target_pairs={{0,4},{4,0},{8,12},{12,8},{16,20},{20,16},{24,28},{28,24},{1,5},{5... | collective-permute-start | bytes 3538952 | tf_op jit(solution)/shard_map/ppermute | solution.py:34
  245.3 21.0 %collective-permute-start.15 = (bf16[512,1024]{1,0:T(8,128)(2,1)}, bf16[512,1024]{1,0:T(8,128)(2,1)}, u32[]{:S(2)}, u32[]{:S(2)}) collective-permute-start(bf16[512,1024]{1,0:T(8,128)(2,1)} %slice.196), channel_id=1, source_target_pairs={{0,1},{1,0},{2,3},{3,2},{4,5},{5,4},{6,7},{7,6},{8,9},{9,8},{10,11... | collective-permute-start | bytes 3145736 | tf_op jit(solution)/shard_map/ppermute | solution.py:34
  249.5 22.3 %collective-permute-start.13 = (bf16[512,1024]{1,0:T(8,128)(2,1)}, bf16[512,1024]{1,0:T(8,128)(2,1)}, u32[]{:S(2)}, u32[]{:S(2)}) collective-permute-start(bf16[512,1024]{1,0:T(8,128)(2,1)} %slice.192), channel_id=1, source_target_pairs={{0,1},{1,0},{2,3},{3,2},{4,5},{5,4},{6,7},{7,6},{8,9},{9,8},{10,11... | collective-permute-start | bytes 3145736 | tf_op jit(solution)/shard_map/ppermute | solution.py:34
  268.4 13.2 %collective-permute-start.16 = (bf16[256,1024]{1,0:T(8,128)(2,1)S(1)}, bf16[256,1024]{1,0:T(8,128)(2,1)S(1)}, u32[]{:S(2)}, u32[]{:S(2)}) collective-permute-start(bf16[256,1024]{1,0:T(8,128)(2,1)S(1)} %slice.261), channel_id=1, source_target_pairs={{0,2},{1,3},{2,0},{3,1},{4,6},{5,7},{6,4},{7,5},{8,10},{9,11},{10,... | collective-permute-start | bytes 1572872 | tf_op jit(solution)/shard_map/ppermute | solution.py:34
  273.5 13.7 %collective-permute-start.14 = (bf16[256,1024]{1,0:T(8,128)(2,1)S(1)}, bf16[256,1024]{1,0:T(8,128)(2,1)S(1)}, u32[]{:S(2)}, u32[]{:S(2)}) collective-permute-start(bf16[256,1024]{1,0:T(8,128)(2,1)S(1)} %slice.262), channel_id=1, source_target_pairs={{0,2},{1,3},{2,0},{3,1},{4,6},{5,7},{6,4},{7,5},{8,10},{9,11},{10,... | collective-permute-start | bytes 1572872 | tf_op jit(solution)/shard_map/ppermute | solution.py:34
  290.6 9.1 %all-to-all-start.2 = ((bf16[4,32,1024]{2,1,0:T(8,128)(2,1)}), bf16[4,32,1024]{2,1,0:T(8,128)(2,1)S(1)}, u32[]{:S(2)}, u32[]{:S(2)}) async-start(bf16[4,32,1024]{2,1,0:T(8,128)(2,1)} %bitcast.182), calls=%async_computation.4 | async-start | bytes 524288 | tf_op jit(solution)/shard_map/all_to_all | solution.py:335
  313.3 16.6 %all-to-all-start.1 = ((bf16[4,32,896]{2,1,0:T(8,128)(2,1)}), bf16[4,32,896]{2,1,0:T(8,128)(2,1)S(1)}, u32[]{:S(2)}, u32[]{:S(2)}) async-start(bf16[4,32,896]{2,1,0:T(8,128)(2,1)} %bitcast.56), calls=%async_computation.2 | async-start | bytes 458752 | tf_op jit(solution)/shard_map/all_to_all | solution.py:400
  319.5 9.8 %collective-permute-start.18 = (bf16[32,1024]{1,0:T(8,128)(2,1)S(1)}, bf16[32,1024]{1,0:T(8,128)(2,1)S(1)}, u32[]{:S(2)}, u32[]{:S(2)}) collective-permute-start(bf16[32,1024]{1,0:T(8,128)(2,1)S(1)} %bitcast.184), channel_id=1, source_target_pairs={{0,0},{1,8},{2,16},{3,24},{4,1},{5,9},{6,17},{7,25},{8,2},{9,10},{... | collective-permute-start | bytes 196616 | tf_op jit(solution)/shard_map/ppermute | solution.py:41
  (33 other events, 278.4 us)
Sparse Core Ops, SparseCore 0:
  27.8 31.8 all-gather.5
  61.8 39.3 all-gather.7
  219.3 33.4 reduce-scatter.5
  255.0 25.8 reduce-scatter.7
  283.0 27.7 reduce-scatter.3

commit v2 on v1

v2 whole, which is shorter than its diff:
```python
from functools import partial
import math

import jax
import jax.numpy as jnp
from jax import lax
from jax.experimental import pallas as pl
from jax.experimental.pallas import tpu as pltpu
from jax.sharding import PartitionSpec as P

H = 16
HD = 64
ROT = 16

EPS = 1e-05
NEG = -1000000000.0
BF = jnp.bfloat16
F32 = jnp.float32


def contract_rows(left, right):
    return lax.dot_general(left, right, (((0,), (0,)), ((), ())), preferred_element_type=F32)


def contract_cols(left, right):
    return lax.dot_general(left, right, (((1,), (1,)), ((), ())), preferred_element_type=F32)


def dot(left, right):
    return jnp.dot(left, right, preferred_element_type=F32)


def swap(value, axis, size, bits):
    return lax.ppermute(value, axis, [(i, i ^ bits) for i in range(size)])


class Layout:
    def __init__(self, seq, ctx):
        self.seq, self.ctx = seq, ctx
        self.near = 2 if seq % 2 == 0 and H % (2 * ctx) == 0 else 1
        self.far = seq // self.near
        self.team = self.near * ctx
        self.inner = lax.axis_index("seq") % self.near
        self.spot = lax.axis_index("ctx")
        self.index = self.inner * ctx + self.spot
        self.far_index = lax.axis_index("seq") // self.near
        self.groups = [[self.near * z + x for z in range(self.far)] for x in range(self.near)]

    def gather_far(self, shard):
        return lax.all_gather(shard, "seq", axis=0, axis_index_groups=self.groups)

    def scatter_far(self, terms):
        return lax.psum_scatter(
            terms, "seq", scatter_dimension=0, tiled=True, axis_index_groups=self.groups
        )[0]

    def exchange_near(self, pieces):
        if self.near == 1:
            return pieces[0][:, None]
        mine = lax.dynamic_index_in_dim(pieces, self.inner, 0, keepdims=False)
        sent = lax.dynamic_index_in_dim(pieces, 1 - self.inner, 0, keepdims=False)
        got = swap(sent, "seq", self.seq, 1)
        low = self.inner == 0
        return jnp.stack([jnp.where(low, mine, got), jnp.where(low, got, mine)], 1)

    def exchange(self, pieces):
        return lax.all_to_all(self.exchange_near(pieces), "ctx", 0, 0, tiled=True)

    def own_heads(self, value, back=False):
        pairs = []
        for z in range(self.far):
            for x in range(self.near):
                for c in range(self.ctx):
                    block = (x * self.ctx + c) * self.far + z
                    pairs.append((block, (z * self.near + x) * self.ctx + c))
        if back:
            pairs = [(b, a) for a, b in pairs]
        return lax.ppermute(value, ("seq", "ctx"), pairs)

    def gather_team(self, own, beside, across, route, first=()):
        swap_ctx = lambda v, k: swap(v, "ctx", self.ctx, k)
        if self.near == 1:
            blocks = [own] + across
        elif route == 0:
            blocks = [own, beside]
            for k, block in zip(range(2, self.ctx, 2), across):
                blocks += [block, swap_ctx(beside, k)]
        else:
            blocks = [own, beside]
            for block in across:
                blocks += [block, swap(block, "seq", self.seq, 1)]
        even = after(jnp.concatenate(blocks, 0), *first)
        return even, swap_ctx(even, 1)

    def beside(self, own):
        return swap(own, "seq", self.seq, 1) if self.near == 2 else own

    def across(self, own):
        return [swap(own, "ctx", self.ctx, k) for k in range(2, self.ctx, 2)]

    def spread(self):
        seq_bits = jnp.arange(self.seq) ^ lax.axis_index("seq")
        ctx_bits = jnp.arange(self.ctx) ^ self.spot
        return (ctx_bits[None, :] * self.seq + seq_bits[:, None]).reshape(-1)

    def gather_all(self, vector):
        table = vector[None]
        for axis, size in (("seq", self.seq), ("ctx", self.ctx)):
            bit = 1
            while bit < size:
                table = jnp.concatenate([table, swap(table, axis, size, bit)], 0)
                bit *= 2
        return table[self.spread()]

    def scatter_all(self, table):
        seq_bits = jnp.arange(self.seq) ^ lax.axis_index("seq")
        ctx_bits = jnp.arange(self.ctx) ^ self.spot
        place = (seq_bits[None, :] * self.ctx + ctx_bits[:, None]).reshape(-1)
        table = table[place].reshape(self.ctx, self.seq // 2, 2, -1)
        table = table[:, :, 0] + swap(table[:, :, 1], "seq", self.seq, 1)
        bit = self.ctx // 2
        while bit:
            table = table[:bit] + swap(table[bit:], "ctx", self.ctx, bit)
            bit //= 2
        table = table[0]
        bit = self.seq // 4
        while bit:
            table = table[:bit] + swap(table[bit:], "seq", self.seq, 2 * bit)
            bit //= 2
        return table[0]

    def order(self):
        ks = list(range(0, self.ctx, 2)) + list(range(1, self.ctx, 2))
        return [(x, k) for k in ks for x in range(self.near)]

    def pair_blocks(self, even, got):
        rows = even.shape[0] * 2 // self.team
        width = even.shape[1]
        if self.near == 2 and self.ctx == 4 and width % 256 == 0:
            return list(pair_sums(even, got, rows))
        table = even.astype(F32) + got.astype(F32)
        table = table.reshape(self.ctx // 2, self.near, rows, width)
        return [table[0], table[1:].astype(BF)]

    def scatter_team(self, blocks):
        def over_ctx(kept, sent):
            came = [swap(sent[k - 1], "ctx", self.ctx, 2 * k) for k in range(1, self.ctx // 2)]
            for v in came:
                kept = kept + v.astype(F32)
            return kept, came

        def over_seq(kept, sent):
            came = swap(sent, "seq", self.seq, 1)
            return kept + came.astype(F32), [came]

        kept, first = over_ctx(*blocks[:2])
        if self.near == 2:
            kept, done = over_seq(kept[0], kept[1].astype(BF))
        else:
            kept = kept[0]
        if len(blocks) == 2:
            return kept, first, first
        other, second = over_seq(*blocks[2:])
        other, last = over_ctx(other[0], other[1:].astype(BF))
        done = done + last
        return jnp.concatenate([kept, other], 1), first + second, done


def after(value, *first):
    return lax.optimization_barrier((value,) + first)[0]


def normed(value, gain, shift):
    wide = value.astype(F32)
    centred = wide - jnp.mean(wide, -1, keepdims=True)
    unit = centred * lax.rsqrt(jnp.mean(centred * centred, -1, keepdims=True) + EPS)
    return unit, (unit * gain + shift).astype(BF)


def turn(u, cosine, sine):
    width = u.shape[-1]
    lane = lax.broadcasted_iota(jnp.int32, u.shape, 1) % HD
    moved = jnp.where(
        lane < ROT // 2, pltpu.roll(u, width - ROT // 2, 1), pltpu.roll(u, ROT // 2, 1)
    )
    return u * cosine + moved * sine


def row_sum(value):
    return jnp.sum(value, 0, keepdims=True)


def pack_rows(target, start, size, source, peers):
    rows = source.shape[0] // peers
    depth = target.shape[0] // peers
    for z in range(peers):
        for n in range(source.shape[1] // size):
            at = pl.ds(z * depth + n * rows, rows)
            piece = source[pl.ds(z * rows, rows), pl.ds(n * size, size)]
            target[at, pl.ds(start, size)] = piece.astype(BF)


def mlp_kernel(
    peers, x_ref, g_ref, up_ref, down_ref, gain_ref, shift_ref, bias_ref, gain_one_ref, shift_one_ref,
    hid_ref, flow_ref, one_ref, terms_out, gain_out, shift_out, bias_out,
    down_s, up_s,
):
    step = pl.program_id(0)

    @pl.when(step == 0)
    def _():
        for ref in (down_s, up_s, gain_out, shift_out, bias_out):
            ref[...] = jnp.zeros_like(ref)

    gain = gain_ref[...]
    unit, value = normed(load(x_ref), gain, shift_ref[...])
    one_ref[...] = (unit * gain_one_ref[...] + shift_one_ref[...]).astype(BF)
    grad = load(g_ref)
    upper = dot(value, up_ref[...]) + bias_ref[...]
    grad_active = contract_cols(grad, down_ref[...])
    cdf = 0.5 * (1.0 + lax.erf(upper * math.sqrt(0.5)))
    density = jnp.exp(-0.5 * upper * upper) * (1.0 / math.sqrt(2.0 * math.pi))
    active = (upper * cdf).astype(BF)
    grad_upper = (grad_active * (cdf + upper * density)).astype(BF)
    store(hid_ref, dot(active, down_ref[...]).astype(BF))
    down_s[...] += contract_rows(active, grad)
    up_s[...] += contract_rows(value, grad_upper)
    back = contract_cols(grad_upper, up_ref[...])
    store(flow_ref, (back * gain).astype(BF))
    gain_out[...] += row_sum(back * unit)
    shift_out[...] += row_sum(back)
    bias_out[...] += row_sum(grad_upper.astype(F32))

    @pl.when(step == pl.num_programs(0) - 1)
    def _():
        share = up_s.shape[1]
        terms_out[:, 0:share] = up_s[...].astype(BF)
        pack_rows(terms_out, share, share, down_s, peers)


def head_kernel(
    peers, g_ref, value_ref, cos_ref, sin_ref, third_ref, bias_ref, pack_ref, qkv_ref, out_ref
):
    @pl.when(pl.program_id(0) == 0)
    def _():
        size = third_ref.shape[1] - qkv_ref.shape[1]
        depth, rows = [v.shape[0] // max(peers, 1) for v in (third_ref, out_ref)]
        qkv_ref[...] = third_ref[:, 0 : qkv_ref.shape[1]]
        if not peers:
            out_ref[...] = third_ref[:, qkv_ref.shape[1] :].T
        for z in range(peers):
            for n in range(out_ref.shape[1] // size):
                at = pl.ds(z * depth + n * rows, rows)
                piece = third_ref[at, pl.ds(qkv_ref.shape[1], size)]
                out_ref[pl.ds(z * rows, rows), pl.ds(n * size, size)] = piece

    width = cos_ref.shape[1]
    linear = dot(value_ref[...], qkv_ref[...]) + bias_ref[...]
    cosine, sine = cos_ref[...], sin_ref[...]
    scale = 1.0 / math.sqrt(HD)
    query = turn(linear[:, 0:width], cosine, sine) * scale
    pack_ref[:, 0:width] = query.astype(BF)
    pack_ref[:, width : 2 * width] = turn(linear[:, width : 2 * width], cosine, sine).astype(BF)
    pack_ref[:, 2 * width : 3 * width] = linear[:, 2 * width : 3 * width].astype(BF)
    pack_ref[:, 3 * width : 4 * width] = contract_cols(load(g_ref), out_ref[...]).astype(BF)


def weights_kernel(
    peers, g_ref, value_ref, att_ref, back_ref, cos_ref, sin_ref,
    linear_out, terms_out, bias_out, *rest
):
    *out_out, qkv_s, out_s = rest
    step = pl.program_id(0)
    width = cos_ref.shape[1]

    @pl.when(step == 0)
    def _():
        for ref in (qkv_s, out_s, bias_out):
            ref[...] = jnp.zeros_like(ref)

    cosine, sine = cos_ref[...], -sin_ref[...]
    scale = 1.0 / math.sqrt(HD)
    linear = jnp.concatenate(
        [
            turn(back_ref[:, 0:width] * scale, cosine, sine),
            turn(back_ref[:, width : 2 * width], cosine, sine),
            back_ref[:, 2 * width : 3 * width],
        ],
        -1,
    ).astype(BF)
    linear_out[...] = linear
    qkv_s[...] += contract_rows(value_ref[...], linear)
    out_s[...] += contract_rows(att_ref[...], load(g_ref))
    bias_out[...] += row_sum(linear.astype(F32))

    @pl.when(step == pl.num_programs(0) - 1)
    def _():
        terms_out[:, 0 : 3 * width] = qkv_s[...].astype(BF)
        if peers:
            pack_rows(terms_out, 3 * width, terms_out.shape[1] - 3 * width, out_s, peers)
        else:
            out_out[0][...] = out_s[...].astype(BF)


def flow_kernel(
    x_ref, flow_ref, linear_ref, qkv_ref, gain_ref, shift_ref, flow_out, gain_out, shift_out
):
    @pl.when(pl.program_id(0) == 0)
    def _():
        for ref in (gain_out, shift_out):
            ref[...] = jnp.zeros_like(ref)

    gain = gain_ref[...]
    unit, _ = normed(load(x_ref), gain, shift_ref[...])
    back = contract_cols(linear_ref[...], qkv_ref[...])
    store(flow_out, (load(flow_ref).astype(F32) + back * gain).astype(BF))
    gain_out[...] += row_sum(back * unit)
    shift_out[...] += row_sum(back)


def hidden_kernel(hid_ref, att_ref, out_ref, hid_out):
    store(hid_out, (load(hid_ref).astype(F32) + dot(att_ref[...], out_ref[...])).astype(BF))


def pair_kernel(rows, even_ref, got_ref, left_ref, left_sent, right_ref, right_sent):
    half = even_ref.shape[1] // 2
    for k in range(4):
        at = pl.ds(k * rows, rows)
        total = even_ref[at, :].astype(F32) + got_ref[at, :].astype(F32)
        left, right = total[:, :half], total[:, half:]
        if k < 2:
            left_ref[k] = left
        else:
            left_sent[0, k - 2] = left.astype(BF)
        if k % 2 == 0:
            right_ref[k // 2] = right
        else:
            right_sent[k // 2] = right.astype(BF)


def pair_sums(even, got, rows):
    shape = (2, rows, even.shape[1] // 2)
    return pl.pallas_call(
        partial(pair_kernel, rows),
        out_shape=[
            jax.ShapeDtypeStruct(shape, F32),
            jax.ShapeDtypeStruct((1,) + shape, BF),
            jax.ShapeDtypeStruct(shape, F32),
            jax.ShapeDtypeStruct(shape, BF),
        ],
        in_specs=[pl.BlockSpec(memory_space=pltpu.VMEM)] * 2,
        out_specs=[pl.BlockSpec(memory_space=pltpu.VMEM)] * 4,
        compiler_params=pltpu.CompilerParams(vmem_limit_bytes=60 * 1024 * 1024),
        cost_estimate=pl.CostEstimate(flops=1024, bytes_accessed=1024, transcendentals=0),
        name="pair_sums",
    )(even, got)


def first_half():
    return pl.program_id(0) < pl.num_programs(0) // 2


def load(pair):
    return jnp.where(first_half(), pair[0][...], pair[1][...])


def store(pair, value):
    @pl.when(first_half())
    def _():
        pair[0][...] = value

    @pl.when(jnp.logical_not(first_half()))
    def _():
        pair[1][...] = value


def by_tokens(kernel, tokens, pairs, streamed, fixed, pairs_out, streamed_out, fixed_out, scratch, name):
    block = math.gcd(tokens // 2, 512)
    steps = tokens // block
    stream = lambda n: pl.BlockSpec((block, n), lambda i: (i, 0))
    whole = lambda shape: pl.BlockSpec(shape, lambda i: (0, 0))
    halves = lambda n: [
        pl.BlockSpec((block, n), lambda i: (jnp.minimum(i, steps // 2 - 1), 0)),
        pl.BlockSpec((block, n), lambda i: (jnp.maximum(i - steps // 2, 0), 0)),
    ]
    counts = [2] * len(pairs) + [1] * (len(streamed) + len(fixed))
    counts += [2] * len(pairs_out) + [1] * (len(streamed_out) + len(fixed_out) + len(scratch))

    def body(*refs):
        refs, given = list(refs), []
        for count in counts:
            given.append(refs.pop(0) if count == 1 else (refs.pop(0), refs.pop(0)))
        kernel(*given)

    inputs = [v for pair in pairs for v in pair] + list(streamed) + list(fixed)
    outputs = [jax.ShapeDtypeStruct((tokens // 2, n), BF) for n in pairs_out for _ in range(2)]
    outputs += [jax.ShapeDtypeStruct((tokens, n), BF) for n in streamed_out] + list(fixed_out)
    result = pl.pallas_call(
        body,
        grid=(steps,),
        in_specs=[spec for pair in pairs for spec in halves(pair[0].shape[1])]
        + [stream(v.shape[1]) for v in streamed]
        + [whole(v.shape) for v in fixed],
        out_specs=[spec for n in pairs_out for spec in halves(n)]
        + [stream(n) for n in streamed_out]
        + [whole(v.shape) for v in fixed_out],
        out_shape=outputs,
        scratch_shapes=scratch,
        compiler_params=pltpu.CompilerParams(vmem_limit_bytes=60 * 1024 * 1024),
        cost_estimate=pl.CostEstimate(flops=1024, bytes_accessed=1024, transcendentals=0),
        name=name,
    )(*inputs)
    result, given = list(result), []
    for count in [2] * len(pairs_out) + [1] * (len(streamed_out) + len(fixed_out)):
        given.append(result.pop(0) if count == 1 else (result.pop(0), result.pop(0)))
    return given


def attend_kernel(
    heads, ctx, near,
    spot_ref, pack_ref, seg_col_ref, seg_row_ref,
    out_ref, back_ref,
    q_s, k_s, v_s, g_s, dq_s, dk_s, dv_s,
):
    length = pack_ref.shape[0] // near
    width = out_ref.shape[1]
    rows = length // ctx
    block = math.gcd(rows, 256)
    spot = spot_ref[0]

    def place(i, x):
        other = spot ^ i
        return pl.multiple_of((((other >> 1) + (other & 1) * (ctx // 2)) * near + x) * rows, rows)

    def prepare(step, carry):
        i, x = step // near, step % near
        pack = pack_ref[pl.ds(place(i, x), rows), :]
        for n, target in enumerate((q_s, k_s, v_s, g_s)):
            for h in range(heads):
                low = n * width + h * HD
                target[x * heads + h, pl.ds(i * rows, rows), :] = pack[:, low : low + HD]
        return carry

    lax.fori_loop(0, ctx * near, prepare, 0)
    dk_s[...] = jnp.zeros_like(dk_s)
    dv_s[...] = jnp.zeros_like(dv_s)

    def one(h, start, size):
        at = pl.ds(start, block)
        query, grad = q_s[h, at, :], g_s[h, at, :]
        keys, values = k_s[h, 0:size, :], v_s[h, 0:size, :]
        scores = contract_cols(query, keys)
        row = start + lax.broadcasted_iota(jnp.int32, (block, size), 0)
        col = lax.broadcasted_iota(jnp.int32, (block, size), 1)
        x = h // heads
        seg_col = seg_col_ref[pl.ds(x * length + start, block), :]
        allowed = (seg_col == seg_row_ref[pl.ds(x, 1), 0:size]) & (row >= col)
        scores = jnp.where(allowed, scores, NEG)
        raw = jnp.exp(scores - jnp.max(scores, -1, keepdims=True))
        prob = raw * (1.0 / jnp.sum(raw, -1, keepdims=True))
        prob_low = prob.astype(BF)
        grad_prob = contract_cols(grad, values)
        delta = jnp.sum(prob * grad_prob, -1, keepdims=True)
        grad_score = (prob * (grad_prob - delta)).astype(BF)
        dv_s[h, 0:size, :] += contract_rows(prob_low, grad)
        dk_s[h, 0:size, :] += contract_rows(grad_score, query)
        dq_s[h, at, :] = dot(grad_score, keys)
        q_s[h, at, :] = dot(prob_low, values).astype(BF)

    count = length // block
    if count <= 4:

        def each(h, carry):
            for i in range(count):
                one(h, i * block, (i + 1) * block)
            return carry

        lax.fori_loop(0, near * heads, each, 0)
    else:

        def each(step, carry):
            one(step // count, pl.multiple_of(step % count * block, block), length)
            return carry

        lax.fori_loop(0, near * heads * count, each, 0)

    def finish(step, carry):
        i, x = step // near, step % near
        at = pl.ds(place(i, x), rows)

        def join(source):
            return jnp.concatenate(
                [source[x * heads + h, pl.ds(i * rows, rows), :] for h in range(heads)], -1
            )

        out_ref[at, :] = join(q_s)
        for n, source in enumerate((dq_s, dk_s, dv_s)):
            back_ref[at, n * width : (n + 1) * width] = join(source)
        return carry

    lax.fori_loop(0, ctx * near, finish, 0)


def attend(spot, pack, seg, heads, ctx):
    near = seg.shape[0]
    tokens, width = pack.shape[0], pack.shape[1] // 4
    length = tokens // near
    whole = lambda: pl.BlockSpec(memory_space=pltpu.VMEM)
    shape = (near * heads, length, HD)
    return pl.pallas_call(
        partial(attend_kernel, heads, ctx, near),
        out_shape=(
            jax.ShapeDtypeStruct((tokens, width), BF),
            jax.ShapeDtypeStruct((tokens, 3 * width), F32),
        ),
        in_specs=[pl.BlockSpec(memory_space=pltpu.SMEM)] + [whole() for _ in range(3)],
        out_specs=(whole(), whole()),
        scratch_shapes=[pltpu.VMEM(shape, BF)] * 4 + [pltpu.VMEM(shape, F32)] * 3,
        compiler_params=pltpu.CompilerParams(vmem_limit_bytes=60 * 1024 * 1024),
        cost_estimate=pl.CostEstimate(flops=1024, bytes_accessed=1024, transcendentals=0),
        name="attend",
    )(spot[None], pack, seg.reshape(-1, 1), seg)


def local(
    seq,
    ctx,
    hidden_in,
    segments,
    positions,
    ln1_gain,
    ln1_bias,
    ln2_gain,
    ln2_bias,
    qkv_weight,
    qkv_bias,
    out_weight,
    out_bias,
    up_weight,
    up_bias,
    down_weight,
    down_bias,
    out_grad,
):
    lay = Layout(seq, ctx)
    near, far, team = lay.near, lay.far, lay.team
    tokens, width = hidden_in.shape[1:]
    rows = qkv_weight.shape[0]
    depth = rows * team
    hidden = up_weight.shape[1]
    piece = hidden // (seq * ctx)
    share = hidden // team
    heads = H // team
    part = heads * HD
    out_rows = part // far
    cuts = depth // out_rows
    source_own = hidden_in[0]
    cotangent_own = out_grad[0]

    w_down = lay.gather_far(down_weight).reshape(share, width)

    qkv_cut = qkv_weight.reshape(rows, 3, near, ctx, part).transpose(2, 3, 0, 1, 4)
    up_cut = up_weight.reshape(rows, far, near, ctx, piece).transpose(2, 3, 0, 1, 4)
    payload = jnp.concatenate(
        [qkv_cut.reshape(near, ctx, rows, 3 * part), up_cut.reshape(near, ctx, rows, share)], 3
    )
    payload = lay.exchange_near(payload)
    source_steps = lay.beside(after(source_own, payload)), lay.across(source_own)
    across = lay.across(cotangent_own)
    small = [ln1_gain, ln1_bias, ln2_gain, ln2_bias, out_bias, down_bias, qkv_bias, up_bias]
    small = [v.astype(F32) for v in small + [segments[0], positions[0]]]
    sizes = [v.shape[0] for v in small]
    vectors = lay.gather_all(after(jnp.concatenate(small), payload))
    cut_at = [sum(sizes[:k]) for k in range(len(sizes) + 1)]
    small = [vectors[:, cut_at[k] : cut_at[k + 1]] for k in range(len(sizes))]
    seg, places = small.pop(-2), small.pop(-1)
    small = [v.reshape(-1) for v in small]
    gain_one, bias_one, gain_two, bias_two, b_out, b_down, b_qkv, b_up = small
    b_qkv = lax.dynamic_index_in_dim(b_qkv.reshape(3, team, part), lay.index, 1, keepdims=False)
    b_up = lax.dynamic_index_in_dim(b_up.reshape(far, team, piece), lay.index, 1, keepdims=False)
    seg, places = [
        lax.dynamic_index_in_dim(v.reshape(far, team, tokens), lay.far_index, 0, keepdims=False)
        for v in (seg, places)
    ]
    x_bits = jnp.arange(near)
    seg = seg.reshape(near, ctx * tokens)[x_bits ^ lay.inner].astype(jnp.int32)
    order = jnp.array([(x * ctx + k) for x, k in lay.order()])
    places = places[order ^ lay.index].reshape(-1)

    line = lambda v: v.reshape(1, -1)
    lines = [line(v) for v in (gain_two, bias_two, b_up, gain_one, bias_one, b_qkv)]

    lane = jnp.arange(part) % HD
    frequency = 10000.0 ** (-2.0 * (lane % (ROT // 2)).astype(F32) / ROT)
    frequency = jnp.where(lane < ROT, frequency, 0.0)
    theta = places[:, None] * frequency[None, :]
    cos_wide = jnp.cos(theta)
    sin_wide = jnp.where(lane < ROT // 2, -1.0, 1.0)[None, :] * jnp.sin(theta)

    payload = after(payload, vectors, source_steps[0], *source_steps[1], *across)
    payload = lax.all_to_all(payload, "ctx", 0, 0, tiled=True)
    cotangent_steps = lay.beside(after(cotangent_own, payload)), across
    payload = payload.transpose(1, 0, 2, 3).reshape(depth, -1)
    w_up = lay.gather_far(payload[:, 3 * part :]).reshape(width, share)

    source = lay.gather_team(source_own, *source_steps, 0, [w_down, cos_wide, sin_wide] + lines)
    cotangent = lay.gather_team(cotangent_own, *cotangent_steps, 1)

    out_part = lay.own_heads(after(out_weight, payload))
    out_part = out_part.reshape(out_rows, cuts, width // cuts).transpose(1, 0, 2)
    third = jnp.concatenate([payload[:, : 3 * part], out_part.reshape(depth, -1)], 1)
    third = lay.gather_far(after(third, w_up)).reshape(width, -1)

    count_all = team * tokens
    vector = jax.ShapeDtypeStruct((1, width), F32)

    hid, flow, input_one, terms, gain_two_sum, shift_two_sum, grad_up_b = by_tokens(
        partial(mlp_kernel, far),
        count_all,
        [source, cotangent],
        [],
        [w_up, w_down] + lines[:5],
        [width, width],
        [width],
        [
            jax.ShapeDtypeStruct((width, 2 * share), BF),
            vector,
            vector,
            jax.ShapeDtypeStruct((1, share), F32),
        ],
        [pltpu.VMEM((share, width), F32), pltpu.VMEM((width, share), F32)],
        "feed_forward",
    )
    terms_sum = lay.scatter_far(terms.reshape(far, depth, 2 * share))

    column = width // cuts
    packed = out_rows % 16 == 0 and column % 128 == 0
    if not packed:
        w_out = third[:, 3 * part :].reshape(far, cuts, out_rows, column)
        w_out = w_out.transpose(0, 2, 1, 3).reshape(part, width)
        third = jnp.concatenate([third[:, : 3 * part], w_out.T], 1)
    pack, w_qkv, w_out = by_tokens(
        partial(head_kernel, far if packed else 0),
        count_all,
        [cotangent],
        [input_one, cos_wide, sin_wide],
        [third, lines[5]],
        [],
        [4 * part],
        [jax.ShapeDtypeStruct((width, 3 * part), BF), jax.ShapeDtypeStruct((part, width), BF)],
        [],
        "heads",
    )
    attended, back = attend(lay.spot, pack, seg, heads, ctx)
    (hid,) = by_tokens(
        hidden_kernel, count_all, [hid], [attended], [w_out], [width], [], [], [], "hidden"
    )
    hid_got = swap(hid[1], "ctx", ctx, 1)
    linear, last, grad_qkv_b, *out_terms = by_tokens(
        partial(weights_kernel, far if packed else 0),
        count_all,
        [cotangent],
        [after(input_one, *hid), attended, back, cos_wide, sin_wide],
        [],
        [],
        [3 * part],
        [
            jax.ShapeDtypeStruct((width, 3 * part + packed * column), BF),
            jax.ShapeDtypeStruct((1, 3 * part), F32),
        ]
        + [jax.ShapeDtypeStruct((part, width), BF)] * (not packed),
        [pltpu.VMEM((width, 3 * part), F32), pltpu.VMEM((part, width), F32)],
        "weights",
    )
    last = last.reshape(far, depth, -1)
    if not packed:
        out_terms = out_terms[0].reshape(far, out_rows, cuts, column).transpose(0, 2, 1, 3)
        last = jnp.concatenate([last, out_terms.reshape(far, depth, column)], 2)
    last_sum = lay.scatter_far(after(last, terms_sum))
    hid_first = lay.pair_blocks(after(hid[0], linear), hid_got)
    linear, flow = after((linear, tuple(flow)), terms_sum, *hid_first)
    flow, gain_one_sum, shift_one_sum = by_tokens(
        flow_kernel,
        count_all,
        [source, flow],
        [linear],
        [w_qkv, lines[3], lines[4]],
        [width],
        [],
        [vector, vector],
        [],
        "flow",
    )
    hidden_sum, hid_came, _ = lay.scatter_team(hid_first)
    flow = after(tuple(flow), *hid_came)
    flow_first = lay.pair_blocks(after(flow[0], last_sum), swap(flow[1], "ctx", ctx, 1))
    result = (source_own.astype(F32) + hidden_sum + (b_out + b_down)).astype(BF)[None]

    flow, flow_came, flow_done = lay.scatter_team(flow_first)
    last = after(last_sum, *flow_came)
    terms_sum = after(terms_sum, *flow_came)

    cotangent_full = cotangent_own.astype(F32)
    grad_bias = jnp.sum(cotangent_full, 0)
    mine = (jnp.arange(team) == lay.index)[None, :, None]
    grad_qkv_b = jnp.where(mine, grad_qkv_b.reshape(3, 1, part), 0.0)
    grad_up_b = jnp.where(mine, grad_up_b.reshape(far, 1, piece), 0.0)
    table = [gain_one_sum, shift_one_sum, gain_two_sum, shift_two_sum, grad_bias]
    table = [v.reshape(seq * ctx, -1) for v in table + [grad_qkv_b, grad_up_b]]
    sums = lay.scatter_all(after(jnp.concatenate(table, 1), *flow_came))
    sizes = [v.shape[1] for v in table]
    sums = [sums[sum(sizes[:k]) : sum(sizes[: k + 1])] for k in range(len(sizes))]

    grad_down_w = terms_sum[:, share:].reshape(-1, piece, share)
    grad_down_w = grad_down_w.transpose(1, 0, 2).reshape(piece, width).astype(F32)
    both = jnp.concatenate([last[:, : 3 * part], terms_sum[:, :share]], 1)
    both = lay.exchange(both.reshape(near, ctx, rows, -1))
    grad_up_w = (
        both[..., 3 * part :]
        .reshape(ctx, near, rows, far, piece)
        .transpose(2, 3, 1, 0, 4)
        .reshape(rows, hidden)
        .astype(F32)
    )
    out_sum = last[:, 3 * part :].reshape(cuts, out_rows, width // cuts).transpose(1, 0, 2)
    grad_out_w = lay.own_heads(out_sum.reshape(out_rows, width), back=True).astype(F32)
    grad_qkv_w = (
        both[..., : 3 * part]
        .reshape(ctx, near, rows, 3, part)
        .transpose(2, 3, 1, 0, 4)
        .reshape(rows, 3 * width)
        .astype(F32)
    )

    wide = source_own.astype(F32)
    centred = wide - jnp.mean(wide, -1, keepdims=True)
    inverse = lax.rsqrt(jnp.mean(centred * centred, -1, keepdims=True) + EPS)
    unit = centred * inverse
    passed = (
        flow - jnp.mean(flow, -1, keepdims=True) - unit * jnp.mean(flow * unit, -1, keepdims=True)
    ) * inverse
    input_grad = (cotangent_full + passed)[None]
    return (
        result,
        input_grad,
        sums[0],
        sums[1],
        sums[2],
        sums[3],
        grad_qkv_w,
        sums[5],
        grad_out_w,
        sums[4],
        grad_up_w,
        sums[6],
        grad_down_w,
        sums[4],
    )


def solution(mesh):
    both = P(("seq", "ctx"))
    matrix = P(("seq", "ctx"), None)
    row = P("seq", "ctx", None)
    params = (both, both, both, both, matrix, both, matrix, both, matrix, both, matrix, both)
    in_specs = (row, P("seq", "ctx"), P("seq", "ctx")) + params + (row,)
    out_specs = (row, row) + params
    body = partial(local, mesh.shape["seq"], mesh.shape["ctx"])
    return jax.shard_map(body, mesh=mesh, in_specs=in_specs, out_specs=out_specs, check_vma=False)
```

time: 345 us -> 279 us (0.81)
  Pallas kernels: 25.7 us -> 92.3 us
  matrix products: 62.1 us -> 0 us
  blocking collectives: 32 us -> 0 us
  waiting for transfers between devices: 101 us -> 77 us
  local copies, waits for them, and re-layouts: 36.1 us -> 24.8 us
    pallas_call x1 -> x8, Pallas kernels: 25.7 us -> 92.3 us  [the longest x5 61.9 us: by_tokens(): pl.pallas_call(body, grid=(steps,), in_specs=[spec for pair in pairs for...]
    dot_general x12 -> x0, matrix products: 62.1 us -> none  [the longest x4 24.9 us: dot(): return jnp.dot(left, right, preferred_element_type=F32)]
    all_gather x1 -> x0, blocking collectives: 22.1 us -> none  [gather_seq(): lax.all_gather(shard, 'seq', axis=0, axis_index_groups=outer_groups(seq))]
    ppermute x19 -> x30, waiting for transfers between devices: 75.7 us -> 56.8 us  [swap(): return lax.ppermute(value, axis, [(i, i ^ bits) for i in range(size)])]
    all_to_all x1 -> x0, blocking collectives: 9.93 us -> none  [local(): lax.all_to_all(payload, 'ctx', 0, 0, tiled=True).reshape(depth, -1)]
    convert_element_type x10 -> x6, other arithmetic: 10.5 us -> 3.23 us  [the longest x1 1 us: local(): grad_up_w = both[..., 3 * part:].reshape(ctx, near, rows, far, piece).tra...]
    ppermute x2, waiting for transfers between devices: 11.8 us -> 5.64 us  [own_heads(): return lax.ppermute(value, ('seq', 'ctx'), pairs)]
    all_to_all x2, waiting for transfers between devices: 2.58 us -> 8.58 us  [the longest x1 6.17 us: local(): payload = lax.all_to_all(payload, 'ctx', 0, 0, tiled=True)]
  transfers between devices with their start and end apart: 28 -> 39, of which waited for: 11 -> 21; matrix products, arithmetic and copies ran while one was open for 33% -> 18% of each run, Pallas kernels for 8% -> 34%
where the time goes in v2:
time: 279 us; the launch traced here: 275 us
  Pallas kernels  92.3 us (33%)
  waiting for transfers between devices  77 us (28%)
  starting transfers between devices  35.5 us (13%)
  other arithmetic  31 us (11%)
  local copies, waits for them, and re-layouts  24.8 us (9%)
  between operations  14.7 us (5%)
    pallas_call x5, Pallas kernels, by_tokens(): pl.pallas_call(body, grid=(steps,), in_specs=[spec for pair in pairs for...  61.9 us
    ppermute x30, waiting for transfers between devices, swap(): return lax.ppermute(value, axis, [(i, i ^ bits) for i in range(size)])  56.8 us
    pallas_call x1, Pallas kernels, attend(): pl.pallas_call(partial(attend_kernel, heads, ctx, near), out_shape=(jax.S...  22.3 us
    ppermute x30, starting transfers between devices, swap(): return lax.ppermute(value, axis, [(i, i ^ bits) for i in range(size)])  18.1 us
    ppermute x2, starting transfers between devices, own_heads(): return lax.ppermute(value, ('seq', 'ctx'), pairs)  8.49 us
    pallas_call x2, Pallas kernels, pair_sums(): pl.pallas_call(partial(pair_kernel, rows), out_shape=[jax.ShapeDtypeStruc...  8 us
    all_to_all x1, waiting for transfers between devices, local(): payload = lax.all_to_all(payload, 'ctx', 0, 0, tiled=True)  6.17 us
    ppermute x2, waiting for transfers between devices, own_heads(): return lax.ppermute(value, ('seq', 'ctx'), pairs)  5.64 us
  transfers between devices with their start and end apart: 39, of which 21 were waited for; matrix products, arithmetic and copies ran while one was open for 18% of the time, Pallas kernels for 34%

profile of v2, /device:TPU:6, one launch (start us, length us, event | category | flops | bytes accessed | tf_op | source)
XLA Modules:
  0.0 275.2 jit_solution(12538708715653670146)
XLA Ops:
  10.6 2.0 collective-permute-start.2
  13.0 4.4 %collective-permute-done = bf16[4,32,896]{2,1,0:T(8,128)(2,1)S(1)} collective-permute-done((bf16[4,32,896]{2,1,0:T(8,128)(2,1)S(1)}, bf16[4,32,896]{2,1,0:T(8,128)(2,1)S(1)}, u32[]{:S(2)}, u32[]{:S(2)}) %collective-permute-start) | collective-permute-done | bytes 229408 | tf_op jit(solution)/shard_map/ppermute | solution.py:34
  18.8 3.1 %collective-permute-done.4 = f32[1,928]{1,0:T(1,128)S(1)} collective-permute-done((f32[1,928]{1,0:T(1,128)S(1)}, f32[1,928]{1,0:T(1,128)S(1)}, u32[]{:S(2)}, u32[]{:S(2)}) %collective-permute-start.4) | collective-permute-done | bytes 3744 | tf_op jit(solution)/shard_map/ppermute | solution.py:34
  23.5 2.5 collective-permute-done.5
  26.0 2.4 collective-permute-start.6
  29.0 2.6 collective-permute-done.6
  33.5 3.7 %collective-permute-done.8 = f32[16,928]{1,0:T(8,128)S(1)} collective-permute-done((f32[16,928]{1,0:T(8,128)S(1)}, f32[16,928]{1,0:T(8,128)S(1)}, u32[]{:S(2)}, u32[]{:S(2)}) %collective-permute-start.8) | collective-permute-done | bytes 59424 | tf_op jit(solution)/shard_map/ppermute | solution.py:34
  39.3 3.9 %all-to-all-start = ((bf16[4,2,32,896]{3,2,1,0:T(8,128)(2,1)}), bf16[4,2,32,896]{3,2,1,0:T(8,128)(2,1)S(1)}, u32[]{:S(2)}, u32[]{:S(2)}) async-start(bf16[4,2,32,896]{3,2,1,0:T(8,128)(2,1)} %pad_maximum_fusion.2), calls=%async_computation | async-start | bytes 917504 | tf_op jit(solution)/shard_map/all_to_all | solution.py:601
  43.5 6.2 %all-to-all-done = bf16[4,2,32,896]{3,2,1,0:T(8,128)(2,1)S(1)} async-done(((bf16[4,2,32,896]{3,2,1,0:T(8,128)(2,1)}), bf16[4,2,32,896]{3,2,1,0:T(8,128)(2,1)S(1)}, u32[]{:S(2)}, u32[]{:S(2)}) %all-to-all-start) | async-done | bytes 458784 | tf_op jit(solution)/shard_map/all_to_all | solution.py:601
  59.4 5.5 %fusion.12 = (f32[2048,128]{1,0:T(8,128)}, f32[2048,128]{1,0:T(8,128)}) fusion(f32[128]{0:T(128)S(1)} %get-tuple-element.146, f32[128]{0:T(128)S(1)} %get-tuple-element.147, f32[2048]{0:T(1024)S(1)} %bitcast.208), kind=kLoop, calls=%fused_computation.24 | loop fusion | flops 524288 | bytes 2106368 | tf_op jit(solution)/shard_map/mul | solution.py:598
  65.8 2.6 pad_maximum_fusion.refs_0_
  68.4 4.0 %collective-permute-done.12 = bf16[256,1024]{1,0:T(8,128)(2,1)} collective-permute-done((bf16[256,1024]{1,0:T(8,128)(2,1)S(1)}, bf16[256,1024]{1,0:T(8,128)(2,1)}, u32[]{:S(2)}, u32[]{:S(2)}) %collective-permute-start.12) | collective-permute-done | bytes 524320 | tf_op jit(solution)/shard_map/ppermute | solution.py:34
  72.4 9.6 %collective-permute-done.11 = bf16[256,1024]{1,0:T(8,128)(2,1)} collective-permute-done((bf16[256,1024]{1,0:T(8,128)(2,1)S(1)}, bf16[256,1024]{1,0:T(8,128)(2,1)}, u32[]{:S(2)}, u32[]{:S(2)}) %collective-permute-start.11) | collective-permute-done | bytes 524320 | tf_op jit(solution)/shard_map/ppermute | solution.py:34
  83.6 3.7 %collective-permute-start.14 = (bf16[32,1024]{1,0:T(8,128)(2,1)S(1)}, bf16[32,1024]{1,0:T(8,128)(2,1)S(1)}, u32[]{:S(2)}, u32[]{:S(2)}) collective-permute-start(bf16[32,1024]{1,0:T(8,128)(2,1)S(1)} %copy-done.32), channel_id=1, source_target_pairs={{0,0},{4,1},{8,2},{12,3},{16,4},{20,5},{24,6},{28,7},{1,8},{5,9},{... | collective-permute-start | bytes 196616 | tf_op jit(solution)/shard_map/ppermute | solution.py:78
  88.2 5.6 %collective-permute-done.14 = bf16[32,1024]{1,0:T(8,128)(2,1)S(1)} collective-permute-done((bf16[32,1024]{1,0:T(8,128)(2,1)S(1)}, bf16[32,1024]{1,0:T(8,128)(2,1)S(1)}, u32[]{:S(2)}, u32[]{:S(2)}) %collective-permute-start.14) | collective-permute-done | bytes 65568 | tf_op jit(solution)/shard_map/ppermute | solution.py:78
  94.7 27.0 %feed_forward.1 = (bf16[1024,1024]{1,0:T(8,128)(2,1)}, bf16[1024,1024]{1,0:T(8,128)(2,1)}, bf16[1024,1024]{1,0:T(8,128)(2,1)}, bf16[1024,1024]{1,0:T(8,128)(2,1)...) custom-call(bf16[1024,1024]{1,0:T(8,128)(2,1)} %pad_maximum_fusion.r, ...), custom_call_target="tpu_custom_call" | custom-call | flops 1024 | bytes 1024 | tf_op jit(solution)/shard_map/feed_forward/pallas_call | solution.py:398
  124.6 8.4 %heads.1 = (bf16[2048,512]{1,0:T(8,128)(2,1)}, bf16[1024,384]{1,0:T(8,128)(2,1)}, bf16[128,1024]{1,0:T(8,128)(2,1)}) custom-call(bf16[1024,1024]{1,0:T(8,128)(2,1)} %copy-done, bf16[1024,1024]{1,0:T(8,128)(2,1)} %collective-permute-done.13.refs_3_.refs_1_, bf16[2048,1024]{1,0:T(8,128)(2,1)} %get-tuple-element.79.refs_2_, ...), custom_call_target="tpu_custom_call" | custom-call | flops 1024 | bytes 1024 | tf_op jit(solution)/shard_map/heads/pallas_call | solution.py:398
  133.0 22.3 %attend.1 = (bf16[2048,128]{1,0:T(8,128)(2,1)}, f32[2048,384]{1,0:T(8,128)}) custom-call(s32[1]{0:T(128)} %bitcast.19.spot_ref, bf16[2048,512]{1,0:T(8,128)(2,1)} %get-tuple-element.74.pack_ref, s32[2048,1]{1,0:T(8,128)} %bitcast.180, s32[2,1024]{1,0:T(2,128)} %get-tuple-element.137.seg_row_ref), custom_call_target="tpu_custom_call" | custom-call | flops 1024 | bytes 1024 | tf_op jit(solution)/shard_map/attend/pallas_call | solution.py:510
  155.4 6.2 %hidden.1 = (bf16[1024,1024]{1,0:T(8,128)(2,1)}, bf16[1024,1024]{1,0:T(8,128)(2,1)}) custom-call(bf16[1024,1024]{1,0:T(8,128)(2,1)} %get-tuple-element.69.refs_0_, bf16[1024,1024]{1,0:T(8,128)(2,1)} %get-tuple-element.70.refs_1_, bf16[2048,128]{1,0:T(8,128)(2,1)} %get-tuple-element.75.refs_2_.refs_3_, bf16[128,1024]{1,0:T(8,128)(2,1)} %get-tuple-element.76.refs_3_), custom_call_target="tpu_custom_call" | custom-call | flops 1024 | bytes 1024 | tf_op jit(solution)/shard_map/hidden/pallas_call | solution.py:398
  161.7 9.3 %weights.1 = (bf16[2048,384]{1,0:T(8,128)(2,1)}, bf16[1024,512]{1,0:T(8,128)(2,1)}, f32[1,384]{1,0:T(1,128)}) custom-call(bf16[1024,1024]{1,0:T(8,128)(2,1)} %copy-done, bf16[1024,1024]{1,0:T(8,128)(2,1)} %collective-permute-done.13.refs_3_.refs_1_, bf16[2048,1024]{1,0:T(8,128)(2,1)} %get-tuple-element.79.refs_2_, ...), custom_call_target="tpu_custom_call" | custom-call | flops 1024 | bytes 1024 | tf_op jit(solution)/shard_map/weights/pallas_call | solution.py:398
  172.4 4.0 %pair_sums.2 = (f32[2,256,512]{2,1,0:T(8,128)}, bf16[1,2,256,512]{3,2,1,0:T(8,128)(2,1)}, f32[2,256,512]{2,1,0:T(8,128)}, bf16[2,256,512]{2,1,0:T(8,128)(2,1)}) custom-call(bf16[1024,1024]{1,0:T(8,128)(2,1)} %get-tuple-element.82.even_ref, bf16[1024,1024]{1,0:T(8,128)(2,1)} %copy-done.5), custom_call_target="tpu_custom_call" | custom-call | flops 1024 | bytes 1024 | tf_op jit(solution)/shard_map/pair_sums/pallas_call | solution.py:343
  176.8 11.0 %flow.1 = (bf16[1024,1024]{1,0:T(8,128)(2,1)}, bf16[1024,1024]{1,0:T(8,128)(2,1)}, f32[1,1024]{1,0:T(1,128)}, f32[1,1024]{1,0:T(1,128)}) custom-call(bf16[1024,1024]{1,0:T(8,128)(2,1)} %pad_maximum_fusion.refs_0_, bf16[1024,1024]{1,0:T(8,128)(2,1)} %collective-permute-done.9.refs_1_, bf16[1024,1024]{1,0:T(8,128)(2,1)} %get-tuple-element.90.refs_2_, ...), custom_call_target="tpu_custom_call" | custom-call | flops 1024 | bytes 1024 | tf_op jit(solution)/shard_map/flow/pallas_call | solution.py:398
  187.8 3.1 %collective-permute-done.16 = bf16[2,256,512]{2,1,0:T(8,128)(2,1)S(1)} collective-permute-done((bf16[2,256,512]{2,1,0:T(8,128)(2,1)}, bf16[2,256,512]{2,1,0:T(8,128)(2,1)S(1)}, u32[]{:S(2)}, u32[]{:S(2)}) %collective-permute-start.16) | collective-permute-done | bytes 524320 | tf_op jit(solution)/shard_map/ppermute | solution.py:34
  199.8 5.2 %reduce-scatter.5.cloned.1.call-done = bf16[1,256,512]{2,1,0:T(8,128)(2,1)} async-done(((bf16[4,256,512]{2,1,0:T(8,128)(2,1)}), bf16[1,256,512]{2,1,0:T(8,128)(2,1)}) %reduce-scatter.5.cloned.1.call-update) | async-done | bytes 262160 | tf_op jit(solution)/shard_map/reduce_scatter | solution.py:53
  205.0 4.0 %pair_sums.3 = (f32[2,256,512]{2,1,0:T(8,128)}, bf16[1,2,256,512]{3,2,1,0:T(8,128)(2,1)}, f32[2,256,512]{2,1,0:T(8,128)}, bf16[2,256,512]{2,1,0:T(8,128)(2,1)}) custom-call(bf16[1024,1024]{1,0:T(8,128)(2,1)} %get-tuple-element.99.even_ref, bf16[1024,1024]{1,0:T(8,128)(2,1)} %collective-permute-done.20.got_ref), custom_call_target="tpu_custom_call" | custom-call | flops 1024 | bytes 1024 | tf_op jit(solution)/shard_map/pair_sums/pallas_call | solution.py:343
  214.6 8.2 %collective-permute-done.21 = bf16[2,256,512]{2,1,0:T(8,128)(2,1)} collective-permute-done((bf16[2,256,512]{2,1,0:T(8,128)(2,1)}, bf16[2,256,512]{2,1,0:T(8,128)(2,1)}, u32[]{:S(2)}, u32[]{:S(2)}) %collective-permute-start.21) | collective-permute-done | bytes 524320 | tf_op jit(solution)/shard_map/ppermute | solution.py:34
  225.0 4.2 %collective-permute-done.23 = bf16[2,256,512]{2,1,0:T(8,128)(2,1)} collective-permute-done((bf16[2,256,512]{2,1,0:T(8,128)(2,1)}, bf16[2,256,512]{2,1,0:T(8,128)(2,1)}, u32[]{:S(2)}, u32[]{:S(2)}) %collective-permute-start.23) | collective-permute-done | bytes 524320 | tf_op jit(solution)/shard_map/ppermute | solution.py:34
  230.7 4.8 %collective-permute-start.31 = (bf16[32,1024]{1,0:T(8,128)(2,1)S(1)}, bf16[32,1024]{1,0:T(8,128)(2,1)S(1)}, u32[]{:S(2)}, u32[]{:S(2)}) collective-permute-start(bf16[32,1024]{1,0:T(8,128)(2,1)S(1)} %bitcast.207), channel_id=1, source_target_pairs={{0,0},{1,4},{2,8},{3,12},{4,16},{5,20},{6,24},{7,28},{8,1},{9,5},{... | collective-permute-start | bytes 196616 | tf_op jit(solution)/shard_map/ppermute | solution.py:78
  236.2 3.1 %collective-permute-done.26 = f32[2,4,384]{2,1,0:T(4,128)S(1)} collective-permute-done((f32[2,4,384]{2,1,0:T(4,128)S(1)}, f32[2,4,384]{2,1,0:T(4,128)S(1)}, u32[]{:S(2)}, u32[]{:S(2)}) %collective-permute-start.26) | collective-permute-done | bytes 12320 | tf_op jit(solution)/shard_map/ppermute | solution.py:34
  242.3 2.9 %collective-permute-done.28 = f32[2,384]{1,0:T(2,128)S(1)} collective-permute-done((f32[2,384]{1,0:T(2,128)S(1)}, f32[2,384]{1,0:T(2,128)S(1)}, u32[]{:S(2)}, u32[]{:S(2)}) %collective-permute-start.28) | collective-permute-done | bytes 3104 | tf_op jit(solution)/shard_map/ppermute | solution.py:34
  252.1 4.6 %all-to-all-start.1 = ((bf16[4,2,32,896]{3,2,1,0:T(8,128)(2,1)}), bf16[4,2,32,896]{3,2,1,0:T(8,128)(2,1)}, u32[]{:S(2)}, u32[]{:S(2)}) async-start(bf16[4,2,32,896]{3,2,1,0:T(8,128)(2,1)} %copy.91), calls=%async_computation.3 | async-start | bytes 917504 | tf_op jit(solution)/shard_map/all_to_all | solution.py:67
  260.9 2.4 all-to-all-done.1
  (267 shorter events, 68.0 us)
Async XLA Ops:
  7.2 61.2 %all-gather.7.cloned.1.call-start = ((), (), s32[]{:S(2)}) async-start(), calls=%async_computation.6 | async-start | bytes 1310720 | tf_op jit(solution)/shard_map/all_gather | solution.py:50
  10.0 7.4 %collective-permute-start = (bf16[4,32,896]{2,1,0:T(8,128)(2,1)S(1)}, bf16[4,32,896]{2,1,0:T(8,128)(2,1)S(1)}, u32[]{:S(2)}, u32[]{:S(2)}) collective-permute-start(bf16[4,32,896]{2,1,0:T(8,128)(2,1)S(1)} %dynamic-slice_bitcast_fusion.1), channel_id=1, source_target_pairs={{0,4},{4,0},{8,12},{12,8},{16,20},{20,16},{24,28},{28,24},{1,5},{5... | collective-permute-start | bytes 688136 | tf_op jit(solution)/shard_map/ppermute | solution.py:34
  10.6 27.3 %collective-permute-start.10 = (bf16[256,1024]{1,0:T(8,128)(2,1)S(1)}, bf16[256,1024]{1,0:T(8,128)(2,1)S(1)}, u32[]{:S(2)}, u32[]{:S(2)}) collective-permute-start(bf16[256,1024]{1,0:T(8,128)(2,1)S(1)} %bitcast.177), channel_id=1, source_target_pairs={{0,2},{1,3},{2,0},{3,1},{4,6},{5,7},{6,4},{7,5},{8,10},{9,11},{10,... | collective-permute-start | bytes 1572872 | tf_op jit(solution)/shard_map/ppermute | solution.py:34
  10.6 27.3 %collective-permute-start.2 = (bf16[256,1024]{1,0:T(8,128)(2,1)S(1)}, bf16[256,1024]{1,0:T(8,128)(2,1)S(1)}, u32[]{:S(2)}, u32[]{:S(2)}) collective-permute-start(bf16[256,1024]{1,0:T(8,128)(2,1)S(1)} %bitcast.172), channel_id=1, source_target_pairs={{0,2},{1,3},{2,0},{3,1},{4,6},{5,7},{6,4},{7,5},{8,10},{9,11},{10,... | collective-permute-start | bytes 1572872 | tf_op jit(solution)/shard_map/ppermute | solution.py:34
  26.0 5.5 %collective-permute-start.6 = (f32[4,928]{1,0:T(4,128)S(1)}, f32[4,928]{1,0:T(4,128)S(1)}, u32[]{:S(2)}, u32[]{:S(2)}) collective-permute-start(f32[4,928]{1,0:T(4,128)S(1)} %pad_maximum_fusion.7), channel_id=1, source_target_pairs={{0,16},{4,20},{8,24},{12,28},{16,0},{20,4},{24,8},{28,12},{1,17},{... | collective-permute-start | bytes 44552 | tf_op jit(solution)/shard_map/ppermute | solution.py:34
  28.4 10.8 %collective-permute-start.1 = (bf16[256,1024]{1,0:T(8,128)(2,1)S(1)}, bf16[256,1024]{1,0:T(8,128)(2,1)}, u32[]{:S(2)}, u32[]{:S(2)}) collective-permute-start(bf16[256,1024]{1,0:T(8,128)(2,1)S(1)} %bitcast.173), channel_id=1, source_target_pairs={{0,4},{4,0},{8,12},{12,8},{16,20},{20,16},{24,28},{28,24},{1,5},{5... | collective-permute-start | bytes 1572872 | tf_op jit(solution)/shard_map/ppermute | solution.py:34
  39.3 10.4 %all-to-all-start = ((bf16[4,2,32,896]{3,2,1,0:T(8,128)(2,1)}), bf16[4,2,32,896]{3,2,1,0:T(8,128)(2,1)S(1)}, u32[]{:S(2)}, u32[]{:S(2)}) async-start(bf16[4,2,32,896]{3,2,1,0:T(8,128)(2,1)} %pad_maximum_fusion.2), calls=%async_computation | async-start | bytes 917504 | tf_op jit(solution)/shard_map/all_to_all | solution.py:601
  43.2 51.4 %all-gather.9.cloned.1.call-start = ((), (), s32[]{:S(2)}) async-start(), calls=%async_computation.7 | async-start | bytes 1310720 | tf_op jit(solution)/shard_map/all_gather | solution.py:50
  51.2 73.4 %all-gather.11.cloned.1.call-start = ((), (), s32[]{:S(2)}) async-start(), calls=%async_computation.8 | async-start | bytes 1310720 | tf_op jit(solution)/shard_map/all_gather | solution.py:50
  51.9 13.9 %collective-permute-start.3 = (bf16[256,1024]{1,0:T(8,128)(2,1)}, bf16[256,1024]{1,0:T(8,128)(2,1)S(1)}, u32[]{:S(2)}, u32[]{:S(2)}) collective-permute-start(bf16[256,1024]{1,0:T(8,128)(2,1)} %collective-permute-done.1), channel_id=1, source_target_pairs={{0,2},{1,3},{2,0},{3,1},{4,6},{5,7},{6,4},{7,5},{8,10},{9,11},{10,... | collective-permute-start | bytes 1572872 | tf_op jit(solution)/shard_map/ppermute | solution.py:34
  57.4 15.0 %collective-permute-start.12 = (bf16[256,1024]{1,0:T(8,128)(2,1)S(1)}, bf16[256,1024]{1,0:T(8,128)(2,1)}, u32[]{:S(2)}, u32[]{:S(2)}) collective-permute-start(bf16[256,1024]{1,0:T(8,128)(2,1)S(1)} %collective-permute-done.10), channel_id=1, source_target_pairs={{0,4},{4,0},{8,12},{12,8},{16,20},{20,16},{24,28},{28,24},{1,5},{5... | collective-permute-start | bytes 1572872 | tf_op jit(solution)/shard_map/ppermute | solution.py:34
  58.0 23.9 %collective-permute-start.11 = (bf16[256,1024]{1,0:T(8,128)(2,1)S(1)}, bf16[256,1024]{1,0:T(8,128)(2,1)}, u32[]{:S(2)}, u32[]{:S(2)}) collective-permute-start(bf16[256,1024]{1,0:T(8,128)(2,1)S(1)} %bitcast.178), channel_id=1, source_target_pairs={{0,4},{4,0},{8,12},{12,8},{16,20},{20,16},{24,28},{28,24},{1,5},{5... | collective-permute-start | bytes 1572872 | tf_op jit(solution)/shard_map/ppermute | solution.py:34
  68.4 26.3 %collective-permute-start.9 = (bf16[1024,1024]{1,0:T(8,128)(2,1)}, bf16[1024,1024]{1,0:T(8,128)(2,1)}, u32[]{:S(2)}, u32[]{:S(2)}) collective-permute-start(bf16[1024,1024]{1,0:T(8,128)(2,1)} %pad_maximum_fusion.refs_0_), channel_id=1, source_target_pairs={{0,1},{1,0},{2,3},{3,2},{4,5},{5,4},{6,7},{7,6},{8,9},{9,8},{10,11... | collective-permute-start | bytes 6291464 | tf_op jit(solution)/shard_map/ppermute | solution.py:34
  83.5 11.2 %collective-permute-start.13 = (bf16[1024,1024]{1,0:T(8,128)(2,1)S(1)}, bf16[1024,1024]{1,0:T(8,128)(2,1)}, u32[]{:S(2)}, u32[]{:S(2)}) collective-permute-start(bf16[1024,1024]{1,0:T(8,128)(2,1)S(1)} %pad_maximum_fusion.1.refs_2_.refs_0_), channel_id=1, source_target_pairs={{0,1},{1,0},{2,3},{3,2},{4,5},{5,4},{6,7},{7,6},{8,9},{9,8},{10,11... | collective-permute-start | bytes 6291464 | tf_op jit(solution)/shard_map/ppermute | solution.py:34
  83.6 10.3 %collective-permute-start.14 = (bf16[32,1024]{1,0:T(8,128)(2,1)S(1)}, bf16[32,1024]{1,0:T(8,128)(2,1)S(1)}, u32[]{:S(2)}, u32[]{:S(2)}) collective-permute-start(bf16[32,1024]{1,0:T(8,128)(2,1)S(1)} %copy-done.32), channel_id=1, source_target_pairs={{0,0},{4,1},{8,2},{12,3},{16,4},{20,5},{24,6},{28,7},{1,8},{5,9},{... | collective-permute-start | bytes 196616 | tf_op jit(solution)/shard_map/ppermute | solution.py:78
  94.6 82.0 %reduce-scatter.3.cloned.1.call-start = ((), (), s32[]{:S(2)}) async-start(), calls=%async_computation.4 | async-start | bytes 2621440 | tf_op jit(solution)/shard_map/reduce_scatter | solution.py:53
  121.8 83.2 %reduce-scatter.5.cloned.1.call-start = ((), (), s32[]{:S(2)}) async-start(), calls=%async_computation.5 | async-start | bytes 1310720 | tf_op jit(solution)/shard_map/reduce_scatter | solution.py:53
  161.6 9.5 %collective-permute-start.15 = (bf16[1024,1024]{1,0:T(8,128)(2,1)}, bf16[1024,1024]{1,0:T(8,128)(2,1)S(1)}, u32[]{:S(2)}, u32[]{:S(2)}) collective-permute-start(bf16[1024,1024]{1,0:T(8,128)(2,1)} %get-tuple-element.78), channel_id=1, source_target_pairs={{0,1},{1,0},{2,3},{3,2},{4,5},{5,4},{6,7},{7,6},{8,9},{9,8},{10,11... | collective-permute-start | bytes 6291464 | tf_op jit(solution)/shard_map/ppermute | solution.py:34
  176.4 14.6 %collective-permute-start.16 = (bf16[2,256,512]{2,1,0:T(8,128)(2,1)}, bf16[2,256,512]{2,1,0:T(8,128)(2,1)S(1)}, u32[]{:S(2)}, u32[]{:S(2)}) collective-permute-start(bf16[2,256,512]{2,1,0:T(8,128)(2,1)} %bitcast.216), channel_id=1, source_target_pairs={{0,2},{1,3},{2,0},{3,1},{4,6},{5,7},{6,4},{7,5},{8,10},{9,11},{10,... | collective-permute-start | bytes 1572872 | tf_op jit(solution)/shard_map/ppermute | solution.py:34
  176.4 14.6 %collective-permute-start.18 = (bf16[2,256,512]{2,1,0:T(8,128)(2,1)}, bf16[2,256,512]{2,1,0:T(8,128)(2,1)S(1)}, u32[]{:S(2)}, u32[]{:S(2)}) collective-permute-start(bf16[2,256,512]{2,1,0:T(8,128)(2,1)} %get-tuple-element.86), channel_id=1, source_target_pairs={{0,4},{4,0},{8,12},{12,8},{16,20},{20,16},{24,28},{28,24},{1,5},{5... | collective-permute-start | bytes 1572872 | tf_op jit(solution)/shard_map/ppermute | solution.py:34
  190.9 14.0 %collective-permute-start.20 = (bf16[1024,1024]{1,0:T(8,128)(2,1)}, bf16[1024,1024]{1,0:T(8,128)(2,1)}, u32[]{:S(2)}, u32[]{:S(2)}) collective-permute-start(bf16[1024,1024]{1,0:T(8,128)(2,1)} %get-tuple-element.100), channel_id=1, source_target_pairs={{0,1},{1,0},{2,3},{3,2},{4,5},{5,4},{6,7},{7,6},{8,9},{9,8},{10,11... | collective-permute-start | bytes 6291464 | tf_op jit(solution)/shard_map/ppermute | solution.py:34
  195.7 13.9 %collective-permute-start.17 = (bf16[256,512]{1,0:T(8,128)(2,1)}, bf16[256,512]{1,0:T(8,128)(2,1)S(1)}, u32[]{:S(2)}, u32[]{:S(2)}) collective-permute-start(bf16[256,512]{1,0:T(8,128)(2,1)} %fusion.19), channel_id=1, source_target_pairs={{0,4},{4,0},{8,12},{12,8},{16,20},{20,16},{24,28},{28,24},{1,5},{5... | collective-permute-start | bytes 786440 | tf_op jit(solution)/shard_map/ppermute | solution.py:34
  198.1 12.4 %collective-permute-start.19 = (bf16[256,512]{1,0:T(8,128)(2,1)}, bf16[256,512]{1,0:T(8,128)(2,1)}, u32[]{:S(2)}, u32[]{:S(2)}) collective-permute-start(bf16[256,512]{1,0:T(8,128)(2,1)} %fusion.20), channel_id=1, source_target_pairs={{0,2},{1,3},{2,0},{3,1},{4,6},{5,7},{6,4},{7,5},{8,10},{9,11},{10,... | collective-permute-start | bytes 786440 | tf_op jit(solution)/shard_map/ppermute | solution.py:34
  209.0 13.8 %collective-permute-start.21 = (bf16[2,256,512]{2,1,0:T(8,128)(2,1)}, bf16[2,256,512]{2,1,0:T(8,128)(2,1)}, u32[]{:S(2)}, u32[]{:S(2)}) collective-permute-start(bf16[2,256,512]{2,1,0:T(8,128)(2,1)} %bitcast.217), channel_id=1, source_target_pairs={{0,2},{1,3},{2,0},{3,1},{4,6},{5,7},{6,4},{7,5},{8,10},{9,11},{10,... | collective-permute-start | bytes 1572872 | tf_op jit(solution)/shard_map/ppermute | solution.py:34
  214.0 15.2 %collective-permute-start.23 = (bf16[2,256,512]{2,1,0:T(8,128)(2,1)}, bf16[2,256,512]{2,1,0:T(8,128)(2,1)}, u32[]{:S(2)}, u32[]{:S(2)}) collective-permute-start(bf16[2,256,512]{2,1,0:T(8,128)(2,1)} %get-tuple-element.104), channel_id=1, source_target_pairs={{0,4},{4,0},{8,12},{12,8},{16,20},{20,16},{24,28},{28,24},{1,5},{5... | collective-permute-start | bytes 1572872 | tf_op jit(solution)/shard_map/ppermute | solution.py:34
  224.4 32.3 %collective-permute-start.22 = (bf16[256,512]{1,0:T(8,128)(2,1)S(1)}, bf16[256,512]{1,0:T(8,128)(2,1)}, u32[]{:S(2)}, u32[]{:S(2)}) collective-permute-start(bf16[256,512]{1,0:T(8,128)(2,1)S(1)} %fusion.21), channel_id=1, source_target_pairs={{0,4},{4,0},{8,12},{12,8},{16,20},{20,16},{24,28},{28,24},{1,5},{5... | collective-permute-start | bytes 786440 | tf_op jit(solution)/shard_map/ppermute | solution.py:34
  229.9 5.6 %collective-permute-start.25 = (f32[4,4,384]{2,1,0:T(4,128)S(1)}, f32[4,4,384]{2,1,0:T(4,128)S(1)}, u32[]{:S(2)}, u32[]{:S(2)}) collective-permute-start(f32[4,4,384]{2,1,0:T(4,128)S(1)} %bitcast.211), channel_id=1, source_target_pairs={{0,4},{4,0},{8,12},{12,8},{16,20},{20,16},{24,28},{28,24},{1,5},{5... | collective-permute-start | bytes 73736 | tf_op jit(solution)/shard_map/ppermute | solution.py:34
  230.7 19.8 %collective-permute-start.31 = (bf16[32,1024]{1,0:T(8,128)(2,1)S(1)}, bf16[32,1024]{1,0:T(8,128)(2,1)S(1)}, u32[]{:S(2)}, u32[]{:S(2)}) collective-permute-start(bf16[32,1024]{1,0:T(8,128)(2,1)S(1)} %bitcast.207), channel_id=1, source_target_pairs={{0,0},{1,4},{2,8},{3,12},{4,16},{5,20},{6,24},{7,28},{8,1},{9,5},{... | collective-permute-start | bytes 196616 | tf_op jit(solution)/shard_map/ppermute | solution.py:78
  239.5 11.7 %collective-permute-start.30 = (bf16[4,32,896]{2,1,0:T(8,128)(2,1)S(1)}, bf16[4,32,896]{2,1,0:T(8,128)(2,1)S(1)}, u32[]{:S(2)}, u32[]{:S(2)}) collective-permute-start(bf16[4,32,896]{2,1,0:T(8,128)(2,1)S(1)} %dynamic-slice_bitcast_fusion), channel_id=1, source_target_pairs={{0,4},{4,0},{8,12},{12,8},{16,20},{20,16},{24,28},{28,24},{1,5},{5... | collective-permute-start | bytes 688136 | tf_op jit(solution)/shard_map/ppermute | solution.py:34
  240.6 4.6 %collective-permute-start.28 = (f32[2,384]{1,0:T(2,128)S(1)}, f32[2,384]{1,0:T(2,128)S(1)}, u32[]{:S(2)}, u32[]{:S(2)}) collective-permute-start(f32[2,384]{1,0:T(2,128)S(1)} %slice_bitcast_fusion.7), channel_id=1, source_target_pairs={{0,16},{4,20},{8,24},{12,28},{16,0},{20,4},{24,8},{28,12},{1,17},{... | collective-permute-start | bytes 9224 | tf_op jit(solution)/shard_map/ppermute | solution.py:34
  247.1 10.8 %collective-permute-start.24 = (bf16[256,512]{1,0:T(8,128)(2,1)}, bf16[256,512]{1,0:T(8,128)(2,1)}, u32[]{:S(2)}, u32[]{:S(2)}) collective-permute-start(bf16[256,512]{1,0:T(8,128)(2,1)} %fusion.22), channel_id=1, source_target_pairs={{0,2},{1,3},{2,0},{3,1},{4,6},{5,7},{6,4},{7,5},{8,10},{9,11},{10,... | collective-permute-start | bytes 786440 | tf_op jit(solution)/shard_map/ppermute | solution.py:34
  252.1 11.2 %all-to-all-start.1 = ((bf16[4,2,32,896]{3,2,1,0:T(8,128)(2,1)}), bf16[4,2,32,896]{3,2,1,0:T(8,128)(2,1)}, u32[]{:S(2)}, u32[]{:S(2)}) async-start(bf16[4,2,32,896]{3,2,1,0:T(8,128)(2,1)} %copy.91), calls=%async_computation.3 | async-start | bytes 917504 | tf_op jit(solution)/shard_map/all_to_all | solution.py:67
  (41 other events, 289.4 us)
Sparse Core Ops, SparseCore 0:
  9.6 30.2 all-gather.6
  51.4 27.8 all-gather.8
  94.8 26.0 all-gather.10
  123.0 43.3 reduce-scatter.2
  176.8 28.0 reduce-scatter.4

commit v3 on v2

--- a/solution.py
+++ b/solution.py
@@ -105,27 +105,32 @@
 
     def gather_all(self, vector):
         table = vector[None]
-        for axis, size in (("seq", self.seq), ("ctx", self.ctx)):
-            bit = 1
-            while bit < size:
-                table = jnp.concatenate([table, swap(table, axis, size, bit)], 0)
-                bit *= 2
+        table = [table] + [swap(table, "seq", self.seq, k) for k in range(2, self.seq, 2)]
+        table = jnp.concatenate(table, 0)
+        table = jnp.stack([table, swap(table, "seq", self.seq, 1)], 1).reshape(self.seq, -1)
+        bit = 1
+        while bit < self.ctx:
+            table = jnp.concatenate([table, swap(table, "ctx", self.ctx, bit)], 0)
+            bit *= 2
         return table[self.spread()]
 
-    def scatter_all(self, table):
+    def scatter_all_begin(self, table):
         seq_bits = jnp.arange(self.seq) ^ lax.axis_index("seq")
         ctx_bits = jnp.arange(self.ctx) ^ self.spot
         place = (seq_bits[None, :] * self.ctx + ctx_bits[:, None]).reshape(-1)
-        table = table[place].reshape(self.ctx, self.seq // 2, 2, -1)
-        table = table[:, :, 0] + swap(table[:, :, 1], "seq", self.seq, 1)
-        bit = self.ctx // 2
+        table = table[place].reshape(self.ctx // 2, 2, self.seq, -1)
+        table = table[:, 0] + swap(table[:, 1], "ctx", self.ctx, 1)
+        table = table.reshape(self.ctx // 2, self.seq // 2, 2, -1)
+        total = table[:, 0]
+        for k in range(1, self.seq // 2):
+            total = total + swap(table[:, k], "seq", self.seq, 2 * k)
+        return total
+
+    def scatter_all_end(self, table):
+        table = table[:, 0] + swap(table[:, 1], "seq", self.seq, 1)
+        bit = self.ctx // 4
         while bit:
-            table = table[:bit] + swap(table[bit:], "ctx", self.ctx, bit)
-            bit //= 2
-        table = table[0]
-        bit = self.seq // 4
-        while bit:
-            table = table[:bit] + swap(table[bit:], "seq", self.seq, 2 * bit)
+            table = table[:bit] + swap(table[bit:], "ctx", self.ctx, 2 * bit)
             bit //= 2
         return table[0]
 
@@ -142,28 +147,28 @@
         table = table.reshape(self.ctx // 2, self.near, rows, width)
         return [table[0], table[1:].astype(BF)]
 
-    def scatter_team(self, blocks):
-        def over_ctx(kept, sent):
-            came = [swap(sent[k - 1], "ctx", self.ctx, 2 * k) for k in range(1, self.ctx // 2)]
-            for v in came:
-                kept = kept + v.astype(F32)
-            return kept, came
-
-        def over_seq(kept, sent):
-            came = swap(sent, "seq", self.seq, 1)
-            return kept + came.astype(F32), [came]
-
-        kept, first = over_ctx(*blocks[:2])
-        if self.near == 2:
-            kept, done = over_seq(kept[0], kept[1].astype(BF))
-        else:
-            kept = kept[0]
-        if len(blocks) == 2:
-            return kept, first, first
-        other, second = over_seq(*blocks[2:])
-        other, last = over_ctx(other[0], other[1:].astype(BF))
-        done = done + last
-        return jnp.concatenate([kept, other], 1), first + second, done
+    def first_steps(self, blocks):
+        came = [[swap(blocks[1][k - 1], "ctx", self.ctx, 2 * k) for k in range(1, self.ctx // 2)]]
+        if len(blocks) == 4:
+            came.append([swap(blocks[3], "seq", self.seq, 1)])
+        return came
+
+    def second_steps(self, blocks, came):
+        result = []
+        for n, values in enumerate(came):
+            total = blocks[2 * n]
+            for v in values:
+                total = total + v.astype(F32)
+            result.append((total[0], total[1].astype(BF)) if self.near == 2 else (total[0], None))
+        return result
+
+    def last_steps(self, steps):
+        if self.near == 1:
+            return steps[0][0]
+        parts = [steps[0][0] + swap(steps[0][1], "seq", self.seq, 1).astype(F32)]
+        if len(steps) == 2:
+            parts.append(steps[1][0] + swap(steps[1][1], "ctx", self.ctx, 2).astype(F32))
+        return jnp.concatenate(parts, 1)
 
 
 def after(value, *first):
@@ -213,15 +218,21 @@
             ref[...] = jnp.zeros_like(ref)
 
     gain = gain_ref[...]
-    unit, value = normed(load(x_ref), gain, shift_ref[...])
+    source, grad = load(x_ref), load(g_ref)
+    half = source.shape[0] // 2
+    parts = [slice(0, half), slice(half, 2 * half)]
+    stack = lambda values: jnp.concatenate(values, 0)
+    units, values = zip(*[normed(source[p], gain, shift_ref[...]) for p in parts])
+    uppers = [dot(value, up_ref[...]) + bias_ref[...] for value in values]
+    actives, grads = [], []
+    for p, upper in zip(parts, uppers):
+        grad_active = contract_cols(grad[p], down_ref[...])
+        cdf = 0.5 * (1.0 + lax.erf(upper * math.sqrt(0.5)))
+        density = jnp.exp(-0.5 * upper * upper) * (1.0 / math.sqrt(2.0 * math.pi))
+        actives.append((upper * cdf).astype(BF))
+        grads.append((grad_active * (cdf + upper * density)).astype(BF))
+    unit, value, active, grad_upper = [stack(v) for v in (units, values, actives, grads)]
     one_ref[...] = (unit * gain_one_ref[...] + shift_one_ref[...]).astype(BF)
-    grad = load(g_ref)
-    upper = dot(value, up_ref[...]) + bias_ref[...]
-    grad_active = contract_cols(grad, down_ref[...])
-    cdf = 0.5 * (1.0 + lax.erf(upper * math.sqrt(0.5)))
-    density = jnp.exp(-0.5 * upper * upper) * (1.0 / math.sqrt(2.0 * math.pi))
-    active = (upper * cdf).astype(BF)
-    grad_upper = (grad_active * (cdf + upper * density)).astype(BF)
     store(hid_ref, dot(active, down_ref[...]).astype(BF))
     down_s[...] += contract_rows(active, grad)
     up_s[...] += contract_rows(value, grad_upper)
@@ -356,6 +367,22 @@
     )(even, got)
 
 
+def unpack_kernel(far, both_ref, qkv_ref, up_ref):
+    ctx, near = both_ref.shape[:2]
+    team = ctx * near
+    part, piece = qkv_ref.shape[1] // (3 * team), up_ref.shape[1] // (far * team)
+    for c in range(ctx):
+        for x in range(near):
+            value = both_ref[c, x].astype(F32)
+            for n in range(3):
+                at = (n * team + x * ctx + c) * part
+                qkv_ref[:, at : at + part] = value[:, n * part : (n + 1) * part]
+            for z in range(far):
+                at = (z * team + x * ctx + c) * piece
+                low = 3 * part + z * piece
+                up_ref[:, at : at + piece] = value[:, low : low + piece]
+
+
 def first_half():
     return pl.program_id(0) < pl.num_programs(0) // 2
 
@@ -374,8 +401,8 @@
         pair[1][...] = value
 
 
-def by_tokens(kernel, tokens, pairs, streamed, fixed, pairs_out, streamed_out, fixed_out, scratch, name):
-    block = math.gcd(tokens // 2, 512)
+def by_tokens(kernel, tokens, pairs, streamed, fixed, pairs_out, streamed_out, fixed_out, scratch, name, size=512):
+    block = math.gcd(tokens // 2, size)
     steps = tokens // block
     stream = lambda n: pl.BlockSpec((block, n), lambda i: (i, 0))
     whole = lambda shape: pl.BlockSpec(shape, lambda i: (0, 0))
@@ -420,7 +447,7 @@
     heads, ctx, near,
     spot_ref, pack_ref, seg_col_ref, seg_row_ref,
     out_ref, back_ref,
-    q_s, k_s, v_s, g_s, dq_s, dk_s, dv_s,
+    q_s, k_s, v_s, g_s, kt_s, vt_s, dq_s, dk_s, dv_s,
 ):
     length = pack_ref.shape[0] // near
     width = out_ref.shape[1]
@@ -442,41 +469,79 @@
         return carry
 
     lax.fori_loop(0, ctx * near, prepare, 0)
-    dk_s[...] = jnp.zeros_like(dk_s)
-    dv_s[...] = jnp.zeros_like(dv_s)
-
     def one(h, start, size):
         at = pl.ds(start, block)
         query, grad = q_s[h, at, :], g_s[h, at, :]
         keys, values = k_s[h, 0:size, :], v_s[h, 0:size, :]
-        scores = contract_cols(query, keys)
-        row = start + lax.broadcasted_iota(jnp.int32, (block, size), 0)
-        col = lax.broadcasted_iota(jnp.int32, (block, size), 1)
+        scores = contract_cols(keys, query)
+        row = lax.broadcasted_iota(jnp.int32, (size, block), 0)
+        col = start + lax.broadcasted_iota(jnp.int32, (size, block), 1)
         x = h // heads
-        seg_col = seg_col_ref[pl.ds(x * length + start, block), :]
-        allowed = (seg_col == seg_row_ref[pl.ds(x, 1), 0:size]) & (row >= col)
-        scores = jnp.where(allowed, scores, NEG)
-        raw = jnp.exp(scores - jnp.max(scores, -1, keepdims=True))
-        prob = raw * (1.0 / jnp.sum(raw, -1, keepdims=True))
+        seg_col = seg_col_ref[pl.ds(x * length, size), :]
+        seg_row = seg_row_ref[pl.ds(x, 1), at]
+        scores = jnp.where((seg_col == seg_row) & (row <= col), scores, NEG)
+        raw = jnp.exp(scores - jnp.max(scores, 0, keepdims=True))
+        prob = raw * (1.0 / jnp.sum(raw, 0, keepdims=True))
         prob_low = prob.astype(BF)
-        grad_prob = contract_cols(grad, values)
-        delta = jnp.sum(prob * grad_prob, -1, keepdims=True)
+        grad_prob = contract_cols(values, grad)
+        delta = jnp.sum(prob * grad_prob, 0, keepdims=True)
         grad_score = (prob * (grad_prob - delta)).astype(BF)
-        dv_s[h, 0:size, :] += contract_rows(prob_low, grad)
-        dk_s[h, 0:size, :] += contract_rows(grad_score, query)
-        dq_s[h, at, :] = dot(grad_score, keys)
-        q_s[h, at, :] = dot(prob_low, values).astype(BF)
+        dv_s[h, 0:size, :] += dot(prob_low, grad)
+        dk_s[h, 0:size, :] += dot(grad_score, query)
+        dq_s[h, at, :] = dot(kt_s[h, :, 0:size], grad_score).T
+        q_s[h, at, :] = dot(vt_s[h, :, 0:size], prob_low).T.astype(BF)
+
+    def flip(h, carry):
+        kt_s[h] = k_s[h].T
+        vt_s[h] = v_s[h].T
+        return carry
+
+    lax.fori_loop(0, near * heads, flip, 0)
 
     count = length // block
     if count <= 4:
 
         def each(h, carry):
+            x = h // heads
+            ats = [pl.ds(i * block, block) for i in range(count)]
+            queries, grads = [q_s[h, at, :] for at in ats], [g_s[h, at, :] for at in ats]
+            keys, values = k_s[h], v_s[h]
+            seg_col = seg_col_ref[pl.ds(pl.multiple_of(x * length, block), length), :]
+            seg_row = seg_row_ref[pl.ds(x, 1), :]
+            row = lax.broadcasted_iota(jnp.int32, (block, block), 0)
+            col = lax.broadcasted_iota(jnp.int32, (block, block), 1)
+            scores = [
+                contract_cols(keys[: (i + 1) * block], query) for i, query in enumerate(queries)
+            ]
+            grad_probs = [
+                contract_cols(values[: (i + 1) * block], grad) for i, grad in enumerate(grads)
+            ]
+            probs, grad_scores = [], []
             for i in range(count):
-                one(h, i * block, (i + 1) * block)
+                size = (i + 1) * block
+                same = seg_col[:size] == seg_row[:, i * block : size]
+                score = jnp.where(same, scores[i], NEG)
+                last = jnp.where(row <= col, score[i * block :], NEG)
+                score = jnp.concatenate([score[: i * block], last], 0) if i else last
+                raw = jnp.exp(score - jnp.max(score, 0, keepdims=True))
+                prob = raw * (1.0 / jnp.sum(raw, 0, keepdims=True))
+                delta = jnp.sum(prob * grad_probs[i], 0, keepdims=True)
+                probs.append(prob.astype(BF))
+                grad_scores.append((prob * (grad_probs[i] - delta)).astype(BF))
+            for i, at in enumerate(ats):
+                size = (i + 1) * block
+                dq_s[h, at, :] = dot(kt_s[h, :, 0:size], grad_scores[i]).T
+                q_s[h, at, :] = dot(vt_s[h, :, 0:size], probs[i]).T.astype(BF)
+            for j, at in enumerate(ats):
+                low = slice(j * block, (j + 1) * block)
+                dv_s[h, at, :] = sum(dot(probs[i][low], grads[i]) for i in range(j, count))
+                dk_s[h, at, :] = sum(dot(grad_scores[i][low], queries[i]) for i in range(j, count))
             return carry
 
         lax.fori_loop(0, near * heads, each, 0)
     else:
+        dk_s[...] = jnp.zeros_like(dk_s)
+        dv_s[...] = jnp.zeros_like(dv_s)
 
         def each(step, carry):
             one(step // count, pl.multiple_of(step % count * block, block), length)
@@ -515,7 +580,9 @@
         ),
         in_specs=[pl.BlockSpec(memory_space=pltpu.SMEM)] + [whole() for _ in range(3)],
         out_specs=(whole(), whole()),
-        scratch_shapes=[pltpu.VMEM(shape, BF)] * 4 + [pltpu.VMEM(shape, F32)] * 3,
+        scratch_shapes=[pltpu.VMEM(shape, BF)] * 4
+        + [pltpu.VMEM((near * heads, HD, length), BF)] * 2
+        + [pltpu.VMEM(shape, F32)] * 3,
         compiler_params=pltpu.CompilerParams(vmem_limit_bytes=60 * 1024 * 1024),
         cost_estimate=pl.CostEstimate(flops=1024, bytes_accessed=1024, transcendentals=0),
         name="attend",
@@ -566,7 +633,6 @@
     )
     payload = lay.exchange_near(payload)
     source_steps = lay.beside(after(source_own, payload)), lay.across(source_own)
-    across = lay.across(cotangent_own)
     small = [ln1_gain, ln1_bias, ln2_gain, ln2_bias, out_bias, down_bias, qkv_bias, up_bias]
     small = [v.astype(F32) for v in small + [segments[0], positions[0]]]
     sizes = [v.shape[0] for v in small]
@@ -597,9 +663,10 @@
     cos_wide = jnp.cos(theta)
     sin_wide = jnp.where(lane < ROT // 2, -1.0, 1.0)[None, :] * jnp.sin(theta)
 
-    payload = after(payload, vectors, source_steps[0], *source_steps[1], *across)
+    payload = after(payload, vectors, source_steps[0], *source_steps[1])
     payload = lax.all_to_all(payload, "ctx", 0, 0, tiled=True)
-    cotangent_steps = lay.beside(after(cotangent_own, payload)), across
+    late = after(cotangent_own, payload)
+    cotangent_steps = lay.beside(late), lay.across(late)
     payload = payload.transpose(1, 0, 2, 3).reshape(depth, -1)
     w_up = lay.gather_far(payload[:, 3 * part :]).reshape(width, share)
 
@@ -650,10 +717,11 @@
         [jax.ShapeDtypeStruct((width, 3 * part), BF), jax.ShapeDtypeStruct((part, width), BF)],
         [],
         "heads",
+        1024,
     )
     attended, back = attend(lay.spot, pack, seg, heads, ctx)
     (hid,) = by_tokens(
-        hidden_kernel, count_all, [hid], [attended], [w_out], [width], [], [], [], "hidden"
+        hidden_kernel, count_all, [hid], [attended], [w_out], [width], [], [], [], "hidden", 1024
     )
     hid_got = swap(hid[1], "ctx", ctx, 1)
     linear, last, grad_qkv_b, *out_terms = by_tokens(
@@ -671,6 +739,7 @@
         + [jax.ShapeDtypeStruct((part, width), BF)] * (not packed),
         [pltpu.VMEM((width, 3 * part), F32), pltpu.VMEM((part, width), F32)],
         "weights",
+        1024,
     )
     last = last.reshape(far, depth, -1)
     if not packed:
@@ -691,15 +760,9 @@
         [],
         "flow",
     )
-    hidden_sum, hid_came, _ = lay.scatter_team(hid_first)
-    flow = after(tuple(flow), *hid_came)
-    flow_first = lay.pair_blocks(after(flow[0], last_sum), swap(flow[1], "ctx", ctx, 1))
-    result = (source_own.astype(F32) + hidden_sum + (b_out + b_down)).astype(BF)[None]
-
-    flow, flow_came, flow_done = lay.scatter_team(flow_first)
-    last = after(last_sum, *flow_came)
-    terms_sum = after(terms_sum, *flow_came)
-
+    hid_came = after(lay.first_steps(hid_first), gain_one_sum)
+    flow = after(tuple(flow), hid_came)
+    flow_got = swap(flow[1], "ctx", ctx, 1)
     cotangent_full = cotangent_own.astype(F32)
     grad_bias = jnp.sum(cotangent_full, 0)
     mine = (jnp.arange(team) == lay.index)[None, :, None]
@@ -707,31 +770,56 @@
     grad_up_b = jnp.where(mine, grad_up_b.reshape(far, 1, piece), 0.0)
     table = [gain_one_sum, shift_one_sum, gain_two_sum, shift_two_sum, grad_bias]
     table = [v.reshape(seq * ctx, -1) for v in table + [grad_qkv_b, grad_up_b]]
-    sums = lay.scatter_all(after(jnp.concatenate(table, 1), *flow_came))
+    table_all = lay.scatter_all_begin(jnp.concatenate(table, 1))
+
+    hid_second = lay.second_steps(hid_first, hid_came)
+    hid_kept = [v for pair in hid_second for v in pair if v is not None]
+    flow_first = lay.pair_blocks(after(flow[0], table_all, last_sum, *hid_kept), flow_got)
+    flow_came = lay.first_steps(flow_first)
+    flow_second = lay.second_steps(flow_first, flow_came)
+    hidden_sum = lay.last_steps(after(hid_second, flow_came))
+    result = (source_own.astype(F32) + hidden_sum + (b_out + b_down)).astype(BF)[None]
+    last_sum, terms_sum, table_all = after((last_sum, terms_sum, table_all), flow_second)
+    flow = lay.last_steps(flow_second)
+
+    sums = lay.scatter_all_end(table_all)
     sizes = [v.shape[1] for v in table]
     sums = [sums[sum(sizes[:k]) : sum(sizes[: k + 1])] for k in range(len(sizes))]
 
+    last = last_sum
+    both = jnp.concatenate([last[:, : 3 * part], terms_sum[:, :share]], 1)
+    both = lay.exchange(both.reshape(near, ctx, rows, -1))
     grad_down_w = terms_sum[:, share:].reshape(-1, piece, share)
     grad_down_w = grad_down_w.transpose(1, 0, 2).reshape(piece, width).astype(F32)
-    both = jnp.concatenate([last[:, : 3 * part], terms_sum[:, :share]], 1)
-    both = lay.exchange(both.reshape(near, ctx, rows, -1))
-    grad_up_w = (
-        both[..., 3 * part :]
-        .reshape(ctx, near, rows, far, piece)
-        .transpose(2, 3, 1, 0, 4)
-        .reshape(rows, hidden)
-        .astype(F32)
-    )
+    if part % 128 == 0 and piece % 128 == 0:
+        grad_qkv_w, grad_up_w = pl.pallas_call(
+            partial(unpack_kernel, far),
+            out_shape=[
+                jax.ShapeDtypeStruct((rows, 3 * width), F32),
+                jax.ShapeDtypeStruct((rows, hidden), F32),
+            ],
+            in_specs=[pl.BlockSpec(memory_space=pltpu.VMEM)],
+            out_specs=[pl.BlockSpec(memory_space=pltpu.VMEM)] * 2,
+            cost_estimate=pl.CostEstimate(flops=1024, bytes_accessed=1024, transcendentals=0),
+            name="unpack",
+        )(both)
+    else:
+        grad_up_w = (
+            both[..., 3 * part :]
+            .reshape(ctx, near, rows, far, piece)
+            .transpose(2, 3, 1, 0, 4)
+            .reshape(rows, hidden)
+            .astype(F32)
+        )
+        grad_qkv_w = (
+            both[..., : 3 * part]
+            .reshape(ctx, near, rows, 3, part)
+            .transpose(2, 3, 1, 0, 4)
+            .reshape(rows, 3 * width)
+            .astype(F32)
+        )
     out_sum = last[:, 3 * part :].reshape(cuts, out_rows, width // cuts).transpose(1, 0, 2)
     grad_out_w = lay.own_heads(out_sum.reshape(out_rows, width), back=True).astype(F32)
-    grad_qkv_w = (
-        both[..., : 3 * part]
-        .reshape(ctx, near, rows, 3, part)
-        .transpose(2, 3, 1, 0, 4)
-        .reshape(rows, 3 * width)
-        .astype(F32)
-    )
-
     wide = source_own.astype(F32)
     centred = wide - jnp.mean(wide, -1, keepdims=True)
     inverse = lax.rsqrt(jnp.mean(centred * centred, -1, keepdims=True) + EPS)

time: 279 us -> 264 us (0.946)
  waiting for transfers between devices: 77 us -> 62.9 us
  starting transfers between devices: 35.5 us -> 43.8 us
  other arithmetic: 31 us -> 26.3 us
  Pallas kernels: 92.3 us -> 89 us
    ppermute x30 -> x32, starting transfers between devices: 18.1 us -> 24 us  [swap(): return lax.ppermute(value, axis, [(i, i ^ bits) for i in range(size)])]
    ppermute x30 -> x32, waiting for transfers between devices: 56.8 us -> 51.1 us  [swap(): return lax.ppermute(value, axis, [(i, i ^ bits) for i in range(size)])]
    reduce_scatter x2, waiting for transfers between devices: 5.16 us -> 0.02 us  [scatter_far(): lax.psum_scatter(terms, 'seq', scatter_dimension=0, tiled=True, axis_inde...]
    pallas_call x1, Pallas kernels: 22.3 us -> 17.9 us  [attend(): pl.pallas_call(partial(attend_kernel, heads, ctx, near), out_shape=(jax.S...]
    add x10 -> x9, other arithmetic: 5.87 us -> 4.41 us  [the longest x4 4.32 us: second_steps(): total = total + v.astype(F32)]
    unnamed x76 -> x67, local copies, waits for them, and re-layouts: 5.11 us -> 5.87 us
  transfers between devices with their start and end apart: 39 -> 41, of which waited for: 21 -> 18; matrix products, arithmetic and copies ran while one was open for 18% -> 18% of each run, Pallas kernels for 34% -> 32%
where the time goes in v3:
time: 264 us; the launch traced here: 262 us
  Pallas kernels  89 us (34%)
  waiting for transfers between devices  62.9 us (24%)
  starting transfers between devices  43.8 us (17%)
  other arithmetic  26.3 us (10%)
  local copies, waits for them, and re-layouts  25.1 us (10%)
  between operations  14.7 us (6%)
    pallas_call x5, Pallas kernels, by_tokens(): pl.pallas_call(body, grid=(steps,), in_specs=[spec for pair in pairs for...  61.1 us
    ppermute x32, waiting for transfers between devices, swap(): return lax.ppermute(value, axis, [(i, i ^ bits) for i in range(size)])  51.1 us
    ppermute x32, starting transfers between devices, swap(): return lax.ppermute(value, axis, [(i, i ^ bits) for i in range(size)])  24 us
    pallas_call x1, Pallas kernels, attend(): pl.pallas_call(partial(attend_kernel, heads, ctx, near), out_shape=(jax.S...  17.9 us
    ppermute x2, starting transfers between devices, own_heads(): return lax.ppermute(value, ('seq', 'ctx'), pairs)  9.37 us
    pallas_call x2, Pallas kernels, pair_sums(): pl.pallas_call(partial(pair_kernel, rows), out_shape=[jax.ShapeDtypeStruc...  8 us
    all_to_all x1, waiting for transfers between devices, local(): payload = lax.all_to_all(payload, 'ctx', 0, 0, tiled=True)  6.33 us
    all_to_all x1, starting transfers between devices, exchange(): return lax.all_to_all(self.exchange_near(pieces), 'ctx', 0, 0, tiled=True)  6.06 us
  transfers between devices with their start and end apart: 41, of which 18 were waited for; matrix products, arithmetic and copies ran while one was open for 18% of the time, Pallas kernels for 32%

profile of v3, /device:TPU:6, one launch (start us, length us, event | category | flops | bytes accessed | tf_op | source)
XLA Modules:
  0.0 261.7 jit_solution(6920408542644974460)
XLA Ops:
  11.1 6.3 %collective-permute-done = bf16[4,32,896]{2,1,0:T(8,128)(2,1)S(1)} collective-permute-done((bf16[4,32,896]{2,1,0:T(8,128)(2,1)S(1)}, bf16[4,32,896]{2,1,0:T(8,128)(2,1)S(1)}, u32[]{:S(2)}, u32[]{:S(2)}) %collective-permute-start) | collective-permute-done | bytes 229408 | tf_op jit(solution)/shard_map/ppermute | solution.py:34
  17.6 3.7 %collective-permute-start.6 = (f32[1,928]{1,0:T(1,128)S(1)}, f32[1,928]{1,0:T(1,128)S(1)}, u32[]{:S(2)}, u32[]{:S(2)}) collective-permute-start(f32[1,928]{1,0:T(1,128)S(1)} %bitcast.208), channel_id=1, source_target_pairs={{0,24},{4,28},{8,16},{12,20},{16,8},{20,12},{24,0},{28,4},{1,25},{... | collective-permute-start | bytes 11144 | tf_op jit(solution)/shard_map/ppermute | solution.py:34
  23.1 2.8 %collective-permute-done.5 = f32[1,928]{1,0:T(1,128)S(1)} collective-permute-done((f32[1,928]{1,0:T(1,128)S(1)}, f32[1,928]{1,0:T(1,128)S(1)}, u32[]{:S(2)}, u32[]{:S(2)}) %collective-permute-start.5) | collective-permute-done | bytes 3744 | tf_op jit(solution)/shard_map/ppermute | solution.py:34
  28.1 1.9 collective-permute-done.7
  31.9 3.8 %collective-permute-done.9 = f32[16,928]{1,0:T(8,128)S(1)} collective-permute-done((f32[16,928]{1,0:T(8,128)S(1)}, f32[16,928]{1,0:T(8,128)S(1)}, u32[]{:S(2)}, u32[]{:S(2)}) %collective-permute-start.9) | collective-permute-done | bytes 59424 | tf_op jit(solution)/shard_map/ppermute | solution.py:34
  36.4 1.7 collective-permute-done.1
  39.0 4.0 %all-to-all-start = ((bf16[4,2,32,896]{3,2,1,0:T(8,128)(2,1)}), bf16[4,2,32,896]{3,2,1,0:T(8,128)(2,1)S(1)}, u32[]{:S(2)}, u32[]{:S(2)}) async-start(bf16[4,2,32,896]{3,2,1,0:T(8,128)(2,1)} %copy.60), calls=%async_computation | async-start | bytes 917504 | tf_op jit(solution)/shard_map/all_to_all | solution.py:667
  43.1 6.3 %all-to-all-done = bf16[4,2,32,896]{3,2,1,0:T(8,128)(2,1)S(1)} async-done(((bf16[4,2,32,896]{3,2,1,0:T(8,128)(2,1)}), bf16[4,2,32,896]{3,2,1,0:T(8,128)(2,1)S(1)}, u32[]{:S(2)}, u32[]{:S(2)}) %all-to-all-start) | async-done | bytes 458784 | tf_op jit(solution)/shard_map/all_to_all | solution.py:667
  49.4 1.7 collective-permute-start.12
  59.1 5.3 %collective-permute-done.12 = bf16[256,1024]{1,0:T(8,128)(2,1)} collective-permute-done((bf16[256,1024]{1,0:T(8,128)(2,1)S(1)}, bf16[256,1024]{1,0:T(8,128)(2,1)}, u32[]{:S(2)}, u32[]{:S(2)}) %collective-permute-start.12) | collective-permute-done | bytes 524320 | tf_op jit(solution)/shard_map/ppermute | solution.py:34
  65.8 5.5 %fusion.12 = (f32[2048,128]{1,0:T(8,128)}, f32[2048,128]{1,0:T(8,128)}) fusion(f32[128]{0:T(128)S(1)} %get-tuple-element.165, f32[128]{0:T(128)S(1)} %get-tuple-element.166, f32[2048]{0:T(1024)S(1)} %bitcast.205), kind=kLoop, calls=%fused_computation.24 | loop fusion | flops 524288 | bytes 2106368 | tf_op jit(solution)/shard_map/mul | solution.py:664
  71.3 3.1 %collective-permute-done.3 = bf16[256,1024]{1,0:T(8,128)(2,1)S(1)} collective-permute-done((bf16[256,1024]{1,0:T(8,128)(2,1)S(1)}, bf16[256,1024]{1,0:T(8,128)(2,1)S(1)}, u32[]{:S(2)}, u32[]{:S(2)}) %collective-permute-start.3) | collective-permute-done | bytes 524320 | tf_op jit(solution)/shard_map/ppermute | solution.py:34
  75.9 6.2 %collective-permute-done.13 = bf16[256,1024]{1,0:T(8,128)(2,1)} collective-permute-done((bf16[256,1024]{1,0:T(8,128)(2,1)}, bf16[256,1024]{1,0:T(8,128)(2,1)}, u32[]{:S(2)}, u32[]{:S(2)}) %collective-permute-start.13) | collective-permute-done | bytes 524320 | tf_op jit(solution)/shard_map/ppermute | solution.py:34
  83.7 5.3 %collective-permute-start.15 = (bf16[32,1024]{1,0:T(8,128)(2,1)S(1)}, bf16[32,1024]{1,0:T(8,128)(2,1)S(1)}, u32[]{:S(2)}, u32[]{:S(2)}) collective-permute-start(bf16[32,1024]{1,0:T(8,128)(2,1)S(1)} %copy-done.28), channel_id=1, source_target_pairs={{0,0},{4,1},{8,2},{12,3},{16,4},{20,5},{24,6},{28,7},{1,8},{5,9},{... | collective-permute-start | bytes 196616 | tf_op jit(solution)/shard_map/ppermute | solution.py:78
  90.0 3.5 %collective-permute-done.15 = bf16[32,1024]{1,0:T(8,128)(2,1)S(1)} collective-permute-done((bf16[32,1024]{1,0:T(8,128)(2,1)S(1)}, bf16[32,1024]{1,0:T(8,128)(2,1)S(1)}, u32[]{:S(2)}, u32[]{:S(2)}) %collective-permute-start.15) | collective-permute-done | bytes 65568 | tf_op jit(solution)/shard_map/ppermute | solution.py:78
  94.3 26.5 %feed_forward.1 = (bf16[1024,1024]{1,0:T(8,128)(2,1)}, bf16[1024,1024]{1,0:T(8,128)(2,1)}, bf16[1024,1024]{1,0:T(8,128)(2,1)}, bf16[1024,1024]{1,0:T(8,128)(2,1)...) custom-call(bf16[1024,1024]{1,0:T(8,128)(2,1)} %pad_maximum_fusion.r, ...), custom_call_target="tpu_custom_call" | custom-call | flops 1024 | bytes 1024 | tf_op jit(solution)/shard_map/feed_forward/pallas_call | solution.py:425
  123.8 8.3 %heads.1 = (bf16[2048,512]{1,0:T(8,128)(2,1)}, bf16[1024,384]{1,0:T(8,128)(2,1)}, bf16[128,1024]{1,0:T(8,128)(2,1)}) custom-call(bf16[1024,1024]{1,0:T(8,128)(2,1)} %copy-done, bf16[1024,1024]{1,0:T(8,128)(2,1)} %collective-permute-done.14.refs_3_.refs_1_, bf16[2048,1024]{1,0:T(8,128)(2,1)} %get-tuple-element.87.refs_2_, ...), custom_call_target="tpu_custom_call" | custom-call | flops 1024 | bytes 1024 | tf_op jit(solution)/shard_map/heads/pallas_call | solution.py:425
  132.1 17.9 %attend.1 = (bf16[2048,128]{1,0:T(8,128)(2,1)}, f32[2048,384]{1,0:T(8,128)}) custom-call(s32[1]{0:T(128)} %bitcast.19.spot_ref, bf16[2048,512]{1,0:T(8,128)(2,1)} %get-tuple-element.82.pack_ref, s32[2048,1]{1,0:T(8,128)} %bitcast.181, s32[2,1024]{1,0:T(2,128)} %get-tuple-element.156.seg_row_ref), custom_call_target="tpu_custom_call" | custom-call | flops 1024 | bytes 1024 | tf_op jit(solution)/shard_map/attend/pallas_call | solution.py:575
  150.0 6.2 %hidden.1 = (bf16[1024,1024]{1,0:T(8,128)(2,1)}, bf16[1024,1024]{1,0:T(8,128)(2,1)}) custom-call(bf16[1024,1024]{1,0:T(8,128)(2,1)} %get-tuple-element.77.refs_0_, bf16[1024,1024]{1,0:T(8,128)(2,1)} %get-tuple-element.78.refs_1_, bf16[2048,128]{1,0:T(8,128)(2,1)} %get-tuple-element.83.refs_2_.refs_3_, bf16[128,1024]{1,0:T(8,128)(2,1)} %get-tuple-element.84.refs_3_), custom_call_target="tpu_custom_call" | custom-call | flops 1024 | bytes 1024 | tf_op jit(solution)/shard_map/hidden/pallas_call | solution.py:425
  156.8 9.0 %weights.1 = (bf16[2048,384]{1,0:T(8,128)(2,1)}, bf16[1024,512]{1,0:T(8,128)(2,1)}, f32[1,384]{1,0:T(1,128)}) custom-call(bf16[1024,1024]{1,0:T(8,128)(2,1)} %copy-done, bf16[1024,1024]{1,0:T(8,128)(2,1)} %collective-permute-done.14.refs_3_.refs_1_, bf16[2048,1024]{1,0:T(8,128)(2,1)} %get-tuple-element.87.refs_2_, ...), custom_call_target="tpu_custom_call" | custom-call | flops 1024 | bytes 1024 | tf_op jit(solution)/shard_map/weights/pallas_call | solution.py:425
  167.2 4.0 %pair_sums.2 = (f32[2,256,512]{2,1,0:T(8,128)}, bf16[1,2,256,512]{3,2,1,0:T(8,128)(2,1)}, f32[2,256,512]{2,1,0:T(8,128)}, bf16[2,256,512]{2,1,0:T(8,128)(2,1)}) custom-call(bf16[1024,1024]{1,0:T(8,128)(2,1)} %get-tuple-element.90.even_ref, bf16[1024,1024]{1,0:T(8,128)(2,1)} %copy-done.3), custom_call_target="tpu_custom_call" | custom-call | flops 1024 | bytes 1024 | tf_op jit(solution)/shard_map/pair_sums/pallas_call | solution.py:354
  174.4 11.0 %flow.1 = (bf16[1024,1024]{1,0:T(8,128)(2,1)}, bf16[1024,1024]{1,0:T(8,128)(2,1)}, f32[1,1024]{1,0:T(1,128)}, f32[1,1024]{1,0:T(1,128)}) custom-call(bf16[1024,1024]{1,0:T(8,128)(2,1)} %pad_maximum_fusion.refs_0_, bf16[1024,1024]{1,0:T(8,128)(2,1)} %collective-permute-done.10.refs_1_, bf16[1024,1024]{1,0:T(8,128)(2,1)} %get-tuple-element.98.refs_2_, ...), custom_call_target="tpu_custom_call" | custom-call | flops 1024 | bytes 1024 | tf_op jit(solution)/shard_map/flow/pallas_call | solution.py:425
  195.7 4.0 %collective-permute-start.22 = (f32[2,2,384]{2,0,1:T(2,128)S(1)}, f32[2,2,384]{2,0,1:T(2,128)S(1)}, u32[]{:S(2)}, u32[]{:S(2)}) collective-permute-start(f32[2,2,384]{2,0,1:T(2,128)S(1)} %get-tuple-element.150), channel_id=1, source_target_pairs={{0,24},{4,28},{8,16},{12,20},{16,8},{20,12},{24,0},{28,4},{1,25},{... | collective-permute-start | bytes 18440 | tf_op jit(solution)/shard_map/ppermute | solution.py:34
  201.7 2.6 collective-permute-done.21
  204.3 4.0 %pair_sums.3 = (f32[2,256,512]{2,1,0:T(8,128)}, bf16[1,2,256,512]{3,2,1,0:T(8,128)(2,1)}, f32[2,256,512]{2,1,0:T(8,128)}, bf16[2,256,512]{2,1,0:T(8,128)(2,1)}) custom-call(bf16[1024,1024]{1,0:T(8,128)(2,1)} %get-tuple-element.115.even_ref, bf16[1024,1024]{1,0:T(8,128)(2,1)} %collective-permute-done.23.got_ref), custom_call_target="tpu_custom_call" | custom-call | flops 1024 | bytes 1024 | tf_op jit(solution)/shard_map/pair_sums/pallas_call | solution.py:354
  208.8 11.9 %collective-permute-done.24 = bf16[2,256,512]{2,1,0:T(8,128)(2,1)S(1)} collective-permute-done((bf16[2,256,512]{2,1,0:T(8,128)(2,1)}, bf16[2,256,512]{2,1,0:T(8,128)(2,1)S(1)}, u32[]{:S(2)}, u32[]{:S(2)}) %collective-permute-start.24) | collective-permute-done | bytes 524320 | tf_op jit(solution)/shard_map/ppermute | solution.py:34
  224.5 1.8 collective-permute-start.30
  226.3 4.0 %collective-permute-start.33 = (bf16[32,1024]{1,0:T(8,128)(2,1)S(1)}, bf16[32,1024]{1,0:T(8,128)(2,1)S(1)}, u32[]{:S(2)}, u32[]{:S(2)}) collective-permute-start(bf16[32,1024]{1,0:T(8,128)(2,1)S(1)} %bitcast.204), channel_id=1, source_target_pairs={{0,0},{1,4},{2,8},{3,12},{4,16},{5,20},{6,24},{7,28},{8,1},{9,5},{... | collective-permute-start | bytes 196616 | tf_op jit(solution)/shard_map/ppermute | solution.py:78
  235.8 1.7 collective-permute-start.27
  240.0 6.1 %all-to-all-start.1 = ((bf16[4,2,32,896]{3,2,1,0:T(8,128)(2,1)}), bf16[4,2,32,896]{3,2,1,0:T(8,128)(2,1)}, u32[]{:S(2)}, u32[]{:S(2)}) async-start(bf16[4,2,32,896]{3,2,1,0:T(8,128)(2,1)} %pad_maximum_fusion.4), calls=%async_computation.3 | async-start | bytes 917504 | tf_op jit(solution)/shard_map/all_to_all | solution.py:67
  249.9 1.5 fusion.11
  252.6 2.0 unpack.1
  (257 shorter events, 63.4 us)
Async XLA Ops:
  7.2 68.7 %all-gather.7.cloned.1.call-start = ((), (), s32[]{:S(2)}) async-start(), calls=%async_computation.6 | async-start | bytes 1310720 | tf_op jit(solution)/shard_map/all_gather | solution.py:50
  10.1 7.4 %collective-permute-start = (bf16[4,32,896]{2,1,0:T(8,128)(2,1)S(1)}, bf16[4,32,896]{2,1,0:T(8,128)(2,1)S(1)}, u32[]{:S(2)}, u32[]{:S(2)}) collective-permute-start(bf16[4,32,896]{2,1,0:T(8,128)(2,1)S(1)} %dynamic-slice_bitcast_fusion.1), channel_id=1, source_target_pairs={{0,4},{4,0},{8,12},{12,8},{16,20},{20,16},{24,28},{28,24},{1,5},{5... | collective-permute-start | bytes 688136 | tf_op jit(solution)/shard_map/ppermute | solution.py:34
  10.7 25.7 %collective-permute-start.2 = (bf16[256,1024]{1,0:T(8,128)(2,1)S(1)}, bf16[256,1024]{1,0:T(8,128)(2,1)S(1)}, u32[]{:S(2)}, u32[]{:S(2)}) collective-permute-start(bf16[256,1024]{1,0:T(8,128)(2,1)S(1)} %bitcast.173), channel_id=1, source_target_pairs={{0,2},{1,3},{2,0},{3,1},{4,6},{5,7},{6,4},{7,5},{8,10},{9,11},{10,... | collective-permute-start | bytes 1572872 | tf_op jit(solution)/shard_map/ppermute | solution.py:34
  17.6 5.5 %collective-permute-start.6 = (f32[1,928]{1,0:T(1,128)S(1)}, f32[1,928]{1,0:T(1,128)S(1)}, u32[]{:S(2)}, u32[]{:S(2)}) collective-permute-start(f32[1,928]{1,0:T(1,128)S(1)} %bitcast.208), channel_id=1, source_target_pairs={{0,24},{4,28},{8,16},{12,20},{16,8},{20,12},{24,0},{28,4},{1,25},{... | collective-permute-start | bytes 11144 | tf_op jit(solution)/shard_map/ppermute | solution.py:34
  26.6 11.6 %collective-permute-start.1 = (bf16[256,1024]{1,0:T(8,128)(2,1)S(1)}, bf16[256,1024]{1,0:T(8,128)(2,1)S(1)}, u32[]{:S(2)}, u32[]{:S(2)}) collective-permute-start(bf16[256,1024]{1,0:T(8,128)(2,1)S(1)} %bitcast.174), channel_id=1, source_target_pairs={{0,4},{4,0},{8,12},{12,8},{16,20},{20,16},{24,28},{28,24},{1,5},{5... | collective-permute-start | bytes 1572872 | tf_op jit(solution)/shard_map/ppermute | solution.py:34
  39.0 10.5 %all-to-all-start = ((bf16[4,2,32,896]{3,2,1,0:T(8,128)(2,1)}), bf16[4,2,32,896]{3,2,1,0:T(8,128)(2,1)S(1)}, u32[]{:S(2)}, u32[]{:S(2)}) async-start(bf16[4,2,32,896]{3,2,1,0:T(8,128)(2,1)} %copy.60), calls=%async_computation | async-start | bytes 917504 | tf_op jit(solution)/shard_map/all_to_all | solution.py:667
  42.9 51.3 %all-gather.9.cloned.1.call-start = ((), (), s32[]{:S(2)}) async-start(), calls=%async_computation.7 | async-start | bytes 1310720 | tf_op jit(solution)/shard_map/all_gather | solution.py:50
  49.4 14.9 %collective-permute-start.12 = (bf16[256,1024]{1,0:T(8,128)(2,1)S(1)}, bf16[256,1024]{1,0:T(8,128)(2,1)}, u32[]{:S(2)}, u32[]{:S(2)}) collective-permute-start(bf16[256,1024]{1,0:T(8,128)(2,1)S(1)} %bitcast.178), channel_id=1, source_target_pairs={{0,2},{1,3},{2,0},{3,1},{4,6},{5,7},{6,4},{7,5},{8,10},{9,11},{10,... | collective-permute-start | bytes 1572872 | tf_op jit(solution)/shard_map/ppermute | solution.py:34
  52.7 71.0 %all-gather.11.cloned.1.call-start = ((), (), s32[]{:S(2)}) async-start(), calls=%async_computation.8 | async-start | bytes 1310720 | tf_op jit(solution)/shard_map/all_gather | solution.py:50
  53.4 21.0 %collective-permute-start.3 = (bf16[256,1024]{1,0:T(8,128)(2,1)S(1)}, bf16[256,1024]{1,0:T(8,128)(2,1)S(1)}, u32[]{:S(2)}, u32[]{:S(2)}) collective-permute-start(bf16[256,1024]{1,0:T(8,128)(2,1)S(1)} %collective-permute-done.1), channel_id=1, source_target_pairs={{0,2},{1,3},{2,0},{3,1},{4,6},{5,7},{6,4},{7,5},{8,10},{9,11},{10,... | collective-permute-start | bytes 1572872 | tf_op jit(solution)/shard_map/ppermute | solution.py:34
  57.6 18.3 %collective-permute-start.11 = (bf16[256,1024]{1,0:T(8,128)(2,1)S(1)}, bf16[256,1024]{1,0:T(8,128)(2,1)}, u32[]{:S(2)}, u32[]{:S(2)}) collective-permute-start(bf16[256,1024]{1,0:T(8,128)(2,1)S(1)} %bitcast.179), channel_id=1, source_target_pairs={{0,4},{4,0},{8,12},{12,8},{16,20},{20,16},{24,28},{28,24},{1,5},{5... | collective-permute-start | bytes 1572872 | tf_op jit(solution)/shard_map/ppermute | solution.py:34
  64.3 17.8 %collective-permute-start.13 = (bf16[256,1024]{1,0:T(8,128)(2,1)}, bf16[256,1024]{1,0:T(8,128)(2,1)}, u32[]{:S(2)}, u32[]{:S(2)}) collective-permute-start(bf16[256,1024]{1,0:T(8,128)(2,1)} %collective-permute-done.12), channel_id=1, source_target_pairs={{0,4},{4,0},{8,12},{12,8},{16,20},{20,16},{24,28},{28,24},{1,5},{5... | collective-permute-start | bytes 1572872 | tf_op jit(solution)/shard_map/ppermute | solution.py:34
  75.9 18.4 %collective-permute-start.10 = (bf16[1024,1024]{1,0:T(8,128)(2,1)}, bf16[1024,1024]{1,0:T(8,128)(2,1)}, u32[]{:S(2)}, u32[]{:S(2)}) collective-permute-start(bf16[1024,1024]{1,0:T(8,128)(2,1)} %pad_maximum_fusion.refs_0_), channel_id=1, source_target_pairs={{0,1},{1,0},{2,3},{3,2},{4,5},{5,4},{6,7},{7,6},{8,9},{9,8},{10,11... | collective-permute-start | bytes 6291464 | tf_op jit(solution)/shard_map/ppermute | solution.py:34
  83.7 10.7 %collective-permute-start.14 = (bf16[1024,1024]{1,0:T(8,128)(2,1)S(1)}, bf16[1024,1024]{1,0:T(8,128)(2,1)}, u32[]{:S(2)}, u32[]{:S(2)}) collective-permute-start(bf16[1024,1024]{1,0:T(8,128)(2,1)S(1)} %pad_maximum_fusion.1.refs_2_.refs_0_), channel_id=1, source_target_pairs={{0,1},{1,0},{2,3},{3,2},{4,5},{5,4},{6,7},{7,6},{8,9},{9,8},{10,11... | collective-permute-start | bytes 6291464 | tf_op jit(solution)/shard_map/ppermute | solution.py:34
  83.7 9.8 %collective-permute-start.15 = (bf16[32,1024]{1,0:T(8,128)(2,1)S(1)}, bf16[32,1024]{1,0:T(8,128)(2,1)S(1)}, u32[]{:S(2)}, u32[]{:S(2)}) collective-permute-start(bf16[32,1024]{1,0:T(8,128)(2,1)S(1)} %copy-done.28), channel_id=1, source_target_pairs={{0,0},{4,1},{8,2},{12,3},{16,4},{20,5},{24,6},{28,7},{1,8},{5,9},{... | collective-permute-start | bytes 196616 | tf_op jit(solution)/shard_map/ppermute | solution.py:78
  94.3 80.1 %reduce-scatter.3.cloned.1.call-start = ((), (), s32[]{:S(2)}) async-start(), calls=%async_computation.4 | async-start | bytes 2621440 | tf_op jit(solution)/shard_map/reduce_scatter | solution.py:53
  120.9 83.4 %reduce-scatter.5.cloned.1.call-start = ((), (), s32[]{:S(2)}) async-start(), calls=%async_computation.5 | async-start | bytes 1310720 | tf_op jit(solution)/shard_map/reduce_scatter | solution.py:53
  156.2 9.7 %collective-permute-start.16 = (bf16[1024,1024]{1,0:T(8,128)(2,1)}, bf16[1024,1024]{1,0:T(8,128)(2,1)S(1)}, u32[]{:S(2)}, u32[]{:S(2)}) collective-permute-start(bf16[1024,1024]{1,0:T(8,128)(2,1)} %get-tuple-element.86), channel_id=1, source_target_pairs={{0,1},{1,0},{2,3},{3,2},{4,5},{5,4},{6,7},{7,6},{8,9},{9,8},{10,11... | collective-permute-start | bytes 6291464 | tf_op jit(solution)/shard_map/ppermute | solution.py:34
  171.2 17.0 %collective-permute-start.17 = (bf16[2,256,512]{2,1,0:T(8,128)(2,1)}, bf16[2,256,512]{2,1,0:T(8,128)(2,1)S(1)}, u32[]{:S(2)}, u32[]{:S(2)}) collective-permute-start(bf16[2,256,512]{2,1,0:T(8,128)(2,1)} %bitcast.216), channel_id=1, source_target_pairs={{0,2},{1,3},{2,0},{3,1},{4,6},{5,7},{6,4},{7,5},{8,10},{9,11},{10,... | collective-permute-start | bytes 1572872 | tf_op jit(solution)/shard_map/ppermute | solution.py:34
  171.2 17.8 %collective-permute-start.18 = (bf16[2,256,512]{2,1,0:T(8,128)(2,1)}, bf16[2,256,512]{2,1,0:T(8,128)(2,1)}, u32[]{:S(2)}, u32[]{:S(2)}) collective-permute-start(bf16[2,256,512]{2,1,0:T(8,128)(2,1)} %get-tuple-element.93), channel_id=1, source_target_pairs={{0,4},{4,0},{8,12},{12,8},{16,20},{20,16},{24,28},{28,24},{1,5},{5... | collective-permute-start | bytes 1572872 | tf_op jit(solution)/shard_map/ppermute | solution.py:34
  190.6 13.7 %collective-permute-start.23 = (bf16[1024,1024]{1,0:T(8,128)(2,1)}, bf16[1024,1024]{1,0:T(8,128)(2,1)}, u32[]{:S(2)}, u32[]{:S(2)}) collective-permute-start(bf16[1024,1024]{1,0:T(8,128)(2,1)} %get-tuple-element.116), channel_id=1, source_target_pairs={{0,1},{1,0},{2,3},{3,2},{4,5},{5,4},{6,7},{7,6},{8,9},{9,8},{10,11... | collective-permute-start | bytes 6291464 | tf_op jit(solution)/shard_map/ppermute | solution.py:34
  195.7 6.0 %collective-permute-start.22 = (f32[2,2,384]{2,0,1:T(2,128)S(1)}, f32[2,2,384]{2,0,1:T(2,128)S(1)}, u32[]{:S(2)}, u32[]{:S(2)}) collective-permute-start(f32[2,2,384]{2,0,1:T(2,128)S(1)} %get-tuple-element.150), channel_id=1, source_target_pairs={{0,24},{4,28},{8,16},{12,20},{16,8},{20,12},{24,0},{28,4},{1,25},{... | collective-permute-start | bytes 18440 | tf_op jit(solution)/shard_map/ppermute | solution.py:34
  208.3 12.4 %collective-permute-start.24 = (bf16[2,256,512]{2,1,0:T(8,128)(2,1)}, bf16[2,256,512]{2,1,0:T(8,128)(2,1)S(1)}, u32[]{:S(2)}, u32[]{:S(2)}) collective-permute-start(bf16[2,256,512]{2,1,0:T(8,128)(2,1)} %bitcast.217), channel_id=1, source_target_pairs={{0,2},{1,3},{2,0},{3,1},{4,6},{5,7},{6,4},{7,5},{8,10},{9,11},{10,... | collective-permute-start | bytes 1572872 | tf_op jit(solution)/shard_map/ppermute | solution.py:34
  208.7 14.1 %collective-permute-start.25 = (bf16[2,256,512]{2,1,0:T(8,128)(2,1)}, bf16[2,256,512]{2,1,0:T(8,128)(2,1)S(1)}, u32[]{:S(2)}, u32[]{:S(2)}) collective-permute-start(bf16[2,256,512]{2,1,0:T(8,128)(2,1)} %get-tuple-element.118), channel_id=1, source_target_pairs={{0,4},{4,0},{8,12},{12,8},{16,20},{20,16},{24,28},{28,24},{1,5},{5... | collective-permute-start | bytes 1572872 | tf_op jit(solution)/shard_map/ppermute | solution.py:34
  222.8 23.2 %collective-permute-start.28 = (bf16[256,512]{1,0:T(8,128)(2,1)}, bf16[256,512]{1,0:T(8,128)(2,1)}, u32[]{:S(2)}, u32[]{:S(2)}) collective-permute-start(bf16[256,512]{1,0:T(8,128)(2,1)} %fusion.15), channel_id=1, source_target_pairs={{0,4},{4,0},{8,12},{12,8},{16,20},{20,16},{24,28},{28,24},{1,5},{5... | collective-permute-start | bytes 786440 | tf_op jit(solution)/shard_map/ppermute | solution.py:34
  223.8 23.4 %collective-permute-start.29 = (bf16[256,512]{1,0:T(8,128)(2,1)}, bf16[256,512]{1,0:T(8,128)(2,1)}, u32[]{:S(2)}, u32[]{:S(2)}) collective-permute-start(bf16[256,512]{1,0:T(8,128)(2,1)} %fusion.16), channel_id=1, source_target_pairs={{0,2},{1,3},{2,0},{3,1},{4,6},{5,7},{6,4},{7,5},{8,10},{9,11},{10,... | collective-permute-start | bytes 786440 | tf_op jit(solution)/shard_map/ppermute | solution.py:34
  224.5 5.9 %collective-permute-start.30 = (f32[2,384]{1,0:T(2,128)S(1)}, f32[2,384]{1,0:T(2,128)S(1)}, u32[]{:S(2)}, u32[]{:S(2)}) collective-permute-start(f32[2,384]{1,0:T(2,128)S(1)} %slice_bitcast_fusion.13), channel_id=1, source_target_pairs={{0,4},{4,0},{8,12},{12,8},{16,20},{20,16},{24,28},{28,24},{1,5},{5... | collective-permute-start | bytes 9224 | tf_op jit(solution)/shard_map/ppermute | solution.py:34
  226.3 9.5 %collective-permute-start.33 = (bf16[32,1024]{1,0:T(8,128)(2,1)S(1)}, bf16[32,1024]{1,0:T(8,128)(2,1)S(1)}, u32[]{:S(2)}, u32[]{:S(2)}) collective-permute-start(bf16[32,1024]{1,0:T(8,128)(2,1)S(1)} %bitcast.204), channel_id=1, source_target_pairs={{0,0},{1,4},{2,8},{3,12},{4,16},{5,20},{6,24},{7,28},{8,1},{9,5},{... | collective-permute-start | bytes 196616 | tf_op jit(solution)/shard_map/ppermute | solution.py:78
  230.6 8.5 %collective-permute-start.32 = (bf16[4,32,896]{2,1,0:T(8,128)(2,1)S(1)}, bf16[4,32,896]{2,1,0:T(8,128)(2,1)S(1)}, u32[]{:S(2)}, u32[]{:S(2)}) collective-permute-start(bf16[4,32,896]{2,1,0:T(8,128)(2,1)S(1)} %dynamic-slice_bitcast_fusion), channel_id=1, source_target_pairs={{0,4},{4,0},{8,12},{12,8},{16,20},{20,16},{24,28},{28,24},{1,5},{5... | collective-permute-start | bytes 688136 | tf_op jit(solution)/shard_map/ppermute | solution.py:34
  234.1 14.6 %collective-permute-start.26 = (bf16[256,512]{1,0:T(8,128)(2,1)}, bf16[256,512]{1,0:T(8,128)(2,1)S(1)}, u32[]{:S(2)}, u32[]{:S(2)}) collective-permute-start(bf16[256,512]{1,0:T(8,128)(2,1)} %fusion.13), channel_id=1, source_target_pairs={{0,4},{4,0},{8,12},{12,8},{16,20},{20,16},{24,28},{28,24},{1,5},{5... | collective-permute-start | bytes 786440 | tf_op jit(solution)/shard_map/ppermute | solution.py:34
  235.8 13.0 %collective-permute-start.27 = (bf16[256,512]{1,0:T(8,128)(2,1)}, bf16[256,512]{1,0:T(8,128)(2,1)}, u32[]{:S(2)}, u32[]{:S(2)}) collective-permute-start(bf16[256,512]{1,0:T(8,128)(2,1)} %fusion.14), channel_id=1, source_target_pairs={{0,2},{1,3},{2,0},{3,1},{4,6},{5,7},{6,4},{7,5},{8,10},{9,11},{10,... | collective-permute-start | bytes 786440 | tf_op jit(solution)/shard_map/ppermute | solution.py:34
  240.0 12.6 %all-to-all-start.1 = ((bf16[4,2,32,896]{3,2,1,0:T(8,128)(2,1)}), bf16[4,2,32,896]{3,2,1,0:T(8,128)(2,1)}, u32[]{:S(2)}, u32[]{:S(2)}) async-start(bf16[4,2,32,896]{3,2,1,0:T(8,128)(2,1)} %pad_maximum_fusion.4), calls=%async_computation.3 | async-start | bytes 917504 | tf_op jit(solution)/shard_map/all_to_all | solution.py:67
  (39 other events, 205.4 us)
Sparse Core Ops, SparseCore 0:
  9.6 29.7 all-gather.6
  52.9 27.1 all-gather.8
  94.4 26.0 all-gather.10
  122.6 43.3 reduce-scatter.2
  174.6 27.4 reduce-scatter.4

commit v4 on v3

--- a/solution.py
+++ b/solution.py
@@ -208,7 +208,7 @@
 def mlp_kernel(
     peers, x_ref, g_ref, up_ref, down_ref, gain_ref, shift_ref, bias_ref, gain_one_ref, shift_one_ref,
     hid_ref, flow_ref, one_ref, terms_out, gain_out, shift_out, bias_out,
-    down_s, up_s,
+    down_s, up_s, unit_s, value_s, active_s, grad_s,
 ):
     step = pl.program_id(0)
 
@@ -217,30 +217,37 @@
         for ref in (down_s, up_s, gain_out, shift_out, bias_out):
             ref[...] = jnp.zeros_like(ref)
 
-    gain = gain_ref[...]
-    source, grad = load(x_ref), load(g_ref)
-    half = source.shape[0] // 2
-    parts = [slice(0, half), slice(half, 2 * half)]
-    stack = lambda values: jnp.concatenate(values, 0)
-    units, values = zip(*[normed(source[p], gain, shift_ref[...]) for p in parts])
-    uppers = [dot(value, up_ref[...]) + bias_ref[...] for value in values]
-    actives, grads = [], []
-    for p, upper in zip(parts, uppers):
-        grad_active = contract_cols(grad[p], down_ref[...])
-        cdf = 0.5 * (1.0 + lax.erf(upper * math.sqrt(0.5)))
-        density = jnp.exp(-0.5 * upper * upper) * (1.0 / math.sqrt(2.0 * math.pi))
-        actives.append((upper * cdf).astype(BF))
-        grads.append((grad_active * (cdf + upper * density)).astype(BF))
-    unit, value, active, grad_upper = [stack(v) for v in (units, values, actives, grads)]
-    one_ref[...] = (unit * gain_one_ref[...] + shift_one_ref[...]).astype(BF)
+    gain, shift = gain_ref[...], shift_ref[...]
+    gain_one, shift_one = gain_one_ref[...], shift_one_ref[...]
+    for at in chunks(value_s.shape[0]):
+        unit, value = normed(load(x_ref, at), gain, shift)
+        unit_s[at, :] = unit
+        value_s[at, :] = value
+        one_ref[at, :] = (unit * gain_one + shift_one).astype(BF)
+    value, grad = value_s[...], load(g_ref)
+    upper = dot(value, up_ref[...])
+    grad_active = contract_cols(grad, down_ref[...])
+    bias = bias_ref[...]
+    for at in chunks(value_s.shape[0]):
+        u = upper[at] + bias
+        cdf = 0.5 * (1.0 + lax.erf(u * math.sqrt(0.5)))
+        density = jnp.exp(-0.5 * u * u) * (1.0 / math.sqrt(2.0 * math.pi))
+        active_s[at, :] = (u * cdf).astype(BF)
+        low = (grad_active[at] * (cdf + u * density)).astype(BF)
+        grad_s[at, :] = low
+        bias_out[...] += row_sum(low.astype(F32))
+    active, grad_upper = active_s[...], grad_s[...]
     store(hid_ref, dot(active, down_ref[...]).astype(BF))
     down_s[...] += contract_rows(active, grad)
     up_s[...] += contract_rows(value, grad_upper)
     back = contract_cols(grad_upper, up_ref[...])
-    store(flow_ref, (back * gain).astype(BF))
-    gain_out[...] += row_sum(back * unit)
-    shift_out[...] += row_sum(back)
-    bias_out[...] += row_sum(grad_upper.astype(F32))
+    flows = []
+    for at in chunks(value_s.shape[0]):
+        part = back[at]
+        flows.append((part * gain).astype(BF))
+        gain_out[...] += row_sum(part * unit_s[at, :])
+        shift_out[...] += row_sum(part)
+    store(flow_ref, jnp.concatenate(flows, 0))
 
     @pl.when(step == pl.num_programs(0) - 1)
     def _():
@@ -321,12 +328,16 @@
         for ref in (gain_out, shift_out):
             ref[...] = jnp.zeros_like(ref)
 
-    gain = gain_ref[...]
-    unit, _ = normed(load(x_ref), gain, shift_ref[...])
+    gain, shift = gain_ref[...], shift_ref[...]
     back = contract_cols(linear_ref[...], qkv_ref[...])
-    store(flow_out, (load(flow_ref).astype(F32) + back * gain).astype(BF))
-    gain_out[...] += row_sum(back * unit)
-    shift_out[...] += row_sum(back)
+    flows = []
+    for at in chunks(back.shape[0]):
+        part = back[at]
+        unit, _ = normed(load(x_ref, at), gain, shift)
+        flows.append((load(flow_ref, at).astype(F32) + part * gain).astype(BF))
+        gain_out[...] += row_sum(part * unit)
+        shift_out[...] += row_sum(part)
+    store(flow_out, jnp.concatenate(flows, 0))
 
 
 def hidden_kernel(hid_ref, att_ref, out_ref, hid_out):
@@ -387,8 +398,13 @@
     return pl.program_id(0) < pl.num_programs(0) // 2
 
 
-def load(pair):
-    return jnp.where(first_half(), pair[0][...], pair[1][...])
+def chunks(rows):
+    size = math.gcd(rows, 64)
+    return [slice(start, start + size) for start in range(0, rows, size)]
+
+
+def load(pair, at=slice(None)):
+    return jnp.where(first_half(), pair[0][at, :], pair[1][at, :])
 
 
 def store(pair, value):
@@ -401,7 +417,7 @@
         pair[1][...] = value
 
 
-def by_tokens(kernel, tokens, pairs, streamed, fixed, pairs_out, streamed_out, fixed_out, scratch, name, size=512):
+def by_tokens(kernel, tokens, pairs, streamed, fixed, pairs_out, streamed_out, fixed_out, scratch, name, size=512, limit=52):
     block = math.gcd(tokens // 2, size)
     steps = tokens // block
     stream = lambda n: pl.BlockSpec((block, n), lambda i: (i, 0))
@@ -433,7 +449,7 @@
         + [whole(v.shape) for v in fixed_out],
         out_shape=outputs,
         scratch_shapes=scratch,
-        compiler_params=pltpu.CompilerParams(vmem_limit_bytes=60 * 1024 * 1024),
+        compiler_params=pltpu.CompilerParams(vmem_limit_bytes=limit * 1024 * 1024),
         cost_estimate=pl.CostEstimate(flops=1024, bytes_accessed=1024, transcendentals=0),
         name=name,
     )(*inputs)
@@ -583,7 +599,7 @@
         scratch_shapes=[pltpu.VMEM(shape, BF)] * 4
         + [pltpu.VMEM((near * heads, HD, length), BF)] * 2
         + [pltpu.VMEM(shape, F32)] * 3,
-        compiler_params=pltpu.CompilerParams(vmem_limit_bytes=60 * 1024 * 1024),
+        compiler_params=pltpu.CompilerParams(vmem_limit_bytes=48 * 1024 * 1024),
         cost_estimate=pl.CostEstimate(flops=1024, bytes_accessed=1024, transcendentals=0),
         name="attend",
     )(spot[None], pack, seg.reshape(-1, 1), seg)
@@ -681,6 +697,7 @@
     count_all = team * tokens
     vector = jax.ShapeDtypeStruct((1, width), F32)
 
+    block = math.gcd(count_all // 2, 512)
     hid, flow, input_one, terms, gain_two_sum, shift_two_sum, grad_up_b = by_tokens(
         partial(mlp_kernel, far),
         count_all,
@@ -695,8 +712,11 @@
             vector,
             jax.ShapeDtypeStruct((1, share), F32),
         ],
-        [pltpu.VMEM((share, width), F32), pltpu.VMEM((width, share), F32)],
+        [pltpu.VMEM((share, width), F32), pltpu.VMEM((width, share), F32)]
+        + [pltpu.VMEM((block, width), t) for t in (F32, BF)]
+        + [pltpu.VMEM((block, share), BF)] * 2,
         "feed_forward",
+        limit=60,
     )
     terms_sum = lay.scatter_far(terms.reshape(far, depth, 2 * share))
 
@@ -717,11 +737,10 @@
         [jax.ShapeDtypeStruct((width, 3 * part), BF), jax.ShapeDtypeStruct((part, width), BF)],
         [],
         "heads",
-        1024,
     )
     attended, back = attend(lay.spot, pack, seg, heads, ctx)
     (hid,) = by_tokens(
-        hidden_kernel, count_all, [hid], [attended], [w_out], [width], [], [], [], "hidden", 1024
+        hidden_kernel, count_all, [hid], [attended], [w_out], [width], [], [], [], "hidden"
     )
     hid_got = swap(hid[1], "ctx", ctx, 1)
     linear, last, grad_qkv_b, *out_terms = by_tokens(
@@ -739,7 +758,6 @@
         + [jax.ShapeDtypeStruct((part, width), BF)] * (not packed),
         [pltpu.VMEM((width, 3 * part), F32), pltpu.VMEM((part, width), F32)],
         "weights",
-        1024,
     )
     last = last.reshape(far, depth, -1)
     if not packed:
@@ -759,6 +777,7 @@
         [vector, vector],
         [],
         "flow",
+        limit=60,
     )
     hid_came = after(lay.first_steps(hid_first), gain_one_sum)
     flow = after(tuple(flow), hid_came)

time: 264 us -> 261 us (0.989)
  Pallas kernels: 89 us -> 85.9 us
    unnamed x67 -> x75, local copies, waits for them, and re-layouts: 5.87 us -> 6.36 us
  transfers between devices with their start and end apart: 41 -> 41, of which waited for: 18 -> 18; matrix products, arithmetic and copies ran while one was open for 18% -> 18% of each run, Pallas kernels for 32% -> 31%
where the time goes in v4:
time: 261 us; the launch traced here: 258 us
  Pallas kernels  85.9 us (33%)
  waiting for transfers between devices  62 us (24%)
  starting transfers between devices  43.3 us (17%)
  other arithmetic  27.3 us (10%)
  local copies, waits for them, and re-layouts  25 us (10%)
  between operations  14.8 us (6%)
    pallas_call x5, Pallas kernels, by_tokens(): pl.pallas_call(body, grid=(steps,), in_specs=[spec for pair in pairs for...  60 us
    ppermute x32, waiting for transfers between devices, swap(): return lax.ppermute(value, axis, [(i, i ^ bits) for i in range(size)])  50.5 us
    ppermute x32, starting transfers between devices, swap(): return lax.ppermute(value, axis, [(i, i ^ bits) for i in range(size)])  25.5 us
    pallas_call x1, Pallas kernels, attend(): pl.pallas_call(partial(attend_kernel, heads, ctx, near), out_shape=(jax.S...  15.9 us
    ppermute x2, starting transfers between devices, own_heads(): return lax.ppermute(value, ('seq', 'ctx'), pairs)  9.08 us
    pallas_call x2, Pallas kernels, pair_sums(): pl.pallas_call(partial(pair_kernel, rows), out_shape=[jax.ShapeDtypeStruc...  8 us
    unnamed x75, local copies, waits for them, and re-layouts  6.36 us
    all_to_all x1, waiting for transfers between devices, local(): payload = lax.all_to_all(payload, 'ctx', 0, 0, tiled=True)  6.33 us
  transfers between devices with their start and end apart: 41, of which 18 were waited for; matrix products, arithmetic and copies ran while one was open for 18% of the time, Pallas kernels for 31%

profile of v4, /device:TPU:6, one launch (start us, length us, event | category | flops | bytes accessed | tf_op | source)
XLA Modules:
  0.0 258.3 jit_solution(11967464929863172513)
XLA Ops:
  11.1 6.3 %collective-permute-done = bf16[4,32,896]{2,1,0:T(8,128)(2,1)S(1)} collective-permute-done((bf16[4,32,896]{2,1,0:T(8,128)(2,1)S(1)}, bf16[4,32,896]{2,1,0:T(8,128)(2,1)S(1)}, u32[]{:S(2)}, u32[]{:S(2)}) %collective-permute-start) | collective-permute-done | bytes 229408 | tf_op jit(solution)/shard_map/ppermute | solution.py:34
  17.6 3.7 %collective-permute-start.6 = (f32[1,928]{1,0:T(1,128)S(1)}, f32[1,928]{1,0:T(1,128)S(1)}, u32[]{:S(2)}, u32[]{:S(2)}) collective-permute-start(f32[1,928]{1,0:T(1,128)S(1)} %bitcast.207), channel_id=1, source_target_pairs={{0,24},{4,28},{8,16},{12,20},{16,8},{20,12},{24,0},{28,4},{1,25},{... | collective-permute-start | bytes 11144 | tf_op jit(solution)/shard_map/ppermute | solution.py:34
  23.1 2.8 %collective-permute-done.5 = f32[1,928]{1,0:T(1,128)S(1)} collective-permute-done((f32[1,928]{1,0:T(1,128)S(1)}, f32[1,928]{1,0:T(1,128)S(1)}, u32[]{:S(2)}, u32[]{:S(2)}) %collective-permute-start.5) | collective-permute-done | bytes 3744 | tf_op jit(solution)/shard_map/ppermute | solution.py:34
  28.1 1.9 collective-permute-done.7
  31.9 3.8 %collective-permute-done.9 = f32[16,928]{1,0:T(8,128)S(1)} collective-permute-done((f32[16,928]{1,0:T(8,128)S(1)}, f32[16,928]{1,0:T(8,128)S(1)}, u32[]{:S(2)}, u32[]{:S(2)}) %collective-permute-start.9) | collective-permute-done | bytes 59424 | tf_op jit(solution)/shard_map/ppermute | solution.py:34
  36.4 1.7 collective-permute-done.1
  39.0 4.0 %all-to-all-start = ((bf16[4,2,32,896]{3,2,1,0:T(8,128)(2,1)}), bf16[4,2,32,896]{3,2,1,0:T(8,128)(2,1)S(1)}, u32[]{:S(2)}, u32[]{:S(2)}) async-start(bf16[4,2,32,896]{3,2,1,0:T(8,128)(2,1)} %copy.60), calls=%async_computation | async-start | bytes 917504 | tf_op jit(solution)/shard_map/all_to_all | solution.py:683
  43.1 6.3 %all-to-all-done = bf16[4,2,32,896]{3,2,1,0:T(8,128)(2,1)S(1)} async-done(((bf16[4,2,32,896]{3,2,1,0:T(8,128)(2,1)}), bf16[4,2,32,896]{3,2,1,0:T(8,128)(2,1)S(1)}, u32[]{:S(2)}, u32[]{:S(2)}) %all-to-all-start) | async-done | bytes 458784 | tf_op jit(solution)/shard_map/all_to_all | solution.py:683
  49.4 1.7 collective-permute-start.12
  57.7 6.6 %collective-permute-done.12 = bf16[256,1024]{1,0:T(8,128)(2,1)} collective-permute-done((bf16[256,1024]{1,0:T(8,128)(2,1)S(1)}, bf16[256,1024]{1,0:T(8,128)(2,1)}, u32[]{:S(2)}, u32[]{:S(2)}) %collective-permute-start.12) | collective-permute-done | bytes 524320 | tf_op jit(solution)/shard_map/ppermute | solution.py:34
  65.8 5.5 %fusion.12 = (f32[2048,128]{1,0:T(8,128)}, f32[2048,128]{1,0:T(8,128)}) fusion(f32[128]{0:T(128)S(1)} %get-tuple-element.165, f32[128]{0:T(128)S(1)} %get-tuple-element.166, f32[2048]{0:T(1024)S(1)} %bitcast.204), kind=kLoop, calls=%fused_computation.24 | loop fusion | flops 524288 | bytes 2106368 | tf_op jit(solution)/shard_map/mul | solution.py:680
  71.3 3.2 %collective-permute-done.3 = bf16[256,1024]{1,0:T(8,128)(2,1)} collective-permute-done((bf16[256,1024]{1,0:T(8,128)(2,1)S(1)}, bf16[256,1024]{1,0:T(8,128)(2,1)}, u32[]{:S(2)}, u32[]{:S(2)}) %collective-permute-start.3) | collective-permute-done | bytes 524320 | tf_op jit(solution)/shard_map/ppermute | solution.py:34
  74.5 2.6 %pad_maximum_fusion.refs_0_ = bf16[1024,1024]{1,0:T(8,128)(2,1)} fusion(bf16[256,1024]{1,0:T(8,128)(2,1)} %collective-permute-done.3, bf16[256,1024]{1,0:T(8,128)(2,1)S(1)} %collective-permute-done.2, bf16[256,1024]{1,0:T(8,128)(2,1)S(1)} %collective-permute-done.1, bf16[256,1024]{1,0:T(8,128)(2,1)S(1)} %bitcast.176), kind=kLoop, calls=%fused_computation.4 | loop fusion | flops 8388608 | bytes 4194304 | tf_op jit(solution)/shard_map/concatenate | solution.py:92
  77.1 3.6 %collective-permute-done.13 = bf16[256,1024]{1,0:T(8,128)(2,1)} collective-permute-done((bf16[256,1024]{1,0:T(8,128)(2,1)}, bf16[256,1024]{1,0:T(8,128)(2,1)}, u32[]{:S(2)}, u32[]{:S(2)}) %collective-permute-start.13) | collective-permute-done | bytes 524320 | tf_op jit(solution)/shard_map/ppermute | solution.py:34
  82.4 5.3 %collective-permute-start.15 = (bf16[32,1024]{1,0:T(8,128)(2,1)S(1)}, bf16[32,1024]{1,0:T(8,128)(2,1)S(1)}, u32[]{:S(2)}, u32[]{:S(2)}) collective-permute-start(bf16[32,1024]{1,0:T(8,128)(2,1)S(1)} %copy-done.32), channel_id=1, source_target_pairs={{0,0},{4,1},{8,2},{12,3},{16,4},{20,5},{24,6},{28,7},{1,8},{5,9},{... | collective-permute-start | bytes 196616 | tf_op jit(solution)/shard_map/ppermute | solution.py:78
  88.7 3.5 %collective-permute-done.15 = bf16[32,1024]{1,0:T(8,128)(2,1)S(1)} collective-permute-done((bf16[32,1024]{1,0:T(8,128)(2,1)S(1)}, bf16[32,1024]{1,0:T(8,128)(2,1)S(1)}, u32[]{:S(2)}, u32[]{:S(2)}) %collective-permute-start.15) | collective-permute-done | bytes 65568 | tf_op jit(solution)/shard_map/ppermute | solution.py:78
  93.0 25.9 %feed_forward.1 = (bf16[1024,1024]{1,0:T(8,128)(2,1)}, bf16[1024,1024]{1,0:T(8,128)(2,1)}, bf16[1024,1024]{1,0:T(8,128)(2,1)}, bf16[1024,1024]{1,0:T(8,128)(2,1)...) custom-call(bf16[1024,1024]{1,0:T(8,128)(2,1)} %pad_maximum_fusion.r, ...), custom_call_target="tpu_custom_call" | custom-call | flops 1024 | bytes 1024 | tf_op jit(solution)/shard_map/feed_forward/pallas_call | solution.py:441
  120.2 8.4 %heads.1 = (bf16[2048,512]{1,0:T(8,128)(2,1)}, bf16[1024,384]{1,0:T(8,128)(2,1)S(1)}, bf16[128,1024]{1,0:T(8,128)(2,1)S(1)}) custom-call(bf16[1024,1024]{1,0:T(8,128)(2,1)} %copy-done.2, bf16[1024,1024]{1,0:T(8,128)(2,1)} %collective-permute-done.14.refs_3_.refs_1_, bf16[2048,1024]{1,0:T(8,128)(2,1)} %get-tuple-element.87.refs_2_, ...), custom_call_target="tpu_custom_call" | custom-call | flops 1024 | bytes 1024 | tf_op jit(solution)/shard_map/heads/pallas_call | solution.py:441
  128.6 1.9 copy-done
  130.5 15.9 %attend.1 = (bf16[2048,128]{1,0:T(8,128)(2,1)S(1)}, f32[2048,384]{1,0:T(8,128)}) custom-call(s32[1]{0:T(128)} %bitcast.19.spot_ref, bf16[2048,512]{1,0:T(8,128)(2,1)S(1)} %copy-done, s32[2048,1]{1,0:T(8,128)S(1)} %bitcast.173, s32[2,1024]{1,0:T(2,128)S(1)} %get-tuple-element.156.seg_row_ref), custom_call_target="tpu_custom_call" | custom-call | flops 1024 | bytes 1024 | tf_op jit(solution)/shard_map/attend/pallas_call | solution.py:591
  146.4 6.3 %hidden.1 = (bf16[1024,1024]{1,0:T(8,128)(2,1)}, bf16[1024,1024]{1,0:T(8,128)(2,1)}) custom-call(bf16[1024,1024]{1,0:T(8,128)(2,1)} %get-tuple-element.77.refs_0_, bf16[1024,1024]{1,0:T(8,128)(2,1)} %get-tuple-element.78.refs_1_, bf16[2048,128]{1,0:T(8,128)(2,1)S(1)} %get-tuple-element.83.refs_2_.refs_3_, bf16[128,1024]{1,0:T(8,128)(2,1)S(1)} %get-tuple-element.84.refs_3_), custom_call_target="tpu_custom_call" | custom-call | flops 1024 | bytes 1024 | tf_op jit(solution)/shard_map/hidden/pallas_call | solution.py:441
  153.2 9.2 %weights.1 = (bf16[2048,384]{1,0:T(8,128)(2,1)}, bf16[1024,512]{1,0:T(8,128)(2,1)}, f32[1,384]{1,0:T(1,128)S(1)}) custom-call(bf16[1024,1024]{1,0:T(8,128)(2,1)} %copy-done.2, bf16[1024,1024]{1,0:T(8,128)(2,1)} %collective-permute-done.14.refs_3_.refs_1_, bf16[2048,1024]{1,0:T(8,128)(2,1)} %get-tuple-element.87.refs_2_, ...), custom_call_target="tpu_custom_call" | custom-call | flops 1024 | bytes 1024 | tf_op jit(solution)/shard_map/weights/pallas_call | solution.py:441
  162.4 4.0 %pair_sums.2 = (f32[2,256,512]{2,1,0:T(8,128)}, bf16[1,2,256,512]{3,2,1,0:T(8,128)(2,1)}, f32[2,256,512]{2,1,0:T(8,128)}, bf16[2,256,512]{2,1,0:T(8,128)(2,1)}) custom-call(bf16[1024,1024]{1,0:T(8,128)(2,1)} %get-tuple-element.90.even_ref, bf16[1024,1024]{1,0:T(8,128)(2,1)} %collective-permute-done.16.got_ref), custom_call_target="tpu_custom_call" | custom-call | flops 1024 | bytes 1024 | tf_op jit(solution)/shard_map/pair_sums/pallas_call | solution.py:365
  169.7 10.3 %flow.1 = (bf16[1024,1024]{1,0:T(8,128)(2,1)}, bf16[1024,1024]{1,0:T(8,128)(2,1)}, f32[1,1024]{1,0:T(1,128)}, f32[1,1024]{1,0:T(1,128)}) custom-call(bf16[1024,1024]{1,0:T(8,128)(2,1)} %pad_maximum_fusion.refs_0_, bf16[1024,1024]{1,0:T(8,128)(2,1)} %collective-permute-done.10.refs_1_, bf16[1024,1024]{1,0:T(8,128)(2,1)} %get-tuple-element.98.refs_2_, ...), custom_call_target="tpu_custom_call" | custom-call | flops 1024 | bytes 1024 | tf_op jit(solution)/shard_map/flow/pallas_call | solution.py:441
  190.0 3.6 %collective-permute-start.22 = (f32[2,2,384]{2,0,1:T(2,128)S(1)}, f32[2,2,384]{2,0,1:T(2,128)S(1)}, u32[]{:S(2)}, u32[]{:S(2)}) collective-permute-start(f32[2,2,384]{2,0,1:T(2,128)S(1)} %get-tuple-element.150), channel_id=1, source_target_pairs={{0,24},{4,28},{8,16},{12,20},{16,8},{20,12},{24,0},{28,4},{1,25},{... | collective-permute-start | bytes 18440 | tf_op jit(solution)/shard_map/ppermute | solution.py:34
  195.8 2.4 collective-permute-done.21
  198.2 4.0 %pair_sums.3 = (f32[2,256,512]{2,1,0:T(8,128)}, bf16[1,2,256,512]{3,2,1,0:T(8,128)(2,1)}, f32[2,256,512]{2,1,0:T(8,128)}, bf16[2,256,512]{2,1,0:T(8,128)(2,1)}) custom-call(bf16[1024,1024]{1,0:T(8,128)(2,1)} %get-tuple-element.115.even_ref, bf16[1024,1024]{1,0:T(8,128)(2,1)} %collective-permute-done.23.got_ref), custom_call_target="tpu_custom_call" | custom-call | flops 1024 | bytes 1024 | tf_op jit(solution)/shard_map/pair_sums/pallas_call | solution.py:365
  204.0 11.3 %collective-permute-done.24 = bf16[2,256,512]{2,1,0:T(8,128)(2,1)S(1)} collective-permute-done((bf16[2,256,512]{2,1,0:T(8,128)(2,1)}, bf16[2,256,512]{2,1,0:T(8,128)(2,1)S(1)}, u32[]{:S(2)}, u32[]{:S(2)}) %collective-permute-start.24) | collective-permute-done | bytes 524320 | tf_op jit(solution)/shard_map/ppermute | solution.py:34
  223.1 3.8 %collective-permute-start.33 = (bf16[32,1024]{1,0:T(8,128)(2,1)S(1)}, bf16[32,1024]{1,0:T(8,128)(2,1)S(1)}, u32[]{:S(2)}, u32[]{:S(2)}) collective-permute-start(bf16[32,1024]{1,0:T(8,128)(2,1)S(1)} %bitcast.203), channel_id=1, source_target_pairs={{0,0},{1,4},{2,8},{3,12},{4,16},{5,20},{6,24},{7,28},{8,1},{9,5},{... | collective-permute-start | bytes 196616 | tf_op jit(solution)/shard_map/ppermute | solution.py:78
  234.7 2.1 collective-permute-done.32
  237.6 4.3 %all-to-all-start.1 = ((bf16[4,2,32,896]{3,2,1,0:T(8,128)(2,1)}), bf16[4,2,32,896]{3,2,1,0:T(8,128)(2,1)S(1)}, u32[]{:S(2)}, u32[]{:S(2)}) async-start(bf16[4,2,32,896]{3,2,1,0:T(8,128)(2,1)} %pad_maximum_fusion.4), calls=%async_computation.3 | async-start | bytes 917504 | tf_op jit(solution)/shard_map/all_to_all | solution.py:67
  249.2 2.0 unpack.1
  (265 shorter events, 65.6 us)
Async XLA Ops:
  7.2 69.9 %all-gather.7.cloned.1.call-start = ((), (), s32[]{:S(2)}) async-start(), calls=%async_computation.6 | async-start | bytes 1310720 | tf_op jit(solution)/shard_map/all_gather | solution.py:50
  10.1 7.4 %collective-permute-start = (bf16[4,32,896]{2,1,0:T(8,128)(2,1)S(1)}, bf16[4,32,896]{2,1,0:T(8,128)(2,1)S(1)}, u32[]{:S(2)}, u32[]{:S(2)}) collective-permute-start(bf16[4,32,896]{2,1,0:T(8,128)(2,1)S(1)} %dynamic-slice_bitcast_fusion.1), channel_id=1, source_target_pairs={{0,4},{4,0},{8,12},{12,8},{16,20},{20,16},{24,28},{28,24},{1,5},{5... | collective-permute-start | bytes 688136 | tf_op jit(solution)/shard_map/ppermute | solution.py:34
  10.7 25.8 %collective-permute-start.2 = (bf16[256,1024]{1,0:T(8,128)(2,1)S(1)}, bf16[256,1024]{1,0:T(8,128)(2,1)S(1)}, u32[]{:S(2)}, u32[]{:S(2)}) collective-permute-start(bf16[256,1024]{1,0:T(8,128)(2,1)S(1)} %bitcast.174), channel_id=1, source_target_pairs={{0,2},{1,3},{2,0},{3,1},{4,6},{5,7},{6,4},{7,5},{8,10},{9,11},{10,... | collective-permute-start | bytes 1572872 | tf_op jit(solution)/shard_map/ppermute | solution.py:34
  17.6 5.5 %collective-permute-start.6 = (f32[1,928]{1,0:T(1,128)S(1)}, f32[1,928]{1,0:T(1,128)S(1)}, u32[]{:S(2)}, u32[]{:S(2)}) collective-permute-start(f32[1,928]{1,0:T(1,128)S(1)} %bitcast.207), channel_id=1, source_target_pairs={{0,24},{4,28},{8,16},{12,20},{16,8},{20,12},{24,0},{28,4},{1,25},{... | collective-permute-start | bytes 11144 | tf_op jit(solution)/shard_map/ppermute | solution.py:34
  26.6 11.6 %collective-permute-start.1 = (bf16[256,1024]{1,0:T(8,128)(2,1)S(1)}, bf16[256,1024]{1,0:T(8,128)(2,1)S(1)}, u32[]{:S(2)}, u32[]{:S(2)}) collective-permute-start(bf16[256,1024]{1,0:T(8,128)(2,1)S(1)} %bitcast.175), channel_id=1, source_target_pairs={{0,4},{4,0},{8,12},{12,8},{16,20},{20,16},{24,28},{28,24},{1,5},{5... | collective-permute-start | bytes 1572872 | tf_op jit(solution)/shard_map/ppermute | solution.py:34
  39.0 10.5 %all-to-all-start = ((bf16[4,2,32,896]{3,2,1,0:T(8,128)(2,1)}), bf16[4,2,32,896]{3,2,1,0:T(8,128)(2,1)S(1)}, u32[]{:S(2)}, u32[]{:S(2)}) async-start(bf16[4,2,32,896]{3,2,1,0:T(8,128)(2,1)} %copy.60), calls=%async_computation | async-start | bytes 917504 | tf_op jit(solution)/shard_map/all_to_all | solution.py:683
  42.9 50.0 %all-gather.9.cloned.1.call-start = ((), (), s32[]{:S(2)}) async-start(), calls=%async_computation.7 | async-start | bytes 1310720 | tf_op jit(solution)/shard_map/all_gather | solution.py:50
  49.4 14.9 %collective-permute-start.12 = (bf16[256,1024]{1,0:T(8,128)(2,1)S(1)}, bf16[256,1024]{1,0:T(8,128)(2,1)}, u32[]{:S(2)}, u32[]{:S(2)}) collective-permute-start(bf16[256,1024]{1,0:T(8,128)(2,1)S(1)} %bitcast.179), channel_id=1, source_target_pairs={{0,2},{1,3},{2,0},{3,1},{4,6},{5,7},{6,4},{7,5},{8,10},{9,11},{10,... | collective-permute-start | bytes 1572872 | tf_op jit(solution)/shard_map/ppermute | solution.py:34
  52.0 68.2 %all-gather.11.cloned.1.call-start = ((), (), s32[]{:S(2)}) async-start(), calls=%async_computation.8 | async-start | bytes 1310720 | tf_op jit(solution)/shard_map/all_gather | solution.py:50
  52.6 21.9 %collective-permute-start.3 = (bf16[256,1024]{1,0:T(8,128)(2,1)S(1)}, bf16[256,1024]{1,0:T(8,128)(2,1)}, u32[]{:S(2)}, u32[]{:S(2)}) collective-permute-start(bf16[256,1024]{1,0:T(8,128)(2,1)S(1)} %collective-permute-done.1), channel_id=1, source_target_pairs={{0,2},{1,3},{2,0},{3,1},{4,6},{5,7},{6,4},{7,5},{8,10},{9,11},{10,... | collective-permute-start | bytes 1572872 | tf_op jit(solution)/shard_map/ppermute | solution.py:34
  56.2 20.9 %collective-permute-start.11 = (bf16[256,1024]{1,0:T(8,128)(2,1)S(1)}, bf16[256,1024]{1,0:T(8,128)(2,1)}, u32[]{:S(2)}, u32[]{:S(2)}) collective-permute-start(bf16[256,1024]{1,0:T(8,128)(2,1)S(1)} %bitcast.180), channel_id=1, source_target_pairs={{0,4},{4,0},{8,12},{12,8},{16,20},{20,16},{24,28},{28,24},{1,5},{5... | collective-permute-start | bytes 1572872 | tf_op jit(solution)/shard_map/ppermute | solution.py:34
  64.3 16.4 %collective-permute-start.13 = (bf16[256,1024]{1,0:T(8,128)(2,1)}, bf16[256,1024]{1,0:T(8,128)(2,1)}, u32[]{:S(2)}, u32[]{:S(2)}) collective-permute-start(bf16[256,1024]{1,0:T(8,128)(2,1)} %collective-permute-done.12), channel_id=1, source_target_pairs={{0,4},{4,0},{8,12},{12,8},{16,20},{20,16},{24,28},{28,24},{1,5},{5... | collective-permute-start | bytes 1572872 | tf_op jit(solution)/shard_map/ppermute | solution.py:34
  77.1 15.8 %collective-permute-start.10 = (bf16[1024,1024]{1,0:T(8,128)(2,1)}, bf16[1024,1024]{1,0:T(8,128)(2,1)}, u32[]{:S(2)}, u32[]{:S(2)}) collective-permute-start(bf16[1024,1024]{1,0:T(8,128)(2,1)} %pad_maximum_fusion.refs_0_), channel_id=1, source_target_pairs={{0,1},{1,0},{2,3},{3,2},{4,5},{5,4},{6,7},{7,6},{8,9},{9,8},{10,11... | collective-permute-start | bytes 6291464 | tf_op jit(solution)/shard_map/ppermute | solution.py:34
  82.3 10.7 %collective-permute-start.14 = (bf16[1024,1024]{1,0:T(8,128)(2,1)S(1)}, bf16[1024,1024]{1,0:T(8,128)(2,1)}, u32[]{:S(2)}, u32[]{:S(2)}) collective-permute-start(bf16[1024,1024]{1,0:T(8,128)(2,1)S(1)} %pad_maximum_fusion.1.refs_2_.refs_0_), channel_id=1, source_target_pairs={{0,1},{1,0},{2,3},{3,2},{4,5},{5,4},{6,7},{7,6},{8,9},{9,8},{10,11... | collective-permute-start | bytes 6291464 | tf_op jit(solution)/shard_map/ppermute | solution.py:34
  82.4 9.8 %collective-permute-start.15 = (bf16[32,1024]{1,0:T(8,128)(2,1)S(1)}, bf16[32,1024]{1,0:T(8,128)(2,1)S(1)}, u32[]{:S(2)}, u32[]{:S(2)}) collective-permute-start(bf16[32,1024]{1,0:T(8,128)(2,1)S(1)} %copy-done.32), channel_id=1, source_target_pairs={{0,0},{4,1},{8,2},{12,3},{16,4},{20,5},{24,6},{28,7},{1,8},{5,9},{... | collective-permute-start | bytes 196616 | tf_op jit(solution)/shard_map/ppermute | solution.py:78
  92.9 76.7 %reduce-scatter.3.cloned.1.call-start = ((), (), s32[]{:S(2)}) async-start(), calls=%async_computation.4 | async-start | bytes 2621440 | tf_op jit(solution)/shard_map/reduce_scatter | solution.py:53
  118.9 79.3 %reduce-scatter.5.cloned.1.call-start = ((), (), s32[]{:S(2)}) async-start(), calls=%async_computation.5 | async-start | bytes 1310720 | tf_op jit(solution)/shard_map/reduce_scatter | solution.py:53
  152.6 9.8 %collective-permute-start.16 = (bf16[1024,1024]{1,0:T(8,128)(2,1)}, bf16[1024,1024]{1,0:T(8,128)(2,1)}, u32[]{:S(2)}, u32[]{:S(2)}) collective-permute-start(bf16[1024,1024]{1,0:T(8,128)(2,1)} %get-tuple-element.86), channel_id=1, source_target_pairs={{0,1},{1,0},{2,3},{3,2},{4,5},{5,4},{6,7},{7,6},{8,9},{9,8},{10,11... | collective-permute-start | bytes 6291464 | tf_op jit(solution)/shard_map/ppermute | solution.py:34
  166.4 16.4 %collective-permute-start.17 = (bf16[2,256,512]{2,1,0:T(8,128)(2,1)}, bf16[2,256,512]{2,1,0:T(8,128)(2,1)S(1)}, u32[]{:S(2)}, u32[]{:S(2)}) collective-permute-start(bf16[2,256,512]{2,1,0:T(8,128)(2,1)} %bitcast.215), channel_id=1, source_target_pairs={{0,2},{1,3},{2,0},{3,1},{4,6},{5,7},{6,4},{7,5},{8,10},{9,11},{10,... | collective-permute-start | bytes 1572872 | tf_op jit(solution)/shard_map/ppermute | solution.py:34
  166.4 16.4 %collective-permute-start.18 = (bf16[2,256,512]{2,1,0:T(8,128)(2,1)}, bf16[2,256,512]{2,1,0:T(8,128)(2,1)}, u32[]{:S(2)}, u32[]{:S(2)}) collective-permute-start(bf16[2,256,512]{2,1,0:T(8,128)(2,1)} %get-tuple-element.93), channel_id=1, source_target_pairs={{0,4},{4,0},{8,12},{12,8},{16,20},{20,16},{24,28},{28,24},{1,5},{5... | collective-permute-start | bytes 1572872 | tf_op jit(solution)/shard_map/ppermute | solution.py:34
  184.4 13.9 %collective-permute-start.23 = (bf16[1024,1024]{1,0:T(8,128)(2,1)}, bf16[1024,1024]{1,0:T(8,128)(2,1)}, u32[]{:S(2)}, u32[]{:S(2)}) collective-permute-start(bf16[1024,1024]{1,0:T(8,128)(2,1)} %get-tuple-element.116), channel_id=1, source_target_pairs={{0,1},{1,0},{2,3},{3,2},{4,5},{5,4},{6,7},{7,6},{8,9},{9,8},{10,11... | collective-permute-start | bytes 6291464 | tf_op jit(solution)/shard_map/ppermute | solution.py:34
  190.0 5.8 %collective-permute-start.22 = (f32[2,2,384]{2,0,1:T(2,128)S(1)}, f32[2,2,384]{2,0,1:T(2,128)S(1)}, u32[]{:S(2)}, u32[]{:S(2)}) collective-permute-start(f32[2,2,384]{2,0,1:T(2,128)S(1)} %get-tuple-element.150), channel_id=1, source_target_pairs={{0,24},{4,28},{8,16},{12,20},{16,8},{20,12},{24,0},{28,4},{1,25},{... | collective-permute-start | bytes 18440 | tf_op jit(solution)/shard_map/ppermute | solution.py:34
  202.3 13.0 %collective-permute-start.24 = (bf16[2,256,512]{2,1,0:T(8,128)(2,1)}, bf16[2,256,512]{2,1,0:T(8,128)(2,1)S(1)}, u32[]{:S(2)}, u32[]{:S(2)}) collective-permute-start(bf16[2,256,512]{2,1,0:T(8,128)(2,1)} %bitcast.216), channel_id=1, source_target_pairs={{0,2},{1,3},{2,0},{3,1},{4,6},{5,7},{6,4},{7,5},{8,10},{9,11},{10,... | collective-permute-start | bytes 1572872 | tf_op jit(solution)/shard_map/ppermute | solution.py:34
  202.6 16.2 %collective-permute-start.25 = (bf16[2,256,512]{2,1,0:T(8,128)(2,1)}, bf16[2,256,512]{2,1,0:T(8,128)(2,1)S(1)}, u32[]{:S(2)}, u32[]{:S(2)}) collective-permute-start(bf16[2,256,512]{2,1,0:T(8,128)(2,1)} %get-tuple-element.118), channel_id=1, source_target_pairs={{0,4},{4,0},{8,12},{12,8},{16,20},{20,16},{24,28},{28,24},{1,5},{5... | collective-permute-start | bytes 1572872 | tf_op jit(solution)/shard_map/ppermute | solution.py:34
  218.4 23.5 %collective-permute-start.28 = (bf16[256,512]{1,0:T(8,128)(2,1)}, bf16[256,512]{1,0:T(8,128)(2,1)}, u32[]{:S(2)}, u32[]{:S(2)}) collective-permute-start(bf16[256,512]{1,0:T(8,128)(2,1)} %fusion.15), channel_id=1, source_target_pairs={{0,4},{4,0},{8,12},{12,8},{16,20},{20,16},{24,28},{28,24},{1,5},{5... | collective-permute-start | bytes 786440 | tf_op jit(solution)/shard_map/ppermute | solution.py:34
  220.8 22.2 %collective-permute-start.29 = (bf16[256,512]{1,0:T(8,128)(2,1)}, bf16[256,512]{1,0:T(8,128)(2,1)}, u32[]{:S(2)}, u32[]{:S(2)}) collective-permute-start(bf16[256,512]{1,0:T(8,128)(2,1)} %fusion.16), channel_id=1, source_target_pairs={{0,2},{1,3},{2,0},{3,1},{4,6},{5,7},{6,4},{7,5},{8,10},{9,11},{10,... | collective-permute-start | bytes 786440 | tf_op jit(solution)/shard_map/ppermute | solution.py:34
  221.4 5.5 %collective-permute-start.30 = (f32[2,384]{1,0:T(2,128)S(1)}, f32[2,384]{1,0:T(2,128)S(1)}, u32[]{:S(2)}, u32[]{:S(2)}) collective-permute-start(f32[2,384]{1,0:T(2,128)S(1)} %slice_bitcast_fusion.13), channel_id=1, source_target_pairs={{0,4},{4,0},{8,12},{12,8},{16,20},{20,16},{24,28},{28,24},{1,5},{5... | collective-permute-start | bytes 9224 | tf_op jit(solution)/shard_map/ppermute | solution.py:34
  223.1 10.1 %collective-permute-start.33 = (bf16[32,1024]{1,0:T(8,128)(2,1)S(1)}, bf16[32,1024]{1,0:T(8,128)(2,1)S(1)}, u32[]{:S(2)}, u32[]{:S(2)}) collective-permute-start(bf16[32,1024]{1,0:T(8,128)(2,1)S(1)} %bitcast.203), channel_id=1, source_target_pairs={{0,0},{1,4},{2,8},{3,12},{4,16},{5,20},{6,24},{7,28},{8,1},{9,5},{... | collective-permute-start | bytes 196616 | tf_op jit(solution)/shard_map/ppermute | solution.py:78
  228.2 8.6 %collective-permute-start.32 = (bf16[4,32,896]{2,1,0:T(8,128)(2,1)S(1)}, bf16[4,32,896]{2,1,0:T(8,128)(2,1)S(1)}, u32[]{:S(2)}, u32[]{:S(2)}) collective-permute-start(bf16[4,32,896]{2,1,0:T(8,128)(2,1)S(1)} %dynamic-slice_bitcast_fusion), channel_id=1, source_target_pairs={{0,4},{4,0},{8,12},{12,8},{16,20},{20,16},{24,28},{28,24},{1,5},{5... | collective-permute-start | bytes 688136 | tf_op jit(solution)/shard_map/ppermute | solution.py:34
  230.6 14.1 %collective-permute-start.26 = (bf16[256,512]{1,0:T(8,128)(2,1)}, bf16[256,512]{1,0:T(8,128)(2,1)S(1)}, u32[]{:S(2)}, u32[]{:S(2)}) collective-permute-start(bf16[256,512]{1,0:T(8,128)(2,1)} %fusion.13), channel_id=1, source_target_pairs={{0,4},{4,0},{8,12},{12,8},{16,20},{20,16},{24,28},{28,24},{1,5},{5... | collective-permute-start | bytes 786440 | tf_op jit(solution)/shard_map/ppermute | solution.py:34
  233.1 11.7 %collective-permute-start.27 = (bf16[256,512]{1,0:T(8,128)(2,1)}, bf16[256,512]{1,0:T(8,128)(2,1)}, u32[]{:S(2)}, u32[]{:S(2)}) collective-permute-start(bf16[256,512]{1,0:T(8,128)(2,1)} %fusion.14), channel_id=1, source_target_pairs={{0,2},{1,3},{2,0},{3,1},{4,6},{5,7},{6,4},{7,5},{8,10},{9,11},{10,... | collective-permute-start | bytes 786440 | tf_op jit(solution)/shard_map/ppermute | solution.py:34
  237.6 10.8 %all-to-all-start.1 = ((bf16[4,2,32,896]{3,2,1,0:T(8,128)(2,1)}), bf16[4,2,32,896]{3,2,1,0:T(8,128)(2,1)S(1)}, u32[]{:S(2)}, u32[]{:S(2)}) async-start(bf16[4,2,32,896]{3,2,1,0:T(8,128)(2,1)} %pad_maximum_fusion.4), calls=%async_computation.3 | async-start | bytes 917504 | tf_op jit(solution)/shard_map/all_to_all | solution.py:67
  (43 other events, 247.1 us)
Sparse Core Ops, SparseCore 0:
  9.6 29.4 all-gather.6
  52.1 27.1 all-gather.8
  93.0 26.0 all-gather.10
  121.3 43.3 reduce-scatter.2
  169.8 27.7 reduce-scatter.4
